TPU v7x, 32 devices: a whole 2x2x4 slice. The times are simulated.
32 devices in a mesh: dp: 8 (over z, x), mp: 4 (over y, core).
Axes of the slice: x: 2, y: 2, z: 4, core: 2. Of those that a mesh axis runs over, the one named last changes fastest.
Arguments:
- patches: bfloat16 [16, 20480], P(None, ('dp', 'mp')), may hold values from -6 to 6
- target: float32 [32, 20480], P(None, ('dp', 'mp')), may hold values from -6 to 6
- segments: int32 [20480], P('dp'), may hold values from 0 to 15, as said below
- positions: int32 [2, 20480], P(None, 'dp'), may hold values from 0 to 31, as said below
- classes: int32 [128], P('dp'), may hold values from 0 to 1000
- timesteps: int32 [128], P('dp'), may hold values from 0 to 999
- t_weight: float32 [128], P('dp'), may hold values from 0.3 to 3
- step_count: int32 [1], replicated, may hold values from 2 to 20
- qkv_w: float32 [3, 1152, 1152], P(None, 'dp', 'mp'), may hold values from -0.1875 to 0.1875
- qkv_m: float32 [3, 1152, 1152], P(None, 'dp', 'mp'), may hold values from -4.172325e-07 to 4.172325e-07
- qkv_v: float32 [3, 1152, 1152], P(None, 'dp', 'mp'), may hold values from 1.096693e-14 to 1.7447389e-13
- out_w: float32 [1152, 1152], P('mp', 'dp'), may hold values from -0.75 to 0.75
- out_m: float32 [1152, 1152], P('mp', 'dp'), may hold values from -4.172325e-07 to 4.172325e-07
- out_v: float32 [1152, 1152], P('mp', 'dp'), may hold values from 1.096693e-14 to 1.7447389e-13
- ffn_in_w: float32 [2, 1152, 3072], P(None, 'dp', 'mp'), may hold values from -0.1875 to 0.1875
- ffn_in_m: float32 [2, 1152, 3072], P(None, 'dp', 'mp'), may hold values from -4.172325e-07 to 4.172325e-07
- ffn_in_v: float32 [2, 1152, 3072], P(None, 'dp', 'mp'), may hold values from 1.096693e-14 to 1.7447389e-13
- ffn_out_w: float32 [3072, 1152], P('mp', 'dp'), may hold values from -0.109375 to 0.109375
- ffn_out_m: float32 [3072, 1152], P('mp', 'dp'), may hold values from -4.172325e-07 to 4.172325e-07
- ffn_out_v: float32 [3072, 1152], P('mp', 'dp'), may hold values from 1.096693e-14 to 1.7447389e-13
- mod_w: float32 [1152, 9216], P('dp'), may hold values from -0.1875 to 0.1875
- mod_m: float32 [1152, 9216], P('dp'), may hold values from -4.172325e-07 to 4.172325e-07
- mod_v: float32 [1152, 9216], P('dp'), may hold values from 1.096693e-14 to 1.7447389e-13
- table_w: float32 [2468, 1152], P('mp'), as said below
- table_m: float32 [2468, 1152], P('mp'), may hold values from -4.172325e-07 to 4.172325e-07
- table_v: float32 [2468, 1152], P('mp'), may hold values from 1.096693e-14 to 1.7447389e-13
Outputs:
- loss: float32 [1], replicated
- grad_norm: float32 [1], replicated
- qkv_w_new: float32 [3, 1152, 1152], P(None, 'dp', 'mp')
- qkv_m_new: float32 [3, 1152, 1152], P(None, 'dp', 'mp')
- qkv_v_new: float32 [3, 1152, 1152], P(None, 'dp', 'mp')
- out_w_new: float32 [1152, 1152], P('mp', 'dp')
- out_m_new: float32 [1152, 1152], P('mp', 'dp')
- out_v_new: float32 [1152, 1152], P('mp', 'dp')
- ffn_in_w_new: float32 [2, 1152, 3072], P(None, 'dp', 'mp')
- ffn_in_m_new: float32 [2, 1152, 3072], P(None, 'dp', 'mp')
- ffn_in_v_new: float32 [2, 1152, 3072], P(None, 'dp', 'mp')
- ffn_out_w_new: float32 [3072, 1152], P('mp', 'dp')
- ffn_out_m_new: float32 [3072, 1152], P('mp', 'dp')
- ffn_out_v_new: float32 [3072, 1152], P('mp', 'dp')
- mod_w_new: float32 [1152, 9216], P('dp')
- mod_m_new: float32 [1152, 9216], P('dp')
- mod_v_new: float32 [1152, 9216], P('dp')
- table_w_new: float32 [2468, 1152], P('mp')
- table_m_new: float32 [2468, 1152], P('mp')
- table_v_new: float32 [2468, 1152], P('mp')
Inputs may be any that keep to these rules, and one draw needn't show every extreme that they name: `segments`: within each group of 2560 consecutive tokens the values number the group's 16 images in order as runs of 64 to 256 tokens; images 2j and 2j+1 of a group hold 320 tokens together; every group has an image of 256 tokens and one of 64. For the k-th token of an image, positions holds k // w and k % w, with a width w of 8 to 16 for that image. `table_w`: rows are drawn with the scale of their fan-in; bias rows of the timestep MLP and the patch embedding are of order one.
All inputs are finite; a program needn't handle non-finite values.
Results may differ from a plain program's by a relative error of at most 0.0012.
The roundings to bfloat16 on the way count: a program that leaves them out, or rounds other values in their place, can miss the bound.
Values may be sent and summed in bfloat16 or wider, within the bound.
A program may use at most 384 MiB of HBM per device.

v0:
```python
import math

import jax
import jax.numpy as jnp
from jax import lax
from jax.sharding import PartitionSpec as P

D = 1152
HD = 72
PATCH_IN = 16
OUT = 32
FREQ = 256
NCLS = 1001


EPS_NORM = 1e-06
BETA_ONE = 0.9
BETA_TWO = 0.95
ADAM_EPS = 1e-08
LEARN_RATE = 0.03
WEIGHT_DECAY = 0.1
CLIP_SCALE = 0.5
HIGH = lax.Precision.HIGHEST


def matmul(left, right):
    return jnp.dot(left, right, preferred_element_type=jnp.float32)


def matmul_tn(left, right):
    return lax.dot_general(
        left, right, (((0,), (0,)), ((), ())), preferred_element_type=jnp.float32
    )


def matmul_nt(left, right):
    return lax.dot_general(
        left, right, (((1,), (1,)), ((), ())), preferred_element_type=jnp.float32
    )


def exact_dot(left, right):
    return jnp.dot(left, right, precision=HIGH)


def layer_norm(values):
    centred = values - jnp.mean(values, -1, keepdims=True)
    inv_std = lax.rsqrt(jnp.mean(centred * centred, -1, keepdims=True) + EPS_NORM)
    return (centred * inv_std, inv_std)


def modulate_back(grad, normed, inv_std, scale_rows):
    inner = grad * (1.0 + scale_rows)
    back = inv_std * (
        inner
        - jnp.mean(inner, -1, keepdims=True)
        - normed * jnp.mean(inner * normed, -1, keepdims=True)
    )
    return (back, grad * normed, grad)


def silu_slope(values):
    sigma = jax.nn.sigmoid(values)
    return sigma * (1.0 + values * (1.0 - sigma))


def rope_tables(positions, quarter):
    freqs = jnp.exp(-math.log(10000.0) * jnp.arange(quarter, dtype=jnp.float32) / quarter)
    tables = []
    for axis_pos in (positions[0], positions[1]):
        angle = axis_pos.astype(jnp.float32)[:, None] * freqs[None, :]
        tables.append((jnp.cos(angle)[:, None, :], jnp.sin(angle)[:, None, :]))
    return tables


def rotate(values, tables, direction):
    quarter = values.shape[-1] // 4
    pieces = []
    for part_index in range(2):
        cosine, sine = tables[part_index]
        first = values[..., 2 * part_index * quarter : (2 * part_index + 1) * quarter]
        second = values[..., (2 * part_index + 1) * quarter : (2 * part_index + 2) * quarter]
        pieces.append(first * cosine - direction * second * sine)
        pieces.append(direction * first * sine + second * cosine)
    return jnp.concatenate(pieces, -1)


def gather_rows(values):
    return lax.all_gather(values, "mp", axis=0, tiled=True)


def scatter_rows(values):
    return lax.psum_scatter(values, "mp", scatter_dimension=0, tiled=True)


def block_shape(token_count):
    block = 640
    return (block, min(token_count, block + 512))


def block_scores(queries, key_rows, segment_ids, start, block, span):
    token_count = segment_ids.shape[0]
    key_start = jnp.clip(start - 256, 0, token_count - span)
    query_blk = lax.dynamic_slice_in_dim(queries, start, block, 0)
    key_blk = lax.dynamic_slice_in_dim(key_rows, key_start, span, 0)
    query_seg = lax.dynamic_slice_in_dim(segment_ids, start, block, 0)
    key_seg = lax.dynamic_slice_in_dim(segment_ids, key_start, span, 0)
    scores = jnp.einsum(
        "qhd,khd->hqk", query_blk, key_blk, preferred_element_type=jnp.float32
    ) * HD ** (-0.5)
    scores = jnp.where((query_seg[:, None] == key_seg[None, :])[None], scores, -1e30)
    return (scores, key_start, query_blk, key_blk)


def attend(queries, key_rows, value_rows, segment_ids):
    token_count = segment_ids.shape[0]
    block, span = block_shape(token_count)

    def one_block(start):
        scores, key_start, unused_q, unused_k = block_scores(
            queries, key_rows, segment_ids, start, block, span
        )
        peak = jnp.max(scores, -1, keepdims=True)
        expo = jnp.exp(scores - peak)
        total = jnp.sum(expo, -1, keepdims=True)
        probs = (expo / total).astype(jnp.bfloat16)
        value_blk = lax.dynamic_slice_in_dim(value_rows, key_start, span, 0)
        result = jnp.einsum("hqk,khd->qhd", probs, value_blk, preferred_element_type=jnp.float32)
        return (result, (peak + jnp.log(total))[..., 0])

    starts = jnp.arange(token_count // block, dtype=jnp.int32) * block
    results, log_sums = lax.map(one_block, starts)
    return (results.reshape(token_count, -1, HD), log_sums)


def attend_back(queries, key_rows, value_rows, segment_ids, log_sums, grad_out):
    token_count = segment_ids.shape[0]
    block, span = block_shape(token_count)
    scale = HD ** (-0.5)
    zeros = jnp.zeros(queries.shape, jnp.float32)

    def one_block(carry, block_index):
        grad_q, grad_k, grad_v = carry
        start = block_index * block
        scores, key_start, query_blk, key_blk = block_scores(
            queries, key_rows, segment_ids, start, block, span
        )
        probs = jnp.exp(scores - log_sums[block_index][..., None])
        value_blk = lax.dynamic_slice_in_dim(value_rows, key_start, span, 0)
        grad_blk = lax.dynamic_slice_in_dim(grad_out, start, block, 0)
        grad_probs = jnp.einsum(
            "qhd,khd->hqk", grad_blk, value_blk, preferred_element_type=jnp.float32
        )
        centre = jnp.sum(probs * grad_probs, -1, keepdims=True)
        grad_scores = (probs * (grad_probs - centre)).astype(jnp.bfloat16)
        q_part = (
            jnp.einsum("hqk,khd->qhd", grad_scores, key_blk, preferred_element_type=jnp.float32)
            * scale
        )
        k_part = (
            jnp.einsum("hqk,qhd->khd", grad_scores, query_blk, preferred_element_type=jnp.float32)
            * scale
        )
        v_part = jnp.einsum(
            "hqk,qhd->khd", probs.astype(jnp.bfloat16), grad_blk, preferred_element_type=jnp.float32
        )
        grad_q = lax.dynamic_update_slice_in_dim(grad_q, q_part, start, 0)
        grad_k = lax.dynamic_update_slice_in_dim(
            grad_k, lax.dynamic_slice_in_dim(grad_k, key_start, span, 0) + k_part, key_start, 0
        )
        grad_v = lax.dynamic_update_slice_in_dim(
            grad_v, lax.dynamic_slice_in_dim(grad_v, key_start, span, 0) + v_part, key_start, 0
        )
        return ((grad_q, grad_k, grad_v), None)

    blocks = jnp.arange(token_count // block, dtype=jnp.int32)
    grads, unused = lax.scan(one_block, (zeros, zeros, zeros), blocks)
    return grads


def adam(weight, first, second, grad, count):
    first = BETA_ONE * first + (1.0 - BETA_ONE) * grad
    second = BETA_TWO * second + (1.0 - BETA_TWO) * grad * grad
    m_hat = first / (1.0 - BETA_ONE**count)
    v_hat = second / (1.0 - BETA_TWO**count)
    weight = weight - LEARN_RATE * (m_hat / (jnp.sqrt(v_hat) + ADAM_EPS) + WEIGHT_DECAY * weight)
    return (weight, first, second)


def per_device(
    patches,
    target,
    segments,
    positions,
    classes,
    timesteps,
    t_weight,
    step_count,
    qkv_w,
    qkv_m,
    qkv_v,
    out_w,
    out_m,
    out_v,
    ffn_in_w,
    ffn_in_m,
    ffn_in_v,
    ffn_out_w,
    ffn_out_m,
    ffn_out_v,
    mod_w,
    mod_m,
    mod_v,
    table_w,
    table_m,
    table_v,
):
    low_type = jnp.bfloat16
    mp_count = lax.axis_size("mp")
    dp_count = lax.axis_size("dp")
    row_count = patches.shape[1]
    group_tokens = row_count * mp_count
    image_count = classes.shape[0]
    row_time_in = NCLS
    row_time_bias = row_time_in + FREQ
    row_time_out = row_time_bias + 1
    row_out_bias = row_time_out + D
    row_patch = row_out_bias + 1
    row_patch_bias = row_patch + PATCH_IN
    row_head = row_patch_bias + 1
    row_mod_bias = row_head + OUT
    qkv_all, out_all, ffn_in_all, ffn_out_all = (
        lax.all_gather(qkv_w.astype(low_type), "dp", axis=1, tiled=True),
        lax.all_gather(out_w.astype(low_type), "dp", axis=1, tiled=True),
        lax.all_gather(ffn_in_w.astype(low_type), "dp", axis=1, tiled=True),
        lax.all_gather(ffn_out_w.astype(low_type), "dp", axis=1, tiled=True),
    )
    table_all = lax.all_gather(table_w.astype(low_type), "mp", axis=0, tiled=True)
    mod_all = lax.all_gather(mod_w.astype(low_type), "dp", axis=0, tiled=True)
    class_hot = (classes[:, None] == jnp.arange(NCLS, dtype=jnp.int32)[None, :]).astype(low_type)
    class_rows = matmul(class_hot, table_all[:NCLS])
    half_freq = FREQ // 2
    freqs = jnp.exp(-math.log(10000.0) * jnp.arange(half_freq, dtype=jnp.float32) / half_freq)
    angles = timesteps.astype(jnp.float32)[:, None] * freqs[None, :]
    time_embed = jnp.concatenate([jnp.cos(angles), jnp.sin(angles)], 1).astype(low_type)
    time_pre = matmul(time_embed, table_all[row_time_in:row_time_bias]) + table_all[
        row_time_bias
    ].astype(jnp.float32)
    time_hidden = jax.nn.silu(time_pre).astype(low_type)
    cond_vec = (
        matmul(time_hidden, table_all[row_time_out:row_out_bias])
        + table_all[row_out_bias].astype(jnp.float32)
        + class_rows
    )
    cond_scaled = jax.nn.silu(cond_vec).astype(low_type)
    mod_bias = table_all[row_mod_bias : row_mod_bias + 8].astype(jnp.float32).reshape(-1)
    modulation = matmul(cond_scaled, mod_all) + mod_bias
    image_ids = jnp.arange(image_count, dtype=jnp.int32)
    counts = jnp.sum((segments[:, None] == image_ids[None, :]).astype(jnp.float32), 0)
    own_seg = lax.dynamic_slice_in_dim(segments, lax.axis_index("mp") * row_count, row_count)
    own_hot = (own_seg[:, None] == image_ids[None, :]).astype(jnp.float32)
    mod_tok = exact_dot(own_hot, modulation)
    stretches = [mod_tok[:, j * D : (j + 1) * D] for j in range(8)]
    x_zero = matmul_tn(patches, table_all[row_patch:row_patch_bias]) + table_all[
        row_patch_bias
    ].astype(jnp.float32)
    norm_a, inv_a = layer_norm(x_zero)
    a_all = gather_rows((norm_a * (1.0 + stretches[1]) + stretches[0]).astype(low_type))
    local_heads = qkv_all.shape[2] // HD
    tables = rope_tables(positions, HD // 4)
    queries = rotate(
        matmul(a_all, qkv_all[0]).reshape(group_tokens, local_heads, HD), tables, 1.0
    ).astype(low_type)
    key_rows = rotate(
        matmul(a_all, qkv_all[1]).reshape(group_tokens, local_heads, HD), tables, 1.0
    ).astype(low_type)
    value_rows = matmul(a_all, qkv_all[2]).astype(low_type).reshape(group_tokens, local_heads, HD)
    att_raw, log_sums = attend(queries, key_rows, value_rows, segments)
    att = att_raw.reshape(group_tokens, local_heads * HD).astype(low_type)
    attn_proj = scatter_rows(matmul(att, out_all))
    x_one = x_zero + stretches[2] * attn_proj
    norm_m, inv_m = layer_norm(x_one)
    m_all = gather_rows((norm_m * (1.0 + stretches[4]) + stretches[3]).astype(low_type))
    gate = matmul(m_all, ffn_in_all[0])
    up_val = matmul(m_all, ffn_in_all[1])
    gate_act = jax.nn.silu(gate)
    hidden_mlp = (gate_act * up_val).astype(low_type)
    mlp_out = scatter_rows(matmul(hidden_mlp, ffn_out_all))
    x_two = x_one + stretches[5] * mlp_out
    norm_f, inv_f = layer_norm(x_two)
    f_in = (norm_f * (1.0 + stretches[7]) + stretches[6]).astype(low_type)
    head_rows = table_all[row_head : row_head + OUT]
    diff = matmul_nt(head_rows, f_in) - target
    weight_sum = lax.psum(jnp.sum(t_weight), "dp")
    tok_weight = exact_dot(own_hot, t_weight / counts)
    loss_part = jnp.sum(tok_weight * jnp.mean(diff * diff, 0))
    grad_pred = (2.0 / OUT * diff * tok_weight[None, :] / weight_sum).astype(low_type)
    grad_head = matmul(grad_pred, f_in)
    grad_f = matmul_tn(grad_pred, head_rows)
    grad_x2, dscale_f, dshift_f = modulate_back(grad_f, norm_f, inv_f, stretches[7])
    dgate_m = grad_x2 * mlp_out
    grad_mo = gather_rows((stretches[5] * grad_x2).astype(low_type))
    grad_ffn_out = matmul_tn(hidden_mlp, grad_mo)
    grad_hidden = matmul_nt(grad_mo, ffn_out_all)
    grad_gate = (grad_hidden * up_val * silu_slope(gate)).astype(low_type)
    grad_up = (grad_hidden * gate_act).astype(low_type)
    grad_ffn_in = jnp.stack([matmul_tn(m_all, grad_gate), matmul_tn(m_all, grad_up)])
    grad_m = scatter_rows(matmul_nt(grad_gate, ffn_in_all[0]) + matmul_nt(grad_up, ffn_in_all[1]))
    back_m, dscale_m, dshift_m = modulate_back(grad_m, norm_m, inv_m, stretches[4])
    grad_x1 = grad_x2 + back_m
    dgate_a = grad_x1 * attn_proj
    grad_proj = gather_rows((stretches[2] * grad_x1).astype(low_type))
    grad_out_w = matmul_tn(att, grad_proj)
    grad_att = matmul_nt(grad_proj, out_all).astype(low_type).reshape(group_tokens, local_heads, HD)
    grad_q, grad_k, grad_v = attend_back(
        queries, key_rows, value_rows, segments, log_sums, grad_att
    )
    grad_q = rotate(grad_q, tables, -1.0).astype(low_type).reshape(group_tokens, local_heads * HD)
    grad_k = rotate(grad_k, tables, -1.0).astype(low_type).reshape(group_tokens, local_heads * HD)
    grad_v = grad_v.astype(low_type).reshape(group_tokens, local_heads * HD)
    grad_qkv = jnp.stack(
        [matmul_tn(a_all, grad_q), matmul_tn(a_all, grad_k), matmul_tn(a_all, grad_v)]
    )
    grad_a = scatter_rows(
        matmul_nt(grad_q, qkv_all[0])
        + matmul_nt(grad_k, qkv_all[1])
        + matmul_nt(grad_v, qkv_all[2])
    )
    back_a, dscale_a, dshift_a = modulate_back(grad_a, norm_a, inv_a, stretches[1])
    grad_x0 = (grad_x1 + back_a).astype(low_type)
    grad_patch = matmul(patches, grad_x0)
    grad_pbias = jnp.sum(grad_x0.astype(jnp.float32), 0)
    grad_mod_tok = jnp.concatenate(
        [dshift_a, dscale_a, dgate_a, dshift_m, dscale_m, dgate_m, dshift_f, dscale_f], 1
    )
    grad_mod_part = lax.dot_general(own_hot, grad_mod_tok, (((0,), (0,)), ((), ())), precision=HIGH)
    token_grads = jnp.concatenate([grad_patch, grad_pbias[None, :], grad_head], 0)
    grad_mod, token_grads = lax.psum((grad_mod_part, token_grads), "mp")
    grad_mod_b = grad_mod.astype(low_type)
    grad_mod_bias = jnp.sum(grad_mod_b.astype(jnp.float32), 0).reshape(8, -1)
    grad_cond = matmul_nt(grad_mod_b, mod_all)
    grad_mod_w = lax.psum_scatter(
        matmul_tn(cond_scaled, grad_mod_b), "dp", scatter_dimension=0, tiled=True
    )
    grad_cvec = (grad_cond * silu_slope(cond_vec)).astype(low_type)
    grad_class = matmul_tn(class_hot, grad_cvec)
    grad_time_out = matmul_tn(time_hidden, grad_cvec)
    grad_out_bias = jnp.sum(grad_cvec.astype(jnp.float32), 0)
    grad_time_hidden = matmul_nt(grad_cvec, table_all[row_time_out:row_out_bias])
    grad_pre = (grad_time_hidden * silu_slope(time_pre)).astype(low_type)
    grad_time_in = matmul_tn(time_embed, grad_pre)
    grad_time_bias = jnp.sum(grad_pre.astype(jnp.float32), 0)
    grad_table_all = jnp.concatenate(
        [
            grad_class,
            grad_time_in,
            grad_time_bias[None, :],
            grad_time_out,
            grad_out_bias[None, :],
            token_grads,
            grad_mod_bias,
        ],
        0,
    )
    own_rows = table_w.shape[0]
    grad_table_own = lax.dynamic_slice_in_dim(
        grad_table_all, lax.axis_index("mp") * own_rows, own_rows, 0
    )
    grad_table = lax.psum(grad_table_own, "dp")
    grad_qkv, grad_out_w, grad_ffn_in, grad_ffn_out = (
        lax.psum_scatter(grad_qkv, "dp", scatter_dimension=1, tiled=True),
        lax.psum_scatter(grad_out_w, "dp", scatter_dimension=1, tiled=True),
        lax.psum_scatter(grad_ffn_in, "dp", scatter_dimension=1, tiled=True),
        lax.psum_scatter(grad_ffn_out, "dp", scatter_dimension=1, tiled=True),
    )
    sharded_sq = (
        jnp.sum(grad_qkv * grad_qkv)
        + jnp.sum(grad_out_w * grad_out_w)
        + jnp.sum(grad_ffn_in * grad_ffn_in)
        + jnp.sum(grad_ffn_out * grad_ffn_out)
    )
    copied_sq = (
        jnp.sum(grad_mod_w * grad_mod_w) / mp_count + jnp.sum(grad_table * grad_table) / dp_count
    )
    square_sum, loss_sum = lax.psum((sharded_sq + copied_sq, loss_part), ("dp", "mp"))
    norm = jnp.sqrt(square_sum)
    clip = jnp.minimum(1.0, CLIP_SCALE / math.sqrt(group_tokens * dp_count) / (norm + 1e-06))
    count = step_count[0].astype(jnp.float32)
    results = [(loss_sum / weight_sum).reshape(1), norm.reshape(1)]
    for weight, first, second, grad in (
        (qkv_w, qkv_m, qkv_v, grad_qkv),
        (out_w, out_m, out_v, grad_out_w),
        (ffn_in_w, ffn_in_m, ffn_in_v, grad_ffn_in),
        (ffn_out_w, ffn_out_m, ffn_out_v, grad_ffn_out),
        (mod_w, mod_m, mod_v, grad_mod_w),
        (table_w, table_m, table_v, grad_table),
    ):
        results.extend(adam(weight, first, second, grad * clip, count))
    return tuple(results)


def solution(mesh):
    in_specs = (
        P(None, ("dp", "mp")),
        P(None, ("dp", "mp")),
        P("dp"),
        P(None, "dp"),
        P("dp"),
        P("dp"),
        P("dp"),
        P(),
        P(None, "dp", "mp"),
        P(None, "dp", "mp"),
        P(None, "dp", "mp"),
        P("mp", "dp"),
        P("mp", "dp"),
        P("mp", "dp"),
        P(None, "dp", "mp"),
        P(None, "dp", "mp"),
        P(None, "dp", "mp"),
        P("mp", "dp"),
        P("mp", "dp"),
        P("mp", "dp"),
        P("dp", None),
        P("dp", None),
        P("dp", None),
        P("mp", None),
        P("mp", None),
        P("mp", None),
    )
    out_specs = (
        P(),
        P(),
        P(None, "dp", "mp"),
        P(None, "dp", "mp"),
        P(None, "dp", "mp"),
        P("mp", "dp"),
        P("mp", "dp"),
        P("mp", "dp"),
        P(None, "dp", "mp"),
        P(None, "dp", "mp"),
        P(None, "dp", "mp"),
        P("mp", "dp"),
        P("mp", "dp"),
        P("mp", "dp"),
        P("dp", None),
        P("dp", None),
        P("dp", None),
        P("mp", None),
        P("mp", None),
        P("mp", None),
    )
    return jax.shard_map(
        per_device, mesh=mesh, in_specs=in_specs, out_specs=out_specs, check_vma=False
    )
```

profile of v0, /device:TPU:0, one launch (start us, length us, event | category | flops | bytes accessed | tf_op | source)
XLA Modules:
  0.0 2901.6 jit_solution(9864110223862492261)
XLA Ops:
  16.9 39.6 %all-gather.27.cloned.1.call-done = bf16[4,617,1152]{2,1,0:T(8,128)(2,1)} async-done(((bf16[1,617,1152]{2,1,0:T(8,128)(2,1)}), bf16[4,617,1152]{2,1,0:T(8,128)(2,1)}) %all-gather.27.cloned.1.call-update) | async-done | bytes 5686288 | tf_op jit(solution)/shard_map/all_gather | solution.py:238
  73.2 392.2 %all-gather.11.cloned.1.call-done = bf16[1152,9216]{1,0:T(8,128)(2,1)} async-done(((bf16[144,9216]{1,0:T(8,128)(2,1)}), bf16[1152,9216]{1,0:T(8,128)(2,1)}) %all-gather.11.cloned.1.call-update) | async-done | bytes 21233680 | tf_op jit(solution)/shard_map/all_gather | solution.py:239
  465.3 8.5 convolution_add_fusion.3
  473.9 10.0 fusion.84
  493.9 36.6 %all_gather.34 = bf16[288,1152]{0,1:T(8,128)(2,1)} all-gather(bf16[288,144]{0,1:T(8,128)(2,1)S(1)} %convert_element_type.193), channel_id=1, replica_groups=mesh['dp'=8,'mp'=4] {'dp'}, dimensions={1}, use_global_device_ids=true | all-gather | bytes 746496 | tf_op jit(solution)/shard_map/all_gather | solution.py:234
  543.6 41.2 %all-gather.13.cloned.1.call-done = bf16[2560,1152]{1,0:T(8,128)(2,1)} async-done(((bf16[640,1152]{1,0:T(8,128)(2,1)}), bf16[2560,1152]{1,0:T(8,128)(2,1)}) %all-gather.13.cloned.1.call-update) | async-done | bytes 5898256 | tf_op jit(solution)/shard_map/all_gather | solution.py:89
  601.8 74.8 %while.30 = (s32[]{:T(128)}, bf16[4,640,4,72]{1,3,2,0:T(8,128)(2,1)}, f32[4,4,640]{2,1,0:T(4,128)S(1)}, s32[4]{0:T(128)S(1)}, bf16[2560,4,72]{0,2,1:T(8,128)(2,1...) while((s32[]{:T(128)}, ...), condition=%wide.region_6.7_spmd, body=%wide.region_3.6_spmd.sunk | while | flops 885470720 | bytes 40875252 | solution.py:132
  689.2 91.8 %reduce-scatter.12.cloned.1.call-done = f32[640,1152]{1,0:T(8,128)} async-done(((f32[2560,1152]{1,0:T(8,128)}), f32[640,1152]{1,0:T(8,128)}) %reduce-scatter.12.cloned.1.call-update) | async-done | bytes 2949136 | tf_op jit(solution)/shard_map/reduce_scatter | solution.py:93
  791.5 57.3 %all-gather.19.cloned.1.call-done = bf16[2,1152,768]{2,1,0:T(8,128)(2,1)} async-done(((bf16[2,144,768]{2,1,0:T(8,128)(2,1)}), bf16[2,1152,768]{2,1,0:T(8,128)(2,1)}) %all-gather.19.cloned.1.call-update) | async-done | bytes 3538960 | tf_op jit(solution)/shard_map/all_gather | solution.py:235
  848.8 44.8 %all-gather.17.cloned.1.call-done = bf16[2560,1152]{1,0:T(8,128)(2,1)} async-done(((bf16[640,1152]{1,0:T(8,128)(2,1)}), bf16[2560,1152]{1,0:T(8,128)(2,1)}) %all-gather.17.cloned.1.call-update) | async-done | bytes 5898256 | tf_op jit(solution)/shard_map/all_gather | solution.py:89
  893.6 8.0 fusion.71
  904.8 8.8 multiply_convert_fusion.3
  913.5 28.8 all-gather.21.cloned.1.call-done
  942.3 10.1 fusion.124
  953.6 20.0 psum.43
  974.2 71.2 %reduce-scatter.14.cloned.1.call-done = f32[640,1152]{1,0:T(8,128)} async-done(((f32[2560,1152]{1,0:T(8,128)}), f32[640,1152]{1,0:T(8,128)}) %reduce-scatter.14.cloned.1.call-update) | async-done | bytes 2949136 | tf_op jit(solution)/shard_map/reduce_scatter | solution.py:93
  1065.8 43.8 %all-gather.23.cloned.1.call-done = bf16[2560,1152]{1,0:T(8,128)(2,1)} async-done(((bf16[640,1152]{1,0:T(8,128)(2,1)}), bf16[2560,1152]{1,0:T(8,128)(2,1)}) %all-gather.23.cloned.1.call-update) | async-done | bytes 5898256 | tf_op jit(solution)/shard_map/all_gather | solution.py:89
  1109.6 15.3 multiply_convert_fusion.1
  1132.4 9.7 convolution_add_fusion.2
  1142.4 93.8 %reduce-scatter.16.cloned.1.call-done = f32[640,1152]{1,0:T(8,128)} async-done(((f32[2560,1152]{1,0:T(8,128)}), f32[640,1152]{1,0:T(8,128)}) %reduce-scatter.16.cloned.1.call-update) | async-done | bytes 2949136 | tf_op jit(solution)/shard_map/reduce_scatter | solution.py:93
  1245.5 44.3 %all-gather.25.cloned.1.call-done = bf16[2560,1152]{1,0:T(8,128)(2,1)} async-done(((bf16[640,1152]{1,0:T(8,128)(2,1)}), bf16[2560,1152]{1,0:T(8,128)(2,1)}) %all-gather.25.cloned.1.call-update) | async-done | bytes 5898256 | tf_op jit(solution)/shard_map/all_gather | solution.py:89
  1301.8 175.6 %while.31 = (s32[]{:T(128)}, f32[2560,4,72]{0,2,1:T(8,128)}, f32[2560,4,72]{0,2,1:T(8,128)}, f32[2560,4,72]{0,2,1:T(8,128)}, s32[4]{0:T(128)S(1)}, /*index=5*/bf...) while((s32[]{:T(128)}, f32[2560,4,72]{0,2,1:T(8,128)}, ...), condition=%wide.region_25.26_spmd, body=%wide.region_23.25_spmd.sunk | while | flops 2151822848 | bytes 110149000 | solution.py:177
  1327.3 9.7 dynamic_update_slice.43
  1337.0 9.6 dynamic_update_slice.44
  1372.1 9.6 dynamic_update_slice.43
  1381.7 9.5 dynamic_update_slice.44
  1416.7 9.4 dynamic_update_slice.43
  1426.1 9.2 dynamic_update_slice.44
  1460.6 8.3 dynamic_update_slice.43
  1468.9 8.3 dynamic_update_slice.44
  1504.8 91.7 %reduce-scatter.24.cloned.1.call-done = f32[640,1152]{1,0:T(8,128)} async-done(((f32[2560,1152]{1,0:T(8,128)}), f32[640,1152]{1,0:T(8,128)}) %reduce-scatter.24.cloned.1.call-update) | async-done | bytes 2949136 | tf_op jit(solution)/shard_map/reduce_scatter | solution.py:93
  1608.8 10.5 fusion.126
  1619.5 9.1 convolution_bitcast_fusion
  1628.7 7.9 convolution_bitcast_fusion.1
  1662.8 8.6 copy.89
  1671.4 9.0 reshape.374
  1701.1 11.9 fusion.83
  1713.0 16.9 all-reduce.8
  1730.0 10.6 convert_reduce_fusion.3
  1750.1 36.2 %concatenate.34 = f32[2468,1152]{1,0:T(8,128)} concatenate(f32[1001,1152]{1,0:T(8,128)} %fusion.89, f32[256,1152]{1,0:T(8,128)S(1)} %fusion.98, f32[1,1152]{1,0:T(1,128)S(1)} %broadcast_in_dim.67, f32[1152,1152]{1,0:T(8,128)} %fusion.110, f32[1,1152]{1,0:T(1,128)S(1)} %broadcast_in_dim.106, f32[49,1152]{1,0:T(8,128)} %all-reduce.5.cloned.1.call-done, f32[8,1152]{1,0:T(8,128)S(1)} %reshape.363), dimensions={0} | concatenate | bytes 22745088 | tf_op jit(solution)/shard_map/concatenate | solution.py:353
  1790.2 17.1 fusion.107
  1809.8 46.6 %reduce-scatter.20.cloned.1.call-done = f32[2,144,768]{2,1,0:T(8,128)} async-done(((f32[2,1152,768]{2,1,0:T(8,128)}), f32[2,144,768]{2,1,0:T(8,128)}) %reduce-scatter.20.cloned.1.call-update) | async-done | bytes 884752 | tf_op jit(solution)/shard_map/reduce_scatter | solution.py:373
  1858.3 66.8 %reduce-scatter.18.cloned.1.call-done = f32[288,144]{0,1:T(8,128)} async-done(((f32[288,1152]{0,1:T(8,128)}), f32[288,144]{0,1:T(8,128)}) %reduce-scatter.18.cloned.1.call-update) | async-done | bytes 165904 | tf_op jit(solution)/shard_map/reduce_scatter | solution.py:372
  1926.7 89.4 %reduce-scatter.28.cloned.1.call-done = f32[144,864]{1,0:T(8,128)} async-done(((f32[1152,864]{1,0:T(8,128)}), f32[144,864]{1,0:T(8,128)}) %reduce-scatter.28.cloned.1.call-update) | async-done | bytes 497680
  2021.6 120.9 %all-reduce.7.cloned.1.call-done = f32[617,1152]{1,0:T(8,128)} async-done(((f32[617,1152]{1,0:T(8,128)}), f32[617,1152]{1,0:T(8,128)}) %all-reduce.7.cloned.1.call-update) | async-done | bytes 2843152 | tf_op jit(solution)/shard_map/psum | solution.py:369
  2146.3 672.3 %reduce-scatter.26.cloned.1.call-done = f32[144,9216]{1,0:T(8,128)} async-done(((f32[1152,9216]{1,0:T(8,128)}), f32[144,9216]{1,0:T(8,128)}) %reduce-scatter.26.cloned.1.call-update) | async-done | bytes 5308432 | tf_op jit(solution)/shard_map/reduce_scatter | solution.py:342
  2823.9 39.7 %all-reduce = (f32[]{:T(128)}, f32[]{:T(128)}) all-reduce(f32[]{:T(128)} %get-tuple-element.465, f32[]{:T(128)S(6)} %add.447), channel_id=1, replica_groups=mesh['dp'=8,'mp'=4] {'dp','mp'}, use_global_device_ids=true, to_apply=%region_15.16 | all-reduce | flops 2 | bytes 16 | tf_op jit(solution)/shard_map/psum | solution.py:385
  2883.4 8.9 multiply_subtract_fusion
  (459 shorter events, 432.1 us)
Async XLA Ops:
  7.2 57.5 %copy-start = (bf16[16,640]{1,0:T(8,128)(2,1)S(1)}, bf16[16,640]{1,0:T(8,128)(2,1)}, u32[]{:S(2)}) copy-start(bf16[16,640]{1,0:T(8,128)(2,1)} %param.30) | copy-start | bytes 61444
  7.2 49.3 %all-gather.27.cloned.1.call-start = ((), (), s32[]{:S(2)}) async-start(), calls=%async_computation.27 | async-start | bytes 7188480 | tf_op jit(solution)/shard_map/all_gather | solution.py:238
  10.3 455.0 %all-gather.11.cloned.1.call-start = ((), (), s32[]{:S(2)}) async-start(), calls=%async_computation.9 | async-start | bytes 23887872 | tf_op jit(solution)/shard_map/all_gather | solution.py:239
  14.8 525.7 %all-gather.15.cloned.1.call-start = ((), (), s32[]{:S(2)}) async-start(), calls=%async_computation.11 | async-start | bytes 2985984 | tf_op jit(solution)/shard_map/all_gather | solution.py:233
  16.6 568.1 %all-gather.13.cloned.1.call-start = ((), (), s32[]{:S(2)}) async-start(), calls=%async_computation.10 | async-start | bytes 7372800 | tf_op jit(solution)/shard_map/all_gather | solution.py:89
  16.8 457.1 %copy-start.60 = (s32[640]{0:T(1024)}, s32[640]{0:T(1024)S(1)}, u32[]{:S(2)}) copy-start(s32[640]{0:T(1024)S(1)} %dynamic_slice.103) | copy-start | bytes 7684
  16.9 49.8 %copy-start.83 = (bf16[16,128]{1,0:T(8,128)(2,1)}, bf16[16,128]{1,0:T(8,128)(2,1)S(1)}, u32[]{:S(2)}) copy-start(bf16[16,128]{1,0:T(8,128)(2,1)S(1)} %get-tuple-element.466) | copy-start | bytes 12292
  16.9 49.8 %copy-start.85 = (bf16[16,128]{1,0:T(8,128)(2,1)}, bf16[16,128]{1,0:T(8,128)(2,1)S(1)}, u32[]{:S(2)}) copy-start(bf16[16,128]{1,0:T(8,128)(2,1)S(1)} %get-tuple-element.467) | copy-start | bytes 12292
  66.2 417.7 %copy-start.5 = (f32[640,1152]{1,0:T(8,128)}, f32[640,1152]{1,0:T(8,128)S(1)}, u32[]{:S(2)}) copy-start(f32[640,1152]{1,0:T(8,128)S(1)} %get-tuple-element.472) | copy-start | bytes 8847364
  66.2 417.7 %copy-start.71 = (f32[640]{0:T(1024)}, f32[640]{0:T(1024)S(1)}, u32[]{:S(2)}) copy-start(f32[640]{0:T(1024)S(1)} %broadcast_multiply_fusion.11) | copy-start | bytes 7684
  68.5 415.4 %copy-start.78 = (f32[640]{0:T(1024)}, f32[640]{0:T(1024)S(1)}, u32[]{:S(2)}) copy-start(f32[640]{0:T(1024)S(1)} %add_rsqrt_fusion.2) | copy-start | bytes 7684
  73.2 400.7 %copy-start.51 = (f32[16,1152]{1,0:T(8,128)}, f32[16,1152]{1,0:T(8,128)S(1)}, u32[]{:S(2)}) copy-start(f32[16,1152]{1,0:T(8,128)S(1)} %fusion.57) | copy-start | bytes 221188
  493.7 287.3 %reduce-scatter.12.cloned.1.call-start = ((), (), s32[]{:S(2)}) async-start(), calls=%async_computation.12 | async-start | bytes 14745600 | tf_op jit(solution)/shard_map/reduce_scatter | solution.py:93
  533.0 61.4 %copy-start.33 = (f32[2560,18]{0,1:T(8,128)}, f32[2560,18]{0,1:T(8,128)S(1)}, u32[]{:S(2)}) copy-start(f32[2560,18]{0,1:T(8,128)S(1)} %get-tuple-element.460) | copy-start | bytes 552964
  533.0 61.5 %copy-start.35 = (f32[2560,18]{0,1:T(8,128)}, f32[2560,18]{0,1:T(8,128)S(1)}, u32[]{:S(2)}) copy-start(f32[2560,18]{0,1:T(8,128)S(1)} %get-tuple-element.469) | copy-start | bytes 552964
  686.9 161.9 %all-gather.19.cloned.1.call-start = ((), (), s32[]{:S(2)}) async-start(), calls=%async_computation.14 | async-start | bytes 3981312 | tf_op jit(solution)/shard_map/all_gather | solution.py:235
  688.9 204.7 %all-gather.17.cloned.1.call-start = ((), (), s32[]{:S(2)}) async-start(), calls=%async_computation.13 | async-start | bytes 7372800 | tf_op jit(solution)/shard_map/all_gather | solution.py:89
  785.1 455.1 %copy-start.2 = (f32[640,1152]{1,0:T(8,128)}, f32[640,1152]{1,0:T(8,128)S(1)}, u32[]{:S(2)}) copy-start(f32[640,1152]{1,0:T(8,128)S(1)} %get-tuple-element.424) | copy-start | bytes 8847364
  785.1 455.1 %copy-start.67 = (f32[640]{0:T(1024)}, f32[640]{0:T(1024)S(1)}, u32[]{:S(2)}) copy-start(f32[640]{0:T(1024)S(1)} %broadcast_multiply_fusion.10) | copy-start | bytes 7684
  785.5 454.7 %copy-start.73 = (f32[640]{0:T(1024)}, f32[640]{0:T(1024)S(1)}, u32[]{:S(2)}) copy-start(f32[640]{0:T(1024)S(1)} %add_rsqrt_fusion.1) | copy-start | bytes 7684
  790.7 151.7 %all-gather.21.cloned.1.call-start = ((), (), s32[]{:S(2)}) async-start(), calls=%async_computation.15 | async-start | bytes 1990656 | tf_op jit(solution)/shard_map/all_gather | solution.py:236
  791.4 254.0 %reduce-scatter.14.cloned.1.call-start = ((), (), s32[]{:S(2)}) async-start(), calls=%async_computation.16 | async-start | bytes 14745600 | tf_op jit(solution)/shard_map/reduce_scatter | solution.py:93
  893.6 11.1 copy-start.90
  893.6 11.1 copy-start.91
  952.4 21.4 copy-start.61
  952.4 157.2 %all-gather.23.cloned.1.call-start = ((), (), s32[]{:S(2)}) async-start(), calls=%async_computation.17 | async-start | bytes 7372800 | tf_op jit(solution)/shard_map/all_gather | solution.py:89
  1065.3 171.0 %reduce-scatter.16.cloned.1.call-start = ((), (), s32[]{:S(2)}) async-start(), calls=%async_computation.18 | async-start | bytes 14745600 | tf_op jit(solution)/shard_map/reduce_scatter | solution.py:93
  1109.6 15.3 copy-start.92
  1142.2 147.6 %all-gather.25.cloned.1.call-start = ((), (), s32[]{:S(2)}) async-start(), calls=%async_computation.19 | async-start | bytes 7372800 | tf_op jit(solution)/shard_map/all_gather | solution.py:89
  1245.5 351.0 %reduce-scatter.24.cloned.1.call-start = ((), (), s32[]{:S(2)}) async-start(), calls=%async_computation.23 | async-start | bytes 14745600 | tf_op jit(solution)/shard_map/reduce_scatter | solution.py:93
  1479.5 15.4 copy-start.25
  1502.5 247.6 %all-reduce.5.cloned.1.call-start = ((), (), s32[]{:S(2)}) async-start(), calls=%async_computation.25 | async-start | bytes 516096 | tf_op jit(solution)/shard_map/psum | solution.py:338
  1503.9 96.5 %copy-start.72 = (f32[640]{0:T(1024)S(1)}, f32[640]{0:T(1024)}, u32[]{:S(2)}) copy-start(f32[640]{0:T(1024)} %copy-done.71) | copy-start | bytes 7684
  1503.9 96.5 %copy-start.79 = (f32[640]{0:T(1024)S(1)}, f32[640]{0:T(1024)}, u32[]{:S(2)}) copy-start(f32[640]{0:T(1024)} %copy-done.78) | copy-start | bytes 7684
  1504.8 95.6 %copy-start.6 = (f32[640,1152]{1,0:T(8,128)S(1)}, f32[640,1152]{1,0:T(8,128)}, u32[]{:S(2)}) copy-start(f32[640,1152]{1,0:T(8,128)} %copy-done.5) | copy-start | bytes 8847364
  1608.8 199.2 %reduce-scatter.22.cloned.1.call-start = ((), (), s32[]{:S(2)}) async-start(), calls=%async_computation.22 | async-start | bytes 3981312 | tf_op jit(solution)/shard_map/reduce_scatter | solution.py:374
  1619.3 237.0 %reduce-scatter.20.cloned.1.call-start = ((), (), s32[]{:S(2)}) async-start(), calls=%async_computation.21 | async-start | bytes 7962624 | tf_op jit(solution)/shard_map/reduce_scatter | solution.py:373
  1639.9 285.2 %reduce-scatter.18.cloned.1.call-start = ((), (), s32[]{:S(2)}) async-start(), calls=%async_computation.20 | async-start | bytes 1990656 | tf_op jit(solution)/shard_map/reduce_scatter | solution.py:372
  1648.4 367.7 %reduce-scatter.28.cloned.1.call-start = ((), (), s32[]{:S(2)}) async-start(), calls=%async_computation.28 | async-start | bytes 4644864
  1680.4 462.0 %all-reduce.7.cloned.1.call-start = ((), (), s32[]{:S(2)}) async-start(), calls=%async_computation.26 | async-start | bytes 5750784 | tf_op jit(solution)/shard_map/psum | solution.py:369
  1701.1 28.8 copy-start.52
  1729.9 10.6 copy-start.77
  1790.0 1028.7 %reduce-scatter.26.cloned.1.call-start = ((), (), s32[]{:S(2)}) async-start(), calls=%async_computation.24 | async-start | bytes 47775744 | tf_op jit(solution)/shard_map/reduce_scatter | solution.py:342
  2145.6 720.0 %copy-start.44 = (f32[3,144,288]{2,1,0:T(8,128)S(1)}, f32[3,144,288]{2,1,0:T(8,128)}, u32[]{:S(2)}) copy-start(f32[3,144,288]{2,1,0:T(8,128)} %param.38) | copy-start | bytes 1492996
  2818.6 52.1 %copy-start.63 = (f32[768,144]{0,1:T(8,128)S(1)}, f32[768,144]{0,1:T(8,128)}, u32[]{:S(2)}) copy-start(f32[768,144]{0,1:T(8,128)} %param.49) | copy-start | bytes 1327108
  2818.6 54.6 %copy-start.57 = (f32[2,144,768]{2,1,0:T(8,128)S(1)}, f32[2,144,768]{2,1,0:T(8,128)}, u32[]{:S(2)}) copy-start(f32[2,144,768]{2,1,0:T(8,128)} %param.45) | copy-start | bytes 2654212
  2823.2 45.5 %copy-start.53 = (f32[288,144]{0,1:T(8,128)S(1)}, f32[288,144]{0,1:T(8,128)}, u32[]{:S(2)}) copy-start(f32[288,144]{0,1:T(8,128)} %reduce-scatter.18.cloned.1.call-done) | copy-start | bytes 497668
  2823.2 45.5 %copy-start.55 = (f32[288,144]{0,1:T(8,128)S(1)}, f32[288,144]{0,1:T(8,128)}, u32[]{:S(2)}) copy-start(f32[288,144]{0,1:T(8,128)} %param.41) | copy-start | bytes 497668
  (80 other events, 369.6 us)
Sparse Core Ops, SparseCore 0:
  10.5 46.0 all-gather.26
  58.6 406.6 all-gather.10
  468.2 72.1 all-gather.14
  542.4 42.2 all-gather.12
  687.0 93.8 reduce-scatter.11
  783.6 65.1 all-gather.18
  850.9 42.6 all-gather.16
  896.4 45.9 all-gather.20
  952.5 92.8 reduce-scatter.13
  1065.4 44.1 all-gather.22
  1142.3 93.8 reduce-scatter.15
  1245.6 44.1 all-gather.24
  1502.6 93.8 reduce-scatter.23
  1608.9 31.8 all-reduce.4
  1644.7 79.0 reduce-scatter.21
  1727.7 128.5 reduce-scatter.19
  1860.2 64.8 reduce-scatter.17
  1929.6 86.5 reduce-scatter.27
  2020.4 122.0 all-reduce.6
  2146.7 671.9 reduce-scatter.25
where the time goes:
time: 2920 us; the launch traced here: 2900 us
  waiting for transfers between devices  2040 us (70%)
  matrix products  352 us (12%)
  local copies, waits for them, and re-layouts  195 us (7%)
  other arithmetic  148 us (5%)
  blocking collectives  113 us (4%)
    reduce_scatter x1, waiting for transfers between devices, per_device(): lax.psum_scatter(matmul_tn(cond_scaled, grad_mod_b), 'dp', scatter_dimens...  672 us
    all_gather x1, waiting for transfers between devices, per_device(): mod_all = lax.all_gather(mod_w.astype(low_type), 'dp', axis=0, tiled=True)  392 us
    reduce_scatter x4, waiting for transfers between devices, scatter_rows(): return lax.psum_scatter(values, 'mp', scatter_dimension=0, tiled=True)  349 us
    all_gather x4, waiting for transfers between devices, gather_rows(): return lax.all_gather(values, 'mp', axis=0, tiled=True)  174 us
    psum x1, waiting for transfers between devices, per_device(): grad_table = lax.psum(grad_table_own, 'dp')  121 us
    unnamed x21, waiting for transfers between devices  89.7 us
    dot_general x13, matrix products, matmul_tn(): lax.dot_general(left, right, (((0,), (0,)), ((), ())), preferred_element_...  75.7 us
    dot_general x10, matrix products, matmul_nt(): lax.dot_general(left, right, (((1,), (1,)), ((), ())), preferred_element_...  71 us
  transfers between devices with their start and end apart: 20, of which 18 were waited for; matrix products, arithmetic and copies ran while one was open for 9% of the time, Pallas kernels for 0%

commit v1 on v0

v1 whole, which is shorter than its diff:
```python
import functools
import math

import jax
import jax.numpy as jnp
from jax import lax
from jax.experimental import pallas as pl
from jax.experimental.pallas import tpu as pltpu
from jax.sharding import PartitionSpec as P

D = 1152
HD = 72
PATCH_IN = 16
OUT = 32
FREQ = 256
NCLS = 1001
PAIR = 320

ROW_TIME_IN = NCLS
ROW_TIME_BIAS = ROW_TIME_IN + FREQ
ROW_TIME_OUT = ROW_TIME_BIAS + 1
ROW_OUT_BIAS = ROW_TIME_OUT + D
ROW_PATCH = ROW_OUT_BIAS + 1
ROW_PATCH_BIAS = ROW_PATCH + PATCH_IN
ROW_HEAD = ROW_PATCH_BIAS + 1
ROW_MOD_BIAS = ROW_HEAD + OUT
ROWS = ROW_MOD_BIAS + 8
TAIL = ROWS - ROW_PATCH

EPS_NORM = 1e-06
BETA_ONE = 0.9
BETA_TWO = 0.95
ADAM_EPS = 1e-08
LEARN_RATE = 0.03
WEIGHT_DECAY = 0.1
CLIP_SCALE = 0.5
LOW = jnp.bfloat16
F32 = jnp.float32
BOTH = ("dp", "mp")
MESH = pl.DeviceIdType.MESH
STEP = 1152
HOOKS = (0, 1, 2, 4)
LINE_FIRST = (True, True, False)
DEPTH = 4


def matmul(left, right):
    return jnp.dot(left, right, preferred_element_type=F32)


def matmul_tn(left, right):
    return lax.dot_general(left, right, (((0,), (0,)), ((), ())), preferred_element_type=F32)


def matmul_nt(left, right):
    return lax.dot_general(left, right, (((1,), (1,)), ((), ())), preferred_element_type=F32)


def layer_norm(values):
    centred = values - jnp.mean(values, -1, keepdims=True)
    inv_std = lax.rsqrt(jnp.mean(centred * centred, -1, keepdims=True) + EPS_NORM)
    return (centred * inv_std, inv_std)


def norm_back(grad, normed, inv_std, scale_rows):
    inner = grad * (1.0 + scale_rows)
    return inv_std * (
        inner
        - jnp.mean(inner, -1, keepdims=True)
        - normed * jnp.mean(inner * normed, -1, keepdims=True)
    )


def silu_slope(values):
    sigma = jax.nn.sigmoid(values)
    return sigma * (1.0 + values * (1.0 - sigma))


def adam(weight, first, second, grad, count):
    first = BETA_ONE * first + (1.0 - BETA_ONE) * grad
    second = BETA_TWO * second + (1.0 - BETA_TWO) * grad * grad
    m_hat = first / (1.0 - BETA_ONE**count)
    v_hat = second / (1.0 - BETA_TWO**count)
    weight = weight - LEARN_RATE * (m_hat / (jnp.sqrt(v_hat) + ADAM_EPS) + WEIGHT_DECAY * weight)
    return (weight, first, second)


def rotary_tables(positions):
    quarter = HD // 4
    freqs = jnp.exp(-math.log(10000.0) * jnp.arange(quarter, dtype=F32) / quarter)
    angle = positions.astype(F32)[:, :, None] * freqs[None, None, :]
    cosine, sine = jnp.cos(angle), jnp.sin(angle)
    cos_row = jnp.concatenate([cosine[0], cosine[0], cosine[1], cosine[1]], 1)
    sin_row = jnp.concatenate([-sine[0], sine[0], -sine[1], sine[1]], 1)
    return cos_row, sin_row


def coordinates():
    dp, mp = lax.axis_index("dp"), lax.axis_index("mp")
    z, x = dp // 2, dp % 2
    y, c = mp // 2, mp % 2
    first = (x + (1 - c) * (1 - 2 * x), y + c * (1 - 2 * y))
    second = (x + c * (1 - 2 * x), y + (1 - c) * (1 - 2 * y))
    return z, x, y, c, first, second


def greet(z, x, y, c, first, second, depth):
    barrier = pltpu.get_barrier_semaphore()

    def signal(dp, mp):
        pl.semaphore_signal(barrier, inc=1, device_id=(dp, mp), device_id_type=MESH)

    signal(z * 2 + first[0], first[1] * 2 + c)
    signal(z * 2 + second[0], second[1] * 2 + c)
    signal(z * 2 + x, y * 2 + 1 - c)
    pl.when(z > 0)(lambda: signal((z - 1) * 2 + x, y * 2 + c))
    pl.when(z < depth - 1)(lambda: signal((z + 1) * 2 + x, y * 2 + c))
    peers = 3 + jnp.minimum(z, 1) + jnp.minimum(depth - 1 - z, 1)
    pl.semaphore_wait(barrier, peers)


def peers_greet(dp_count, mp_count):
    dp, mp = lax.axis_index("dp"), lax.axis_index("mp")
    barrier = pltpu.get_barrier_semaphore()
    for hop in range(1, dp_count):
        pl.semaphore_signal(
            barrier, inc=1, device_id=(lax.rem(dp + hop, dp_count), mp), device_id_type=MESH
        )
    for hop in range(1, mp_count):
        pl.semaphore_signal(
            barrier, inc=1, device_id=(dp, lax.rem(mp + hop, mp_count)), device_id_type=MESH
        )
    pl.semaphore_wait(barrier, dp_count + mp_count - 2)


class Round:
    def __init__(self, axis, count, source, target, send, recv, base):
        self.me = lax.axis_index(axis)
        self.axis, self.count, self.source, self.target = axis, count, source, target
        self.send, self.recv, self.base = send, recv, base

    def moves(self):
        for hop in range(1, self.count):
            peer = lax.rem(self.me + hop, self.count)
            other = {"dp": (peer, lax.axis_index("mp")), "mp": (lax.axis_index("dp"), peer)}[self.axis]
            yield pltpu.make_async_remote_copy(
                src_ref=self.source(peer), dst_ref=self.target.at[self.me],
                send_sem=self.send.at[self.base + hop], recv_sem=self.recv.at[self.base + hop],
                device_id=other, device_id_type=MESH,
            )

    def push(self):
        for move in self.moves():
            move.start()

    def wait(self):
        for hop in range(1, self.count):
            slot = self.target.at[lax.rem(self.me + self.count - hop, self.count)]
            pltpu.make_async_copy(slot, slot, self.recv.at[self.base + hop]).wait()

    def finish(self):
        for move in self.moves():
            move.wait_send()


def gather_kernel(
    depth, mp_count, wa_ref, wf_ref, info_ref, emb_ref, t1_ref, b1_ref, t2_ref, part_ref, tail_ref, mcol_ref,
    wa_all, wf_all, mod_ref, tails_ref, pre_ref, cond_ref, scaled_ref, infos_ref, hid_ref,
    info_buf, pre_sum, cond_sum, tail_buf, scaled_buf, hid_buf, mod_part, mod_sum, mod_buf,
    recv, send, local, little_recv, little_send,
):
    dp_count = 2 * depth
    z, x, y, c, first, second = coordinates()
    dp, mp = lax.axis_index("dp"), lax.axis_index("mp")
    rows = wa_ref.shape[0]
    images = emb_ref.shape[0]
    peers_greet(dp_count, mp_count)

    bases = iter(range(0, 64 * dp_count, dp_count))
    little = lambda axis, count, source, target: Round(
        axis, count, source, target, little_send, little_recv, next(bases)
    )
    own = lambda buf, me: lambda peer: buf.at[me]
    info = little("dp", dp_count, own(info_buf, dp), info_buf)
    pre_r = little("mp", mp_count, own(pre_sum, mp), pre_sum)
    tail_r = little("mp", mp_count, own(tail_buf, mp), tail_buf)
    cond_r = little("mp", mp_count, own(cond_sum, mp), cond_sum)
    scaled_a = little("dp", dp_count, own(scaled_buf, dp), scaled_buf)
    hid_a = little("dp", dp_count, own(hid_buf, dp), hid_buf)
    mod_r = little("dp", dp_count, lambda peer: mod_part.at[peer], mod_sum)
    mod_a = little("mp", mp_count, own(mod_buf, mp), mod_buf)
    rounds = (info, pre_r, tail_r, cond_r, scaled_a, hid_a, mod_r, mod_a)
    total = lambda buf, count: functools.reduce(lambda a, b: a + b, [buf[i] for i in range(count)])

    def begin():
        info_buf[dp] = info_ref[...]
        info.push()
        pre_sum[mp] = dot(emb_ref[...], t1_ref[...]) + b1_ref[...]
        pre_r.push()
        tail_buf[mp] = tail_ref[...]
        tail_r.push()

    def hidden():
        pre_r.wait()
        pre = total(pre_sum, mp_count)
        pre_ref[...] = pre
        act = (pre * lax.logistic(pre)).astype(LOW)
        cond_sum[mp] = dot(act, t2_ref[...]) + part_ref[...]
        cond_r.push()
        hid_buf[dp] = act

    def condition():
        cond_r.wait()
        cond = total(cond_sum, mp_count)
        cond_ref[...] = cond
        scaled_buf[dp] = (cond * lax.logistic(cond)).astype(LOW)
        scaled_a.push()

    def modulate():
        scaled_a.wait()
        scaled = scaled_buf[...].reshape(dp_count * images, D)
        row = lax.broadcasted_iota(jnp.int32, (D, rows), 0)
        col = lax.broadcasted_iota(jnp.int32, (D, rows), 1)
        pick = (row == col + dp * rows).astype(F32).astype(LOW)
        mine = dot(scaled, pick).astype(LOW)
        mod_part[...] = dot(mine, mcol_ref[...]).reshape(mod_part.shape)
        mod_sum[dp] = mod_part[dp]
        mod_r.push()

    def collect():
        mod_r.wait()
        mod_buf[mp] = total(mod_sum, dp_count)
        mod_a.push()
        hid_a.push()

    hooks = (hidden, condition, modulate, collect)

    sent = []
    corner = (first[0] + second[0] - x, first[1] + second[1] - y)
    spots = {"here": (x, y), "first": first, "second": second, "corner": corner}
    ids = {"here": 0, "first": 1, "second": 2, "corner": 3}
    swapped = {"here": 0, "first": 2, "second": 1, "corner": 3}
    groups = [(wa_ref, wa_all, 0, LINE_FIRST[0])]
    groups += [(wf_ref, wf_all, i * STEP, LINE_FIRST[1 + i]) for i in range(wf_ref.shape[1] // STEP)]
    count = len(groups)

    def slot(g, zz, spot, core):
        _, ref, column, _ = groups[g]
        return ref.at[spot[1] * 2 + core, pl.ds((zz * 2 + spot[0]) * rows, rows), pl.ds(column, STEP)]

    def mine(g):
        return groups[g][0].at[:, pl.ds(groups[g][2], STEP)]

    def copy(g, zz, kind, route, cond=None, own=False):
        plane, sem_kind = 0, kind
        if route == "up":
            target = ((z + 1) * 2 + x, mp)
        elif route == "down":
            target = ((z - 1) * 2 + x, mp)
        elif route == "first":
            target, sem_kind = (z * 2 + first[0], first[1] * 2 + c), "first"
        elif route == "second":
            target = (z * 2 + second[0], second[1] * 2 + c)
            sem_kind = "second" if kind == "here" else "corner"
        else:
            target, plane = (dp, y * 2 + 1 - c), 1
        made = pltpu.make_async_remote_copy(
            src_ref=mine(g) if own else slot(g, zz, spots[kind], c), dst_ref=slot(g, zz, spots[kind], c),
            send_sem=send.at[len(sent)], recv_sem=recv.at[g, plane, ids[sem_kind], zz],
            device_id=target, device_id_type=MESH,
        )
        sent.append((made, cond))
        if cond is None:
            made.start()
        else:
            pl.when(cond)(made.start)

    def arrive(g, zz, kind, cond=None, plane=0):
        dst = slot(g, zz, spots[kind], c if plane == 0 else 1 - c)
        sem = recv.at[g, plane, ids[kind] if plane == 0 else swapped[kind], zz]
        wait = pltpu.make_async_copy(dst, dst, sem)
        if cond is None:
            wait.wait()
        else:
            pl.when(cond)(wait.wait)

    def sides(k):
        below, above = jnp.maximum(z - k, 0), jnp.minimum(z + k, depth - 1)
        return ((below, z >= k, "up", z < depth - 1), (above, z < depth - k, "down", z > 0))[: 1 if k == 0 else 2]

    def stage(g, k):
        line_first = groups[g][3]
        if k == 0:
            pltpu.make_async_copy(mine(g), slot(g, z, spots["here"], c), local.at[g]).start()
            copy(g, z, "here", "first", None, True)
            copy(g, z, "here", "up", z < depth - 1, True)
            copy(g, z, "here", "down", z > 0, True)
            copy(g, z, "here", "second", None, True)
            copy(g, z, "here", "core", None, True)
        if k == 1 and not line_first:
            arrive(g, z, "first")
            copy(g, z, "first", "up", z < depth - 1)
            copy(g, z, "first", "down", z > 0)
            copy(g, z, "first", "second")
            copy(g, z, "first", "core")
        if 0 < k < depth:
            for kind in ("here",):
                for zz, cond, route, more in sides(k):
                    arrive(g, zz, kind, cond)
                    copy(g, zz, kind, route, cond & more)
                    if line_first:
                        copy(g, zz, kind, "first", cond)
                    copy(g, zz, kind, "second", cond)
                    copy(g, zz, kind, "core", cond)
        if line_first and 0 <= k - 1 < depth:
            for zz, cond, _, _ in sides(k - 1):
                arrive(g, zz, "first", cond)
                copy(g, zz, "first", "second", cond)
                copy(g, zz, "first", "core", cond)
        if not line_first and 0 < k - 1 < depth:
            for zz, cond, route, more in sides(k - 1):
                arrive(g, zz, "first", cond)
                copy(g, zz, "first", route, cond & more)
                copy(g, zz, "first", "second", cond)
                copy(g, zz, "first", "core", cond)
        if 0 <= k - 2 < depth:
            for zz, cond, _, _ in sides(k - 2):
                for kind in ("second", "corner"):
                    arrive(g, zz, kind, cond)
                    copy(g, zz, kind, "core", cond)

    begin()
    for moment in range(depth + 2 + count - 1):
        for g in range(count):
            if 0 <= moment - g < depth + 2:
                stage(g, moment - g)
        for number, hook in enumerate(hooks):
            if HOOKS[number] == moment:
                hook()
    mod_a.wait()
    hid_a.wait()
    info.wait()
    tail_r.wait()
    mod_ref[...] = mod_buf[...]
    tails_ref[...] = tail_buf[...]
    scaled_ref[...] = scaled_buf[...]
    infos_ref[...] = info_buf[...]
    hid_ref[...] = hid_buf[...]
    for g in range(count):
        for zz in range(depth):
            for kind in ("here", "first", "second", "corner"):
                arrive(g, zz, kind, None, 1)
        pltpu.make_async_copy(mine(g), slot(g, z, spots["here"], c), local.at[g]).wait()
    for made, cond in sent:
        if cond is None:
            made.wait_send()
        else:
            pl.when(cond)(made.wait_send)
    for one in rounds:
        one.finish()


def gather_pallas(wa, wf, small, dp, mp, collective_id=0):
    depth = dp // 2
    groups = 1 + wf.shape[1] // STEP
    images, width = small[1].shape[0], small[7].shape[1]
    tail = small[6].shape[0]
    shapes = [
        ((mp, images, width), F32), ((mp, tail, D), LOW), ((images, D), F32), ((images, D), F32),
        ((dp, images, D), LOW), ((dp, 8, 128), F32), ((dp, images, D), LOW),
    ]
    return pl.pallas_call(
        functools.partial(gather_kernel, depth, mp),
        out_shape=[jax.ShapeDtypeStruct((mp, dp * s.shape[0], s.shape[1]), s.dtype) for s in (wa, wf)]
        + [jax.ShapeDtypeStruct(*s) for s in shapes],
        in_specs=[pl.BlockSpec(memory_space=pl.ANY)] * 2 + [pl.BlockSpec(memory_space=pltpu.VMEM)] * 8,
        out_specs=[pl.BlockSpec(memory_space=pl.ANY)] * 2 + [pl.BlockSpec(memory_space=pltpu.VMEM)] * 7,
        scratch_shapes=[
            pltpu.VMEM((dp, 8, 128), F32), pltpu.VMEM((mp, images, D), F32), pltpu.VMEM((mp, images, D), F32),
            pltpu.VMEM((mp, tail, D), LOW), pltpu.VMEM((dp, images, D), LOW), pltpu.VMEM((dp, images, D), LOW),
            pltpu.VMEM((dp, images, width), F32), pltpu.VMEM((dp, images, width), F32),
            pltpu.VMEM((mp, images, width), F32),
            pltpu.SemaphoreType.DMA((groups, 2, 4, depth)),
            pltpu.SemaphoreType.DMA((groups * 64,)),
            pltpu.SemaphoreType.DMA((groups,)),
            pltpu.SemaphoreType.DMA((8 * dp,)),
            pltpu.SemaphoreType.DMA((8 * dp,)),
        ],
        compiler_params=pltpu.CompilerParams(
            collective_id=collective_id, has_side_effects=True, vmem_limit_bytes=48 * 1024 * 1024
        ),
        name="gather_weights",
    )(wa, wf, *small)


TOP = 32766.0
RING = 14
ORDER = (
    (0, 0, 0), (0, 0, 2), (0, 0, 1), (0, 2, 0), (0, 0, 3), (1, 0, 0), (0, 2, 2), (2, 0, 3), (1, 0, 1), (0, 2, 1),
    (0, 1, 0), (1, 1, 0), (1, 1, 1), (1, 2, 0), (2, 0, 0), (1, 2, 1), (1, 0, 2), (0, 1, 2), (2, 1, 1), (0, 1, 1),
    (1, 0, 3), (1, 3, 1), (1, 2, 2), (2, 0, 1), (1, 1, 2), (0, 3, 0), (2, 1, 0), (2, 1, 3), (0, 1, 3), (2, 0, 2),
    (0, 3, 1), (0, 3, 2), (2, 2, 0), (1, 2, 3), (2, 2, 1), (1, 3, 0), (2, 1, 2), (2, 2, 2), (1, 3, 2), (0, 2, 3),
    (2, 2, 3), (2, 3, 0), (2, 3, 1), (1, 1, 3), (2, 3, 2), (0, 3, 3), (1, 3, 3), (2, 3, 3),
)


def lookup(values, base, t):
    digits = {4: 15, 64: 5}[base]
    words = [
        sum(v * base**i for i, v in enumerate(values[at : at + digits])) for at in range(0, len(values), digits)
    ]
    word = functools.reduce(lambda a, iw: jnp.where(t // digits == iw[0], iw[1], a), enumerate(words), 0)
    unit = functools.reduce(lambda a, i: jnp.where(t % digits == i, base**i, a), range(digits), 1)
    return word // unit % base


def encode(value):
    peak = jnp.maximum(jnp.max(jnp.abs(value), 0, keepdims=True), 1e-30)
    return jnp.round(value * (TOP / peak)).astype(jnp.int32).astype(jnp.int16), peak * (1.0 / TOP)


def decode(code, unit):
    return code.astype(jnp.int32).astype(F32) * unit


def weight_grad_kernel(
    depth, widths, mp_count, at_ref, pt_ref, mt_ref, ot_ref, ya_ref, yf_ref, gmod_ref, mod_ref, t2_ref, cond_ref, pre_ref,
    out_ref, vec_ref,
    x_all, ya_all, yf_all, work, q_send, u_send, q_recv, u_recv,
    gmod, panel, scaled_send, scaled_recv, joined, own_vec, hid_part, vec_buf,
    moves, swaps, landing, send, recv, panel_sem, little_send, little_recv,
):
    z, x, y, c, first, second = coordinates()
    dp_count = 2 * depth
    peers_greet(dp_count, mp_count)
    rows = out_ref.shape[1]
    x_refs = (at_ref, pt_ref, mt_ref, ot_ref)
    tokens = at_ref.shape[1]
    width_a, width_f = widths
    here = (x, y)
    corner = (first[0] + second[0] - x, first[1] + second[1] - y)
    mate = (z * 2 + x, y * 2 + 1 - c)
    total = len(ORDER)

    own, theirs = pl.ds(0, tokens), pl.ds(tokens, tokens)
    local, remote = [], []

    def trade(mine, give, to, land):
        n = len(local)
        remote.append(pltpu.make_async_remote_copy(
            src_ref=give, dst_ref=land, send_sem=swaps.at[n], recv_sem=landing.at[n],
            device_id=mate, device_id_type=MESH,
        ))
        local.append(pltpu.make_async_copy(mine, to, moves.at[n]))
        remote[-1].start()
        local[-1].start()

    def trade_x(i):
        trade(x_refs[i], x_refs[i], x_all.at[i, :, own], x_all.at[i, :, theirs])

    def trade_y(ref, full, j):
        trade(ref.at[2 * j + c], ref.at[2 * j + 1 - c], full.at[j, own, :], full.at[j, theirs, :])

    trade_x(2)
    trade_y(yf_ref, yf_all, 1 - y)
    trade_x(3)
    trade_x(0)
    trade_x(1)
    trade_y(ya_ref, ya_all, 1 - y)
    trade_y(yf_ref, yf_all, y)
    trade_y(ya_ref, ya_all, y)
    waits, known = [], set()
    for t, (g, kind, _) in enumerate(ORDER):
        need = [{0, 1}, {0, 1, 2}, {3, 4, 5}][g] | (set() if kind == 0 else {7} if g == 2 else {6})
        if need - known:
            waits.append((t, sorted(need - known)))
            known |= need

    def ready(numbers):
        for n in numbers:
            local[n].wait()
            remote[n].wait_recv()

    codes = tuple(16 * g + 4 * kind + j for g, kind, j in ORDER)

    def plan(t):
        code = lookup(codes, 64, t)
        g, kind, j = code // 16, code // 4 % 4, code % 4
        falling = jnp.where(depth - 1 - j <= z, depth - 2 - j, depth - 1 - j)
        rising = jnp.where(j >= z, j + 1, j)
        zz = jnp.where(z * 2 < depth, falling, rising)
        zz = jnp.where(j == depth - 1, z, zz)
        pick = lambda i: jnp.where(
            kind == 0, corner[i], jnp.where(kind == 1, second[i], jnp.where(kind == 2, first[i], here[i]))
        )
        return g, kind, zz, pick(0), pick(1)

    def product(g, zz, xx, yy):
        cut = pl.ds((zz * 2 + xx) * rows, rows)

        @pl.when(g == 0)
        def _():
            work[...] = dot(x_all[2, cut, :], yf_all[yy, :, :STEP])

        @pl.when(g == 1)
        def _():
            middle = 2 * width_f - STEP
            work[:, :middle] = dot(x_all[2, cut, :], yf_all[yy, :, STEP : 2 * width_f])
            work[:, middle:] = dot(x_all[3, cut, :], yf_all[yy, :, 2 * width_f :])

        @pl.when(g == 2)
        def _():
            edge = 3 * width_a
            low, high = edge // 128 * 128, -(-edge // 128) * 128
            left = dot(x_all[0, cut, :], ya_all[yy, :, :high])
            right = dot(x_all[1, cut, :], ya_all[yy, :, low:])
            lane = lax.broadcasted_iota(jnp.int32, (rows, high - low), 1)
            work[:, :low] = left[:, :low]
            work[:, low:high] = jnp.where(lane < edge - low, left[:, low:], right[:, : high - low])
            work[:, high:] = right[:, high - low :]

    def sent(slot):
        return (
            pltpu.make_async_copy(q_send.at[slot], q_send.at[slot], send.at[0, slot]),
            pltpu.make_async_copy(u_send.at[slot], u_send.at[slot], send.at[1, slot]),
        )

    def ship(t, g, dst_slot, target):
        slot = t % RING

        @pl.when(t >= RING)
        def _():
            for move in sent(slot):
                move.wait()

        code, unit = encode(work[...])
        q_send[slot] = code
        u_send[slot] = unit
        for i, (a, b) in enumerate(((q_send, q_recv), (u_send, u_recv))):
            pltpu.make_async_remote_copy(
                src_ref=a.at[slot], dst_ref=b.at[g, dst_slot],
                send_sem=send.at[i, slot], recv_sem=recv.at[i, g, dst_slot],
                device_id=target, device_id_type=MESH,
            ).start()

    def landed(g, slot):
        pltpu.make_async_copy(q_recv.at[g, slot], q_recv.at[g, slot], recv.at[0, g, slot]).wait()
        pltpu.make_async_copy(u_recv.at[g, slot], u_recv.at[g, slot], recv.at[1, g, slot]).wait()
        work[...] += decode(q_recv[g, slot], u_recv[g, slot])

    dp, mp = lax.axis_index("dp"), lax.axis_index("mp")
    bases = iter(range(0, 64 * dp_count, dp_count))
    little = lambda axis, count, source, target: Round(
        axis, count, source, target, little_send, little_recv, next(bases)
    )
    own_slot = lambda buf, me: lambda peer: buf.at[me]
    gmod_a = little("dp", dp_count, own_slot(gmod, dp), gmod)
    scaled_r = little("dp", dp_count, lambda peer: scaled_send.at[peer], scaled_recv)
    vec_m = little("mp", mp_count, own_slot(own_vec, mp), own_vec)
    hid_r = little("mp", mp_count, own_slot(hid_part, mp), hid_part)
    vec_a = little("dp", dp_count, own_slot(vec_buf, dp), vec_buf)
    lines = gmod_ref.shape[0]
    images = lines // 8

    def panels(count, source, use):
        fetch = lambda i: pltpu.make_async_copy(source(i), panel.at[i % 2], panel_sem.at[i % 2])
        fetch(0).start()
        for i in range(count):
            if i + 1 < count:
                fetch(i + 1).start()
            fetch(i).wait()
            use(i, panel.at[i % 2])

    def one_hot(shape, hit):
        row, col = (lax.broadcasted_iota(jnp.int32, shape, i) for i in range(2))
        return hit(row, col).astype(F32).astype(LOW)

    def begin():
        gmod[dp] = gmod_ref[...]
        gmod_a.push()

    def scaled_grad():
        gmod_a.wait()
        every = gmod[...].reshape(dp_count * lines, D)
        scaled_send[...] = jnp.zeros(scaled_send.shape, F32)

        def use(j, piece):
            hit = lambda r, q: (r // 8 == q // lines) & (q % lines == j * images + r % 8) & (r % 8 < images)
            part = dot(one_hot((8 * dp_count, dp_count * lines), hit), every).astype(LOW)
            scaled_send[...] += dot_nt(part, piece[...]).reshape(scaled_send.shape)

        panels(8, lambda j: mod_ref.at[:, pl.ds(j * D, D)], use)
        scaled_recv[dp] = scaled_send[dp]
        scaled_r.push()

    def vector_grad():
        scaled_r.wait()
        for d in range(dp_count):
            joined[:, d * rows : (d + 1) * rows] = scaled_recv[d]
        own_vec[mp] = (joined[...] * silu_slope(cond_ref[mp])).astype(LOW).astype(F32)
        vec_m.push()

    def hidden_grad():
        vec_m.wait()
        vectors = own_vec[...].reshape(8 * mp_count, D).astype(LOW)
        def use(i, piece):
            hid_part[mp, :, i * rows : (i + 1) * rows] = dot_nt(vectors, piece[...])

        panels(D // rows, lambda i: t2_ref.at[pl.ds(i * rows, rows), :], use)
        hid_r.push()

    def first_grad():
        hid_r.wait()
        grad = functools.reduce(lambda a, b: a + b, [hid_part[i] for i in range(mp_count)])
        grad_pre = (grad * silu_slope(pre_ref[...])).astype(LOW)
        vectors = own_vec[...].reshape(8 * mp_count, D).astype(LOW)
        hit = lambda r, q: (r // images == q // 8) & (r % images == q % 8)
        pick = one_hot((images * mp_count, 8 * mp_count), hit)
        count = images * mp_count
        vec_buf[dp, :count, :] = dot(pick, vectors).astype(LOW)
        vec_buf[dp, count:, :] = dot(pick, grad_pre).astype(LOW)
        vec_a.push()

    hooks = ((0, begin), (8, scaled_grad), (15, vector_grad), (20, hidden_grad), (27, first_grad))

    to_second = (z * 2 + second[0], second[1] * 2 + c)
    to_first = (z * 2 + first[0], first[1] * 2 + c)
    to_up = ((z + 1) * 2 + x, y * 2 + c)
    to_down = ((z - 1) * 2 + x, y * 2 + c)
    kept, passed = 2 * depth, 3 * depth + 1
    after_line = passed + depth + 1

    def step(t, _):
        g, kind, zz, xx, yy = plan(t)
        for at, numbers in waits:
            pl.when(t == at)(functools.partial(ready, numbers))
        for at, hook in hooks:
            pl.when(t == at)(hook)
        product(g, zz, xx, yy)
        line_first = g < 2
        late, mine = kind >= 2, zz == z
        along = late & ((kind == 3) | line_first)
        line = jnp.where(kind == 3, kept, passed)

        @pl.when(kind < 2)
        def _():
            ship(t, g, kind * depth + zz, to_second)

        @pl.when(late)
        def _():
            landed(g, (kind - 2) * depth + zz)

        @pl.when((kind == 3) & (jnp.logical_not(line_first) | mine))
        def _():
            landed(g, jnp.where(line_first, after_line, passed + zz))

        @pl.when(along & (zz >= z) & (z > 0))
        def _():
            landed(g, line + zz)

        @pl.when(along & (zz <= z) & (z < depth - 1))
        def _():
            landed(g, line + jnp.where(mine, depth, zz))

        @pl.when(along & (zz > z))
        def _():
            ship(t, g, line + zz, to_up)

        @pl.when(along & (zz < z))
        def _():
            ship(t, g, line + jnp.where(zz == z - 1, depth, zz), to_down)

        @pl.when((kind == 2) & (jnp.logical_not(line_first) | mine))
        def _():
            ship(t, g, jnp.where(line_first, after_line, passed + zz), to_first)

        @pl.when((kind == 3) & mine)
        def _():
            out_ref[g] = work[...]

        return 0

    lax.fori_loop(0, total, step, 0)

    def drain(slot, _):
        for move in sent(slot):
            move.wait()
        return 0

    lax.fori_loop(0, RING, drain, 0)
    for move in remote:
        move.wait_send()
    vec_a.wait()
    vec_ref[...] = vec_buf[...]
    for one in (gmod_a, scaled_r, vec_m, hid_r, vec_a):
        one.finish()


def weight_grads(turned, ya, yf, grad_mod, mod_rows, second, cond, pre, dp, collective_id=1):
    depth, mp = dp // 2, ya.shape[0]
    tokens = turned[0].shape[1]
    rows = D // dp
    slots = 4 * depth + 3
    images = grad_mod.shape[0] // 8
    hbm, vmem = pl.BlockSpec(memory_space=pl.ANY), pl.BlockSpec(memory_space=pltpu.VMEM)
    vectors = (dp, 2 * images * mp, D)
    return pl.pallas_call(
        functools.partial(weight_grad_kernel, depth, (ya.shape[2] // 4, yf.shape[2] // 3), mp),
        out_shape=[jax.ShapeDtypeStruct((3, rows, STEP), F32), jax.ShapeDtypeStruct(vectors, LOW)],
        in_specs=[hbm] * 6 + [vmem, hbm, hbm, vmem, vmem],
        out_specs=[vmem, vmem],
        scratch_shapes=[
            pltpu.VMEM((4, D, 2 * tokens), LOW),
            pltpu.VMEM((2, 2 * tokens, ya.shape[2]), LOW),
            pltpu.VMEM((2, 2 * tokens, yf.shape[2]), LOW),
            pltpu.VMEM((rows, STEP), F32),
            pltpu.VMEM((RING, rows, STEP), jnp.int16),
            pltpu.VMEM((RING, 1, STEP), F32),
            pltpu.VMEM((3, slots, rows, STEP), jnp.int16),
            pltpu.VMEM((3, slots, 1, STEP), F32),
            pltpu.VMEM((dp, *grad_mod.shape), LOW),
            pltpu.VMEM((2, rows, D), LOW),
            pltpu.VMEM((dp, 8, rows), F32),
            pltpu.VMEM((dp, 8, rows), F32),
            pltpu.VMEM((8, D), F32),
            pltpu.VMEM((mp, 8, D), F32),
            pltpu.VMEM((mp, 8 * mp, D), F32),
            pltpu.VMEM(vectors, LOW),
            pltpu.SemaphoreType.DMA((8,)),
            pltpu.SemaphoreType.DMA((8,)),
            pltpu.SemaphoreType.DMA((8,)),
            pltpu.SemaphoreType.DMA((2, RING)),
            pltpu.SemaphoreType.DMA((2, 3, slots)),
            pltpu.SemaphoreType.DMA((2,)),
            pltpu.SemaphoreType.DMA((5 * dp,)),
            pltpu.SemaphoreType.DMA((5 * dp,)),
        ],
        compiler_params=pltpu.CompilerParams(
            collective_id=collective_id, has_side_effects=True, vmem_limit_bytes=62 * 1024 * 1024
        ),
        name="weight_grads",
    )(*turned, ya, yf, grad_mod, mod_rows, second, cond, pre)


def sum_kernel(mp_count, dp_count, in_ref, out_ref, over_dp, over_mp, send, recv):
    dp, mp = lax.axis_index("dp"), lax.axis_index("mp")
    peers_greet(dp_count, mp_count)
    first = Round("dp", dp_count, lambda peer: over_dp.at[dp], over_dp, send, recv, 0)
    second = Round("mp", mp_count, lambda peer: over_mp.at[mp], over_mp, send, recv, dp_count)
    over_dp[dp] = in_ref[...]
    first.push()
    first.wait()
    over_mp[mp] = functools.reduce(lambda a, b: a + b, [over_dp[i] for i in range(dp_count)])
    second.push()
    second.wait()
    out_ref[...] = functools.reduce(lambda a, b: a + b, [over_mp[i] for i in range(mp_count)])
    first.finish()
    second.finish()


def sum_pallas(values, dp, mp, collective_id=2):
    return pl.pallas_call(
        functools.partial(sum_kernel, mp, dp),
        out_shape=jax.ShapeDtypeStruct(values.shape, F32),
        in_specs=[pl.BlockSpec(memory_space=pltpu.VMEM)],
        out_specs=pl.BlockSpec(memory_space=pltpu.VMEM),
        scratch_shapes=[
            pltpu.VMEM((dp, *values.shape), F32), pltpu.VMEM((mp, *values.shape), F32),
            pltpu.SemaphoreType.DMA((dp + mp,)), pltpu.SemaphoreType.DMA((dp + mp,)),
        ],
        compiler_params=pltpu.CompilerParams(collective_id=collective_id, has_side_effects=True),
        name="sum_scalars",
    )(values)


SLAB = 64
VMEM_LIMIT = 60 * 1024 * 1024


def whole(shape):
    return pl.BlockSpec(shape, lambda m: (0,) * len(shape), pipeline_mode=pl.Buffered(1))


def by_block(*shape):
    return pl.BlockSpec((1, *shape), lambda m: (m, 0, 0))


def dot(left, right):
    return lax.dot_general(left, right, (((1,), (0,)), ((), ())), preferred_element_type=F32)


def dot_nt(left, right):
    return lax.dot_general(left, right, (((1,), (1,)), ((), ())), preferred_element_type=F32)


def dot_tn(left, right):
    return lax.dot_general(left, right, (((0,), (0,)), ((), ())), preferred_element_type=F32)


def slabs(tokens, body, sums=0):
    totals = []
    for block in range(tokens // PAIR):

        def step(i, carry, block=block):
            rows = pl.ds(pl.multiple_of(block * PAIR + i * SLAB, SLAB), SLAB)
            lead, values = body(block, rows)
            head, rest = carry
            head = tuple(h + jnp.sum(jnp.where(lead, v, 0.0), 0, keepdims=True) for h, v in zip(head, values))
            rest = tuple(r + jnp.sum(jnp.where(lead, 0.0, v), 0, keepdims=True) for r, v in zip(rest, values))
            return head, rest

        zero = tuple(jnp.zeros((1, D), F32) for _ in range(sums))
        totals.extend(lax.fori_loop(0, PAIR // SLAB, step, (zero, zero)))
    return totals


def spread(mod_ref, j, block, lead):
    row = lambda i: mod_ref[2 * block + i : 2 * block + i + 1, j * D : (j + 1) * D]
    return jnp.where(lead, row(0), row(1))


def turn(values, cos_row, sin_row, direction):
    quarter = HD // 4
    width = values.shape[1]
    lane = lax.broadcasted_iota(jnp.int32, values.shape, 1)
    ahead = pltpu.roll(values, width - quarter, 1)
    behind = pltpu.roll(values, quarter, 1)
    partner = jnp.where(lane % (2 * quarter) < quarter, ahead, behind)
    return values * cos_row + partner * (sin_row * direction)


def same_image(even_col, even_row, block):
    rows = slice(block * PAIR, (block + 1) * PAIR)
    return even_col[rows, :1] == even_row[block, :1, :]


def softmax(query, key, same):
    scores = jnp.where(same, dot_nt(query, key) * HD ** (-0.5), -1e30)
    expo = jnp.exp(scores - jnp.max(scores, -1, keepdims=True))
    return expo * (1.0 / jnp.sum(expo, -1, keepdims=True))


def attn_forward_kernel(
    patch_ref, prow_ref, pbias_ref, mod_ref, w_ref, cos_ref, sin_ref, col_ref, row_ref,
    x0_ref, x1_ref, proj_ref, m_ref, at_ref, mt_ref, qkv_ref, att_ref, a_ref,
):
    width = att_ref.shape[2]
    tokens = a_ref.shape[0]
    step, last = pl.program_id(0), pl.num_programs(0) - 1

    @pl.when(step == 0)
    def _():
        x0_ref[...] = dot_tn(patch_ref[...], prow_ref[...]) + pbias_ref[...]

        def body(block, rows):
            lead = col_ref[rows, :1] != 0
            normed, _ = layer_norm(x0_ref[rows, :])
            shift, scale = spread(mod_ref, 0, block, lead), spread(mod_ref, 1, block, lead)
            a_ref[rows, :] = (normed * (1.0 + scale) + shift).astype(LOW)
            return lead, ()

        slabs(tokens, body)
        at_ref[...] = a_ref[...].T

    made = dot(a_ref[...], w_ref[0, :, : 3 * width])
    qkv_ref[0, :, : 2 * width] = turn(made[:, : 2 * width], cos_ref[...], sin_ref[...], 1.0).astype(LOW)
    qkv_ref[0, :, 2 * width :] = made[:, 2 * width :].astype(LOW)
    for block in range(tokens // PAIR):
        same = same_image(col_ref, row_ref, block)
        rows = slice(block * PAIR, (block + 1) * PAIR)
        for head in range(width // HD):
            take = lambda i: qkv_ref[0, rows, i * width + head * HD : i * width + (head + 1) * HD]
            probs = softmax(take(0), take(1), same).astype(LOW)
            att_ref[0, rows, head * HD : (head + 1) * HD] = dot(probs, take(2)).astype(LOW)
    part = dot_nt(att_ref[0], w_ref[0, :, 3 * width :])

    @pl.when(step == 0)
    def _():
        proj_ref[...] = part

    @pl.when(step > 0)
    def _():
        proj_ref[...] += part

    @pl.when(step == last)
    def _():
        def body(block, rows):
            lead = col_ref[rows, :1] != 0
            x_one = x0_ref[rows, :] + spread(mod_ref, 2, block, lead) * proj_ref[rows, :]
            x1_ref[rows, :] = x_one
            normed, _ = layer_norm(x_one)
            shift, scale = spread(mod_ref, 3, block, lead), spread(mod_ref, 4, block, lead)
            m_ref[rows, :] = (normed * (1.0 + scale) + shift).astype(LOW)
            return lead, ()

        slabs(tokens, body)
        mt_ref[...] = m_ref[...].T


def attn_forward(patches, patch_rows, patch_bias, modulation, wa_all, tables):
    blocks, _, width = wa_all.shape
    width //= 4
    tokens = patches.shape[1]
    full, turned = (tokens, D), (D, tokens)
    ins = (patches, patch_rows, patch_bias, modulation)
    return pl.pallas_call(
        attn_forward_kernel,
        grid=(blocks,),
        out_shape=[jax.ShapeDtypeStruct(full, F32)] * 3
        + [jax.ShapeDtypeStruct(full, LOW)]
        + [jax.ShapeDtypeStruct(turned, LOW)] * 2
        + [
            jax.ShapeDtypeStruct((blocks, tokens, 3 * width), LOW),
            jax.ShapeDtypeStruct((blocks, tokens, width), LOW),
        ],
        in_specs=[whole(a.shape) for a in ins] + [by_block(D, 4 * width)] + [whole(a.shape) for a in tables],
        out_specs=[whole(full)] * 4
        + [whole(turned)] * 2
        + [by_block(tokens, 3 * width), by_block(tokens, width)],
        scratch_shapes=[pltpu.VMEM(full, LOW)],
        compiler_params=pltpu.CompilerParams(vmem_limit_bytes=VMEM_LIMIT),
        name="attn_forward",
    )(*ins, wa_all, *tables)


def ffn_kernel(
    m_ref, x1_ref, proj_ref, mod_ref, head_ref, target_ref, weight_ref, col_ref, w_ref,
    yf_ref, gx1_ref, gp_ref, gpt_ref, gmot_ref, ghead_ref, loss_ref, sums_ref,
    gu_ref, out_ref, back_ref, low_ref,
):
    width = gu_ref.shape[2] // 2
    tokens = m_ref.shape[0]
    step, count = pl.program_id(0), pl.num_programs(0) // 2

    @pl.when(step < count)
    def _():
        for block in range(tokens // PAIR):
            rows = slice(block * PAIR, (block + 1) * PAIR)
            made = dot(m_ref[rows, :], w_ref[0, :, : 2 * width])
            gu_ref[step, rows, :] = made
            gate, up_val = made[:, :width], made[:, width:]
            hidden = (gate * lax.logistic(gate) * up_val).astype(LOW)
            part = dot_nt(hidden, w_ref[0, :, 2 * width :])

            @pl.when(step == 0)
            def _(part=part, rows=rows):
                out_ref[rows, :] = part

            @pl.when(step > 0)
            def _(part=part, rows=rows):
                out_ref[rows, :] += part

    @pl.when(step == count - 1)
    def _():
        def final_norm(block, rows):
            lead = col_ref[rows, :1] != 0
            x_two = x1_ref[rows, :] + spread(mod_ref, 5, block, lead) * out_ref[rows, :]
            return lead, spread(mod_ref, 7, block, lead), *layer_norm(x_two)

        def before(block, rows):
            lead, scale, normed, _ = final_norm(block, rows)
            low_ref[rows, :] = (normed * (1.0 + scale) + spread(mod_ref, 6, block, lead)).astype(LOW)
            return lead, ()

        slabs(tokens, before)
        diff = dot_nt(head_ref[...], low_ref[...]) - target_ref[...]
        loss = jnp.sum(weight_ref[:1, :] * jnp.mean(diff * diff, 0, keepdims=True), 1, keepdims=True)
        loss_ref[...] = jnp.broadcast_to(loss, loss_ref.shape)
        grad_pred = (2.0 / OUT * diff * weight_ref[1:2, :]).astype(LOW)
        ghead_ref[...] = dot(grad_pred, low_ref[...])
        back_ref[...] = dot_tn(grad_pred, head_ref[...])

        def after(block, rows):
            lead, scale, normed, inv_std = final_norm(block, rows)
            grad_f = back_ref[rows, :]
            grad_x2 = norm_back(grad_f, normed, inv_std, scale)
            gx1_ref[rows, :] = grad_x2
            low_ref[rows, :] = (spread(mod_ref, 5, block, lead) * grad_x2).astype(LOW)
            return lead, (grad_f, grad_f * normed, grad_x2 * out_ref[rows, :])

        for image, rows in enumerate(slabs(tokens, after, 3)):
            for k in range(3):
                sums_ref[k, image : image + 1, :] = rows[k]
        gmot_ref[...] = low_ref[...].T

    @pl.when(step >= count)
    def _():
        for block in range(tokens // PAIR):
            rows = slice(block * PAIR, (block + 1) * PAIR)
            grad_hid = dot(low_ref[rows, :], w_ref[0, :, 2 * width :])
            made = gu_ref[2 * count - 1 - step, rows, :]
            gate, up_val = made[:, :width], made[:, width:]
            sigma = lax.logistic(gate)
            act = gate * sigma
            slope = sigma * (1.0 + gate * (1.0 - sigma))
            yf_ref[0, rows, :width] = (grad_hid * up_val * slope).astype(LOW)
            yf_ref[0, rows, width : 2 * width] = (grad_hid * act).astype(LOW)
            yf_ref[0, rows, 2 * width :] = (act * up_val).astype(LOW)
            part = dot_nt(yf_ref[0, rows, : 2 * width], w_ref[0, :, : 2 * width])

            @pl.when(step == count)
            def _(part=part, rows=rows):
                back_ref[rows, :] = part

            @pl.when(step > count)
            def _(part=part, rows=rows):
                back_ref[rows, :] += part

    @pl.when(step == 2 * count - 1)
    def _():
        def body(block, rows):
            lead = col_ref[rows, :1] != 0
            grad_m = back_ref[rows, :]
            normed, inv_std = layer_norm(x1_ref[rows, :])
            grad_x1 = gx1_ref[rows, :] + norm_back(grad_m, normed, inv_std, spread(mod_ref, 4, block, lead))
            gx1_ref[rows, :] = grad_x1
            gp_ref[rows, :] = (spread(mod_ref, 2, block, lead) * grad_x1).astype(LOW)
            return lead, (grad_m, grad_m * normed, grad_x1 * proj_ref[rows, :])

        for image, rows in enumerate(slabs(tokens, body, 3)):
            for k in range(3):
                sums_ref[3 + k, image : image + 1, :] = rows[k]
        gpt_ref[...] = gp_ref[...].T


def ffn(m_in, x_one, proj, modulation, head_rows, target, weights, even_col, wf_all):
    blocks, _, width = wf_all.shape
    width //= 3
    tokens = m_in.shape[0]
    full, turned = (tokens, D), (D, tokens)
    ins = (m_in, x_one, proj, modulation, head_rows, target, weights, even_col)
    there_and_back = lambda i: (jnp.where(i < blocks, i, 2 * blocks - 1 - i), 0, 0)
    back = lambda i: (jnp.where(i < blocks, blocks - 1, 2 * blocks - 1 - i), 0, 0)
    outs = [
        (full, F32), (full, LOW), (turned, LOW), (turned, LOW),
        ((OUT, D), F32), ((8, 128), F32), ((6, modulation.shape[0], D), F32),
    ]
    return pl.pallas_call(
        ffn_kernel,
        grid=(2 * blocks,),
        out_shape=[jax.ShapeDtypeStruct((blocks, tokens, 3 * width), LOW)]
        + [jax.ShapeDtypeStruct(*o) for o in outs],
        in_specs=[whole(a.shape) for a in ins] + [pl.BlockSpec((1, D, 3 * width), there_and_back)],
        out_specs=[pl.BlockSpec((1, tokens, 3 * width), back)] + [whole(o[0]) for o in outs],
        scratch_shapes=[
            pltpu.VMEM((blocks, tokens, 2 * width), F32),
            pltpu.VMEM(full, F32), pltpu.VMEM(full, F32), pltpu.VMEM(full, LOW),
        ],
        compiler_params=pltpu.CompilerParams(vmem_limit_bytes=VMEM_LIMIT),
        name="feed_forward",
    )(*ins, wf_all)


def attn_backward_kernel(
    grad_ref, gx1_ref, x0_ref, patch_ref, mod_ref, w_ref, qkv_ref, att_ref, cos_ref, sin_ref, col_ref, row_ref,
    out_ref, rows_ref, sums_ref, tmp_ref, back_att, back_ref, low_ref,
):
    width = att_ref.shape[2]
    tokens = grad_ref.shape[0]
    scale = HD ** (-0.5)
    step, last = pl.program_id(0), pl.num_programs(0) - 1
    back_att[...] = dot(grad_ref[...], w_ref[0, :, 3 * width :]).astype(LOW)
    for block in range(tokens // PAIR):
        same = same_image(col_ref, row_ref, block)
        rows = slice(block * PAIR, (block + 1) * PAIR)
        for head in range(width // HD):
            lanes = lambda i: slice(i * width + head * HD, i * width + (head + 1) * HD)
            query, key, value = (qkv_ref[0, rows, lanes(i)] for i in range(3))
            grad = back_att[rows, lanes(0)]
            probs = softmax(query, key, same)
            grad_p = dot_nt(grad, value)
            centre = jnp.sum(probs * grad_p, -1, keepdims=True)
            grad_s = (probs * (grad_p - centre)).astype(LOW)
            tmp_ref[rows, lanes(0)] = dot(grad_s, key) * scale
            tmp_ref[rows, lanes(1)] = dot_tn(grad_s, query) * scale
            tmp_ref[rows, lanes(2)] = dot_tn(probs.astype(LOW), grad)
    out_ref[0, :, : 2 * width] = turn(tmp_ref[:, : 2 * width], cos_ref[...], sin_ref[...], -1.0).astype(LOW)
    out_ref[0, :, 2 * width : 3 * width] = tmp_ref[:, 2 * width :].astype(LOW)
    out_ref[0, :, 3 * width :] = att_ref[0]
    part = dot_nt(out_ref[0, :, : 3 * width], w_ref[0, :, : 3 * width])

    @pl.when(step == 0)
    def _():
        back_ref[...] = part

    @pl.when(step > 0)
    def _():
        back_ref[...] += part

    @pl.when(step == last)
    def _():
        def body(block, rows):
            lead = col_ref[rows, :1] != 0
            grad_a = back_ref[rows, :]
            normed, inv_std = layer_norm(x0_ref[rows, :])
            back = norm_back(grad_a, normed, inv_std, spread(mod_ref, 1, block, lead))
            grad_x0 = (gx1_ref[rows, :] + back).astype(LOW)
            low_ref[rows, :] = grad_x0
            return lead, (grad_a, grad_a * normed, grad_x0.astype(F32))

        bias = jnp.zeros((1, D), F32)
        for image, rows in enumerate(slabs(tokens, body, 3)):
            for k in range(2):
                sums_ref[k, image : image + 1, :] = rows[k]
            bias = bias + rows[2]
        rows_ref[:PATCH_IN, :] = dot(patch_ref[...], low_ref[...])
        rows_ref[PATCH_IN : PATCH_IN + 1, :] = bias
        rows_ref[PATCH_IN + 1 :, :] = jnp.zeros((7, D), F32)


def attn_backward(grad_proj, gx1, x_zero, patches, modulation, wa_all, qkv, att, tables):
    blocks, tokens, width = att.shape
    full = (tokens, D)
    ins = (grad_proj, gx1, x_zero, patches, modulation)
    outs = [((PATCH_IN + 8, D), F32), ((2, modulation.shape[0], D), F32)]
    return pl.pallas_call(
        attn_backward_kernel,
        grid=(blocks,),
        out_shape=[jax.ShapeDtypeStruct((blocks, tokens, 4 * width), LOW)]
        + [jax.ShapeDtypeStruct(*o) for o in outs],
        in_specs=[whole(a.shape) for a in ins]
        + [by_block(D, 4 * width), by_block(tokens, 3 * width), by_block(tokens, width)]
        + [whole(a.shape) for a in tables],
        out_specs=[by_block(tokens, 4 * width)] + [whole(o[0]) for o in outs],
        scratch_shapes=[
            pltpu.VMEM((tokens, 3 * width), F32), pltpu.VMEM((tokens, width), LOW),
            pltpu.VMEM(full, F32), pltpu.VMEM(full, LOW),
        ],
        compiler_params=pltpu.CompilerParams(vmem_limit_bytes=VMEM_LIMIT),
        name="attn_backward",
    )(*ins, wa_all, qkv, att, *tables)


def gather_library(wa, wf, small):
    dp, mp = lax.axis_size("dp"), lax.axis_size("mp")
    info, embed, first, first_bias, second, part, tail, columns = small
    depth = wa.shape[0]

    def one(w):
        full = lax.all_gather(w, BOTH, axis=0)
        full = full.reshape(dp, mp, *w.shape).transpose(1, 0, 2, 3)
        return full.reshape(mp, dp * w.shape[0], w.shape[1])

    over_dp = lambda v: lax.all_gather(v, "dp", axis=0)
    pre = lax.psum(dot(embed, first) + first_bias, "mp")
    cond = lax.psum(dot(jax.nn.silu(pre).astype(LOW), second) + part, "mp")
    scaled_all = over_dp(jax.nn.silu(cond).astype(LOW))
    scaled = scaled_all.reshape(-1, D)
    mine = lax.dynamic_slice_in_dim(scaled, lax.axis_index("dp") * depth, depth, 1)
    mod = lax.psum_scatter(dot(mine, columns), "dp", scatter_dimension=0, tiled=True)
    over_mp = lambda v: lax.all_gather(v, "mp", axis=0)
    return one(wa), one(wf), over_mp(mod), over_mp(tail), pre, cond, scaled_all, over_dp(info), over_dp(jax.nn.silu(pre).astype(LOW))


def sibling(value):
    mp = lax.axis_size("mp")
    return lax.ppermute(value, "mp", [(i, i + 1 - 2 * (i % 2)) for i in range(mp)])


def vector_grads(grad_mod, mod_rows, second, cond, pre):
    images = grad_mod.shape[0] // 8
    group = lax.all_gather(grad_mod.reshape(8, images, D), "mp", axis=1, tiled=True)
    group = group.transpose(1, 0, 2).reshape(cond.shape[0], 8 * D)
    every = lax.all_gather(group, "dp", axis=0, tiled=True)
    scaled = lax.all_gather(dot_nt(every, mod_rows), "dp", axis=1, tiled=True)
    scaled = lax.dynamic_slice_in_dim(scaled, lax.axis_index("dp") * cond.shape[0], cond.shape[0], 0)
    grad_cond = (scaled * silu_slope(cond)).astype(LOW)
    hidden = lax.psum(dot_nt(grad_cond, second), "mp")
    grad_pre = (hidden * silu_slope(pre)).astype(LOW)
    return lax.all_gather(jnp.concatenate([grad_cond, grad_pre], 0), "dp", axis=0)


def plane_grads(turned, ya, yf):
    dp, mp = lax.axis_size("dp"), lax.axis_size("mp")
    core, place = lax.axis_index("mp") % 2, lax.axis_index("mp") // 2
    x_all = jnp.stack(turned)
    x_two = jnp.concatenate([x_all, sibling(x_all)], 2)
    width_a, width_f = ya.shape[2] // 4, yf.shape[2] // 3

    def halves(values):
        split = values.reshape(mp // 2, 2, *values.shape[1:])
        mine = lax.dynamic_index_in_dim(split, core, 1, False)
        theirs = lax.dynamic_index_in_dim(split, 1 - core, 1, False)
        return jnp.concatenate([mine, sibling(theirs)], 1)

    def product(x, values):
        return jnp.einsum("dt,btn->bdn", x, values, preferred_element_type=F32)

    ya_two, yf_two = halves(ya), halves(yf)
    grad_a = jnp.concatenate(
        [product(x_two[0], ya_two[..., : 3 * width_a]), product(x_two[1], ya_two[..., 3 * width_a :])], 2
    )
    grad_f = jnp.concatenate(
        [product(x_two[2], yf_two[..., : 2 * width_f]), product(x_two[3], yf_two[..., 2 * width_f :])], 2
    )
    grad = jnp.stack([grad_f[..., :STEP], grad_f[..., STEP:], grad_a])
    part = lax.psum_scatter(grad, "dp", scatter_dimension=2, tiled=True)
    total = lax.dynamic_index_in_dim(part, place, 1, False)
    for hop in range(1, mp // 2):
        perm = [(i, (i + 2 * hop) % mp) for i in range(mp)]
        out = lax.dynamic_index_in_dim(part, (place + hop) % (mp // 2), 1, False)
        total = total + lax.ppermute(out, "mp", perm)
    return total


def per_device(
    patches, target, segments, positions, classes, timesteps, t_weight, step_count,
    qkv_w, qkv_m, qkv_v, out_w, out_m, out_v, ffn_in_w, ffn_in_m, ffn_in_v,
    ffn_out_w, ffn_out_m, ffn_out_v, mod_w, mod_m, mod_v, table_w, table_m, table_v,
):
    mp_count, dp_count = lax.axis_size("mp"), lax.axis_size("dp")
    mp_index, dp_index = lax.axis_index("mp"), lax.axis_index("dp")
    tokens = patches.shape[1]
    pairs = tokens // PAIR
    images = 2 * pairs
    own_rows = table_w.shape[0]
    depth = mod_w.shape[0]
    width_a, width_f = qkv_w.shape[2], ffn_in_w.shape[2]

    regular = dp_count == 2 * DEPTH and mp_count == 4
    group_images = classes.shape[0]
    wa = jnp.concatenate([qkv_w[0], qkv_w[1], qkv_w[2], out_w.T], 1).astype(LOW)
    wf = jnp.concatenate([ffn_in_w[0], ffn_in_w[1], ffn_out_w.T], 1).astype(LOW)

    table_b = table_w.astype(LOW)
    mod_b = mod_w.astype(LOW)
    gap = D + 16
    padded = lax.dynamic_update_slice(jnp.zeros((2 * gap + own_rows, D), LOW), table_b, (gap, 0))

    def placed(row, count):
        return lax.dynamic_slice_in_dim(padded, row - mp_index * own_rows + gap, count, 0)

    half = FREQ // 2
    freqs = jnp.exp(-math.log(10000.0) * jnp.arange(half, dtype=F32) / half)

    def embedding(times):
        angles = times[:, None] * freqs[None, :]
        return jnp.concatenate([jnp.cos(angles), jnp.sin(angles)], 1).astype(LOW)

    row_ids = mp_index * own_rows + jnp.arange(own_rows, dtype=jnp.int32)
    own_hot = (classes[:, None] == row_ids[None, :]).astype(LOW)
    part = matmul(own_hot, table_b) + placed(ROW_OUT_BIAS, 1).astype(F32)
    info = jnp.zeros((8, 128), F32)
    for i, values in enumerate((classes, timesteps, t_weight)):
        info = info.at[i, :group_images].set(values.astype(F32))
    mod_cols = mod_w.shape[1] // mp_count
    small = (
        info, embedding(timesteps.astype(F32)), placed(ROW_TIME_IN, FREQ),
        placed(ROW_TIME_BIAS, 1).astype(F32), placed(ROW_TIME_OUT, D), part,
        jnp.pad(placed(ROW_PATCH, TAIL), ((0, 64 - TAIL), (0, 0))),
        lax.dynamic_slice_in_dim(mod_b, mp_index * mod_cols, mod_cols, 1),
    )
    if regular:
        gathered = gather_pallas(wa, wf, small, dp_count, mp_count)
    else:
        gathered = gather_library(wa, wf, small)
    wa_all, wf_all, mod_all, tails, pre, cond, scaled, infos, hidden = gathered
    count_all = dp_count * group_images
    scaled = scaled.reshape(count_all, D)
    classes_all, times_all, weights_all = (infos[:, i, :group_images].reshape(-1) for i in range(3))
    tail = jnp.sum(tails.astype(F32), 0)
    mod_own = lax.dynamic_slice_in_dim(mod_all, mp_index * images, images, 1)
    mod_bias = tail[ROW_MOD_BIAS - ROW_PATCH : TAIL].reshape(-1)
    modulation = mod_own.transpose(1, 0, 2).reshape(images, -1) + mod_bias
    patch_rows = tail[:PATCH_IN].astype(LOW)
    patch_bias = tail[PATCH_IN]
    head_rows = tail[PATCH_IN + 1 : PATCH_IN + 1 + OUT].astype(LOW)
    weight_sum = jnp.sum(weights_all)

    ones = jnp.ones((count_all, 1), LOW)
    zeros = lambda n: jnp.zeros((count_all, n), LOW)
    own_cols = lambda a: lax.dynamic_slice_in_dim(a, mp_index * own_rows, own_rows, 1)
    left_pre = own_cols(
        jnp.concatenate([zeros(NCLS), embedding(times_all), ones, zeros(ROWS - ROW_TIME_OUT)], 1)
    )
    class_hot = (classes_all[:, None] == jnp.arange(NCLS, dtype=F32)[None, :]).astype(LOW)
    hidden = hidden.reshape(count_all, D)
    left_cond = own_cols(
        jnp.concatenate(
            [class_hot, zeros(ROW_TIME_OUT - NCLS), hidden, ones, zeros(ROWS - ROW_PATCH)], 1
        )
    )
    own_scaled = lax.dynamic_slice_in_dim(scaled, dp_index * depth, depth, 1)

    own_seg = lax.dynamic_slice_in_dim(segments, mp_index * tokens, tokens)
    own_pos = lax.dynamic_slice_in_dim(positions, mp_index * tokens, tokens, 1)
    even = (own_seg % 2 == 0).reshape(pairs, PAIR)
    heads = 2 * width_a // HD
    cos_row, sin_row = (jnp.tile(t, (1, heads)) for t in rotary_tables(own_pos))
    even_col = even.astype(jnp.int32).reshape(tokens, 1)
    even_row = jnp.broadcast_to(even.astype(jnp.int32)[:, None], (pairs, 8, PAIR))
    tables = (cos_row, sin_row, even_col, even_row)
    x_zero, x_one, proj, m_in, a_turned, m_turned, qkv, att = attn_forward(
        patches, patch_rows, patch_bias[None, :], modulation, wa_all, tables
    )
    first_len = jnp.sum(even.astype(F32), 1)
    own_tw = lax.dynamic_slice_in_dim(t_weight, mp_index * images, images).reshape(pairs, 2)
    per_tok = own_tw / jnp.stack([first_len, PAIR - first_len], 1)
    tok_weight = jnp.where(even, per_tok[:, :1], per_tok[:, 1:]).reshape(1, tokens)
    weights = jnp.concatenate([tok_weight, tok_weight / weight_sum], 0)
    yf, grad_x1, grad_proj, proj_turned, mo_turned, grad_head, loss, sums_f = ffn(
        m_in, x_one, proj, modulation, head_rows, target, weights, even_col, wf_all
    )
    ya, grad_patch, sums_a = attn_backward(
        grad_proj, grad_x1, x_zero, patches, modulation, wa_all, qkv, att, tables
    )
    loss_part = loss[0, 0]
    x_turned = (a_turned, proj_turned, m_turned, mo_turned)
    grad_mod = jnp.concatenate(
        [sums_a[0], sums_a[1], sums_f[5], sums_f[3], sums_f[4], sums_f[2], sums_f[0], sums_f[1]], 0
    ).astype(LOW)
    cond_own = jnp.pad(cond.reshape(mp_count, images, D), ((0, 0), (0, 8 - images), (0, 0)))
    pre_own = jnp.pad(pre.reshape(mp_count, images, D), ((0, 0), (0, 8 - images), (0, 0)))
    if regular:
        summed, vectors = weight_grads(
            x_turned, ya, yf, grad_mod, mod_b, small[4], cond_own, pre_own.reshape(-1, D), dp_count
        )
    else:
        summed = plane_grads(x_turned, ya, yf)
        vectors = vector_grads(grad_mod, mod_b, small[4], cond, pre)
    own_wf, own_wa = jnp.concatenate([summed[0], summed[1]], 1), summed[2]

    grad_mod_all = lax.all_gather(grad_mod, BOTH, axis=0).reshape(-1, 8, images, D)
    grad_mod_all = grad_mod_all.transpose(0, 2, 1, 3).reshape(count_all, 8 * D)
    grad_mod_w = matmul_tn(own_scaled, grad_mod_all)
    grad_mod_bias = jnp.sum(grad_mod_all.astype(F32), 0).reshape(8, D)
    grad_cvec = vectors[:, :group_images].reshape(count_all, D)
    grad_pre = vectors[:, group_images:].reshape(count_all, D)
    token_rows = jnp.concatenate([grad_patch[: PATCH_IN + 1], grad_head], 0)
    token_rows = jnp.concatenate([lax.psum(token_rows, BOTH), grad_mod_bias], 0)
    blank = -(-own_rows // 8) * 8
    start = jnp.clip(mp_index * own_rows - ROW_PATCH + blank, 0, blank + 64)
    spaced = lax.dynamic_update_slice(jnp.zeros((2 * blank + 64, D), F32), token_rows, (blank, 0))
    tail_own = lax.dynamic_slice_in_dim(spaced, start, own_rows, 0)
    grad_table = matmul_tn(left_cond, grad_cvec) + matmul_tn(left_pre, grad_pre) + tail_own

    grad_qkv = jnp.stack([own_wa[:, j * width_a : (j + 1) * width_a] for j in range(3)])
    grad_out_w = own_wa[:, 3 * width_a :].T
    grad_ffn_in = jnp.stack([own_wf[:, j * width_f : (j + 1) * width_f] for j in range(2)])
    grad_ffn_out = own_wf[:, 2 * width_f :].T
    sharded_sq = jnp.sum(own_wa * own_wa) + jnp.sum(own_wf * own_wf)
    copied_sq = (
        jnp.sum(grad_mod_w * grad_mod_w) / mp_count + jnp.sum(grad_table * grad_table) / dp_count
    )
    scalars = jnp.concatenate(
        [jnp.full((1, 128), sharded_sq + copied_sq), jnp.full((1, 128), loss_part), jnp.zeros((6, 128), F32)], 0
    )
    scalars = sum_pallas(scalars, dp_count, mp_count) if regular else lax.psum(scalars, BOTH)
    square_sum, loss_sum = scalars[0, 0], scalars[1, 0]
    norm = jnp.sqrt(square_sum)
    total_tokens = tokens * mp_count * dp_count
    clip = jnp.minimum(1.0, CLIP_SCALE / math.sqrt(total_tokens) / (norm + 1e-06))
    count = step_count[0].astype(F32)
    results = [(loss_sum / weight_sum).reshape(1), norm.reshape(1)]
    for weight, first, second, grad in (
        (qkv_w, qkv_m, qkv_v, grad_qkv),
        (out_w, out_m, out_v, grad_out_w),
        (ffn_in_w, ffn_in_m, ffn_in_v, grad_ffn_in),
        (ffn_out_w, ffn_out_m, ffn_out_v, grad_ffn_out),
        (mod_w, mod_m, mod_v, grad_mod_w),
        (table_w, table_m, table_v, grad_table),
    ):
        results.extend(adam(weight, first, second, grad * clip, count))
    return tuple(results)


def solution(mesh):
    tok, grp = P(None, BOTH), P("dp")
    cols, rows = P(None, "dp", "mp"), P("mp", "dp")
    weights = (cols,) * 3 + (rows,) * 3 + (cols,) * 3 + (rows,) * 3
    weights += (P("dp", None),) * 3 + (P("mp", None),) * 3
    in_specs = (tok, tok, grp, P(None, "dp"), grp, grp, grp, P()) + weights
    return jax.shard_map(
        per_device, mesh=mesh, in_specs=in_specs, out_specs=(P(), P()) + weights, check_vma=False
    )
```

time: 2920 us -> 641 us (0.22)
  waiting for transfers between devices: 2040 us -> 5.94 us
  Pallas kernels: 0 us -> 508 us
  matrix products: 352 us -> 12.5 us
  local copies, waits for them, and re-layouts: 195 us -> 36.3 us
  blocking collectives: 113 us -> 0 us
  other arithmetic: 148 us -> 45.3 us
    reduce_scatter x8 -> x0, waiting for transfers between devices: 1130 us -> none  [the longest x1 672 us: per_device(): lax.psum_scatter(matmul_tn(cond_scaled, grad_mod_b), 'dp', scatter_dimens...]
    all_gather x9 -> x1, waiting for transfers between devices: 699 us -> 0.01 us  [per_device(): lax.all_gather(grad_mod, BOTH, axis=0).reshape(-1, 8, images, D)]
    pallas_call x0 -> x6, Pallas kernels: none -> 508 us  [the longest x1 167 us: weight_grads(): pl.pallas_call(functools.partial(weight_grad_kernel, depth, (ya.shape[2]...]
    dot_general x54 -> x1, matrix products: 277 us -> 0.35 us  [matmul(): return jnp.dot(left, right, preferred_element_type=F32)]
    psum x2 -> x1, waiting for transfers between devices: 121 us -> 5.91 us  [per_device(): token_rows = jnp.concatenate([lax.psum(token_rows, BOTH), grad_mod_bias], 0)]
    unnamed x21 -> x2, waiting for transfers between devices: 89.7 us -> 0.03 us
    psum x3 -> x0, blocking collectives: 76.6 us -> none  [the longest x1 39.7 us: per_device(): lax.psum((sharded_sq + copied_sq, loss_part), ('dp', 'mp'))]
    dynamic_update_slice x8 -> x0, local copies, waits for them, and re-layouts: 73.5 us -> none  [the longest x4 37 us: one_block(): lax.dynamic_update_slice_in_dim(grad_k, lax.dynamic_slice_in_dim(grad_k,...]
  transfers between devices with their start and end apart: 20 -> 2, of which waited for: 18 -> 1; matrix products, arithmetic and copies ran while one was open for 9% -> 4% of each run, Pallas kernels for 0% -> 26%
where the time goes in v1:
time: 641 us; the launch traced here: 631 us
  Pallas kernels  508 us (79%)
  other arithmetic  45.3 us (7%)
  local copies, waits for them, and re-layouts  36.3 us (6%)
  between operations  23.1 us (4%)
  matrix products  12.5 us (2%)
    pallas_call x1, Pallas kernels, weight_grads(): pl.pallas_call(functools.partial(weight_grad_kernel, depth, (ya.shape[2]...  167 us
    pallas_call x1, Pallas kernels, gather_pallas(): pl.pallas_call(functools.partial(gather_kernel, depth, mp), out_shape=[ja...  152 us
    pallas_call x1, Pallas kernels, ffn(): pl.pallas_call(ffn_kernel, grid=(2 * blocks,), out_shape=[jax.ShapeDtypeS...  65.3 us
    pallas_call x1, Pallas kernels, attn_backward(): pl.pallas_call(attn_backward_kernel, grid=(blocks,), out_shape=[jax.Shape...  56.8 us
    pallas_call x1, Pallas kernels, attn_forward(): pl.pallas_call(attn_forward_kernel, grid=(blocks,), out_shape=[jax.ShapeD...  55.5 us
    sub x6, other arithmetic, adam(): weight - LEARN_RATE * (m_hat / (jnp.sqrt(v_hat) + ADAM_EPS) + WEIGHT_DECA...  24.9 us
  transfers between devices with their start and end apart: 2, of which 1 were waited for; matrix products, arithmetic and copies ran while one was open for 4% of the time, Pallas kernels for 26%

profile of v1, /device:TPU:0, one launch (start us, length us, event | category | flops | bytes accessed | tf_op | source)
XLA Modules:
  0.0 631.0 jit_solution(522993827187817190)
XLA Ops:
  7.3 2.0 convert_element_type.70
  9.3 4.1 pad_dynamic-slice_fusion.2.t2_ref
  13.9 4.4 convert_element_type.72.mod_ref
  18.5 0.9 copy-done.5
  19.5 0.7 slice_bitcast_fusion.9
  21.1 1.1 concatenate.62.wa_ref
  22.3 1.2 pad_maximum_fusion.1
  23.5 152.1 %gather_weights.1 = (bf16[4,1152,1152]{2,1,0:T(8,128)(2,1)}, bf16[4,1152,2304]{2,1,0:T(8,128)(2,1)}, f32[4,16,2304]{2,1,0:T(8,128)S(1)}, bf16[4,64,1152]{2,1,0:T...) custom-call(bf16[144,1152]{1,0:T(8,128)(2,1)S(1)} %concatenate.62.wa, ...), custom_call_target="tpu_custom_call" | custom-call | tf_op jit(solution)/shard_map/gather_weights/pallas_call | solution.py:372
  176.3 0.8 fusion.46
  177.1 0.9 reshape.362.col_ref
  178.7 0.7 slice.245.head_ref
  181.0 0.7 broadcast_divide_fusion
  181.7 0.7 dynamic-slice_convert_fusion
  183.1 1.7 copy.69.sin_ref
  184.9 1.7 copy.68.cos_ref
  187.2 0.7 broadcast_add_fusion.mod_ref
  188.5 55.5 %attn_forward.1 = (f32[640,1152]{1,0:T(8,128)}, f32[640,1152]{1,0:T(8,128)}, f32[640,1152]{1,0:T(8,128)}, bf16[640,1152]{1,0:T(8,128)(2,1)}, bf16[1152,640]{1,0:...) custom-call(bf16[16,640]{1,0:T(8,128)(2,1)} %patch_ref.3, ...), custom_call_target="tpu_custom_call" | custom-call | tf_op jit(solution)/shard_map/attn_forward/pallas_call | solution.py:906
  244.0 65.3 %feed_forward.1 = (bf16[4,640,2304]{2,1,0:T(8,128)(2,1)}, f32[640,1152]{1,0:T(8,128)}, bf16[640,1152]{1,0:T(8,128)(2,1)}, bf16[1152,640]{1,0:T(8,128)(2,1)}, bf1...) custom-call(bf16[640,1152]{1,0:T(8,128)(2,1)} %get-tuple-element.90.m_ref, ...), custom_call_target="tpu_custom_call" | custom-call | tf_op jit(solution)/shard_map/feed_forward/pallas_call | solution.py:1038
  309.3 56.8 %attn_backward.1 = (bf16[4,640,1152]{2,1,0:T(8,128)(2,1)}, f32[24,1152]{1,0:T(8,128)}, f32[2,4,1152]{2,1,0:T(4,128)}) custom-call(bf16[640,1152]{1,0:T(8,128)(2,1)} %get-tuple-element.98.grad_ref, f32[640,1152]{1,0:T(8,128)} %get-tuple-element.99.gx1_ref, f32[640,1152]{1,0:T(8,128)} %get-tuple-element.100.x0_ref, bf16[16,640]{1,0:T(8,128)(2,1)} %patch_ref.3, ...), custom_call_target="tpu_custom_call" | custom-call | tf_op jit(solution)/shard_map/attn_backward/pallas_call | solution.py:1116
  366.1 0.8 fusion.50
  366.9 2.5 concatenate.70
  369.5 1.6 pad_maximum_fusion.2
  371.2 0.7 pad.25.cond_ref
  371.9 0.7 pad_bitcast_fusion.pre_ref
  372.5 2.5 concatenate.68.gmod_ref
  375.1 167.2 %weight_grads.1 = (f32[3,144,1152]{2,1,0:T(8,128)}, bf16[8,32,1152]{2,1,0:T(8,128)(2,1)}) custom-call(bf16[1152,640]{1,0:T(8,128)(2,1)} %get-tuple-element.89.at_ref, bf16[1152,640]{1,0:T(8,128)(2,1)} %get-tuple-element.95.pt_ref, bf16[1152,640]{1,0:T(8,128)(2,1)} %get-tuple-element.96.mt_ref, bf16[1152,640]{1,0:T(8,128)(2,1)} %get-tuple-element.97.ot_ref, ...), custom_call_target="tpu_custom_call" | custom-call | tf_op jit(solution)/shard_map/weight_grads/pallas_call | solution.py:707
  542.2 1.6 slice_bitcast_fusion.2
  543.9 2.4 multiply_reduce_fusion.2
  546.2 0.9 fusion.10
  547.2 1.0 slice_bitcast_fusion.3
  548.8 1.2 slice.223
  550.8 1.0 slice_bitcast_fusion.6
  553.6 2.3 fusion.21
  556.0 1.2 concatenate.72
  557.2 4.3 reshape.351
  562.5 5.9 all-reduce.8.cloned.1.call-done
  568.5 6.0 multiply_reduce_fusion.1
  575.1 3.9 multiply_reduce_fusion
  579.8 0.9 maximum_maximum_fusion
  580.7 0.7 broadcast.152.in_ref
  581.4 10.9 %sum_scalars.1 = f32[8,128]{1,0:T(8,128)} custom-call(f32[8,128]{1,0:T(8,128)} %broadcast.152.in_ref), custom_call_target="tpu_custom_call" | custom-call | tf_op jit(solution)/shard_map/sum_scalars/pallas_call | solution.py:762
  592.3 1.3 fusion.51
  595.7 2.8 multiply_subtract_fusion.4
  598.5 2.3 multiply_subtract_fusion.5
  600.8 6.4 %multiply_subtract_fusion.1 = (f32[617,1152]{1,0:T(8,128)}, f32[617,1152]{1,0:T(8,128)}, f32[617,1152]{1,0:T(8,128)}) fusion(f32[617,1152]{1,0:T(8,128)S(1)} %copy-done, f32[]{:T(128)} %bitcast.45, f32[]{:T(128)} %bitcast.44, f32[617,1152]{1,0:T(8,128)} %get-tuple-element.185, f32[]{:T(128)} %bitcast.43, f32[617,1152]{1,0:T(8,128)} %param.57, ...), kind=kLoop, calls=%fused_computation.23 | loop fusion | flops 11372544 | bytes 19901964 | tf_op jit(solution)/shard_map/sub | solution.py:84
  607.3 9.8 %multiply_subtract_fusion = (f32[144,9216]{1,0:T(8,128)}, f32[144,9216]{1,0:T(8,128)}, f32[144,9216]{1,0:T(8,128)}) fusion(f32[144,9216]{1,0:T(8,128)S(1)} %bitcast.108, f32[]{:T(128)} %bitcast.45, f32[]{:T(128)} %bitcast.44, f32[144,9216]{1,0:T(8,128)S(1)} %bitcast.110, f32[]{:T(128)} %bitcast.43, f32[144,9216]{1,0:T(8,128)} %param.54, f32[144,9216]{1,0:T(8,128)} %param.53), kind=kLoop, calls=%fused_computation.9 | loop fusion | flops 21233664 | bytes 37158924 | tf_op jit(solution)/shard_map/sub | solution.py:84
  617.2 2.0 multiply_subtract_fusion.2
  619.8 1.6 multiply_subtract_fusion.3
  (138 shorter events, 9.9 us)
Async XLA Ops:
  7.2 550.0 %all-gather.2.cloned.1.call-start = ((), (), s32[]{:S(2)}) async-start(), calls=%async_computation | async-start | bytes 2433024 | tf_op jit(solution)/shard_map/all_gather | solution.py:1323
  13.9 4.5 copy-start.3
  13.9 4.6 copy-start.7
  18.4 1.1 copy-start.5
  18.4 1.8 copy-start.10
  18.4 1.8 copy-start.25
  18.4 1.8 copy-start.23
  18.4 2.5 copy-start.24
  309.3 57.6 %copy-start.22 = (f32[6,4,1152]{2,1,0:T(4,128)S(1)}, f32[6,4,1152]{2,1,0:T(4,128)}, u32[]{:S(2)}) copy-start(f32[6,4,1152]{2,1,0:T(4,128)} %get-tuple-element.106) | copy-start | bytes 331780
  309.3 60.2 %copy-start.21 = (f32[32,1152]{1,0:T(8,128)S(1)}, f32[32,1152]{1,0:T(8,128)}, u32[]{:S(2)}) copy-start(f32[32,1152]{1,0:T(8,128)} %get-tuple-element.114) | copy-start | bytes 442372
  369.4 199.0 %all-reduce.8.cloned.1.call-start = ((), (), s32[]{:S(2)}) async-start(), calls=%async_computation.1 | async-start | bytes 516096 | tf_op jit(solution)/shard_map/psum | solution.py:1330
  543.9 4.4 copy-start.1
  543.9 6.9 %copy-start.2 = (f32[144,1152]{1,0:T(8,128)}, f32[144,1152]{1,0:T(8,128)S(1)}, u32[]{:S(2)}) copy-start(f32[144,1152]{1,0:T(8,128)S(1)} %get-tuple-element.143) | copy-start | bytes 1990660
  543.9 4.3 copy-start.19
  575.1 23.4 %copy-start.20 = (f32[288,144]{0,1:T(8,128)S(1)}, f32[288,144]{0,1:T(8,128)}, u32[]{:S(2)}) copy-start(f32[288,144]{0,1:T(8,128)} %param.45) | copy-start | bytes 497668
  579.0 19.5 %copy-start.11 = (f32[288,144]{0,1:T(8,128)S(1)}, f32[288,144]{0,1:T(8,128)}, u32[]{:S(2)}) copy-start(f32[288,144]{0,1:T(8,128)} %param.43) | copy-start | bytes 497668
  579.0 21.7 %copy-start = (f32[617,1152]{1,0:T(8,128)S(1)}, f32[617,1152]{1,0:T(8,128)}, u32[]{:S(2)}) copy-start(f32[617,1152]{1,0:T(8,128)} %param.55) | copy-start | bytes 8529412
  595.6 11.6 %slice-start = ((s8[5308416]{0:T(1024)(128)(4,1)}), s8[4194304]{0:T(1024)(128)(4,1)S(1)}, s32[]{:S(2)}) async-start(s8[5308416]{0:T(1024)(128)(4,1)} %bitcast.107), calls=%async_computation.2 | async-start | bytes 8388608
  598.5 8.7 %slice-start.2 = ((s8[5308416]{0:T(1024)(128)(4,1)}), s8[4194304]{0:T(1024)(128)(4,1)S(1)}, s32[]{:S(2)}) async-start(s8[5308416]{0:T(1024)(128)(4,1)} %bitcast.109), calls=%async_computation.4 | async-start | bytes 8388608
  600.8 6.5 %slice-start.1 = ((s8[5308416]{0:T(1024)(128)(4,1)}), s8[1114112]{0:T(1024)(128)(4,1)S(1)}, s32[]{:S(2)}) async-start(s8[5308416]{0:T(1024)(128)(4,1)} %bitcast.107), calls=%async_computation.3 | async-start | bytes 2228224
  600.8 6.5 %slice-start.3 = ((s8[5308416]{0:T(1024)(128)(4,1)}), s8[1114112]{0:T(1024)(128)(4,1)S(1)}, s32[]{:S(2)}) async-start(s8[5308416]{0:T(1024)(128)(4,1)} %bitcast.109), calls=%async_computation.5 | async-start | bytes 2228224
  607.3 9.9 %copy-start.4 = (f32[2,144,768]{2,1,0:T(8,128)S(1)}, f32[2,144,768]{2,1,0:T(8,128)}, u32[]{:S(2)}) copy-start(f32[2,144,768]{2,1,0:T(8,128)} %param.46) | copy-start | bytes 2654212
  607.3 9.8 %copy-start.8 = (f32[1,144,768]{2,1,0:T(8,128)S(1)}, f32[1,144,768]{2,1,0:T(8,128)}, u32[]{:S(2)}) copy-start(f32[1,144,768]{2,1,0:T(8,128)} %get-tuple-element.146) | copy-start | bytes 1327108
  607.3 9.8 %copy-start.9 = (f32[1,144,768]{2,1,0:T(8,128)S(1)}, f32[1,144,768]{2,1,0:T(8,128)}, u32[]{:S(2)}) copy-start(f32[1,144,768]{2,1,0:T(8,128)} %get-tuple-element.147) | copy-start | bytes 1327108
  607.3 9.8 %copy-start.12 = (f32[2,144,768]{2,1,0:T(8,128)S(1)}, f32[2,144,768]{2,1,0:T(8,128)}, u32[]{:S(2)}) copy-start(f32[2,144,768]{2,1,0:T(8,128)} %param.48) | copy-start | bytes 2654212
  607.3 9.8 %copy-start.13 = (f32[2,144,768]{2,1,0:T(8,128)S(1)}, f32[2,144,768]{2,1,0:T(8,128)}, u32[]{:S(2)}) copy-start(f32[2,144,768]{2,1,0:T(8,128)} %param.47) | copy-start | bytes 2654212
  617.1 2.1 copy-start.6
  617.2 2.0 copy-start.14
  617.2 2.0 copy-start.15
  617.2 2.0 copy-start.16
  617.2 2.0 copy-start.17
  617.2 2.6 copy-start.18
Sparse Core Ops, SparseCore 0:
  369.6 64.4 all-gather.1
  440.1 128.2 all-reduce.7

commit v2 on v1

--- a/solution.py
+++ b/solution.py
@@ -39,8 +39,10 @@
 BOTH = ("dp", "mp")
 MESH = pl.DeviceIdType.MESH
 STEP = 1152
-HOOKS = (0, 1, 2, 4)
+HOOKS = (0, 1, 2, 3)
 LINE_FIRST = (True, True, False)
+BEHIND = (0, 4, 5)
+SENDS = 20
 DEPTH = 4
 
 
@@ -165,9 +167,11 @@
 
 def gather_kernel(
     depth, mp_count, wa_ref, wf_ref, info_ref, emb_ref, t1_ref, b1_ref, t2_ref, part_ref, tail_ref, mcol_ref,
+    patch_ref, cos_ref, sin_ref, col_ref, row_ref,
     wa_all, wf_all, mod_ref, tails_ref, pre_ref, cond_ref, scaled_ref, infos_ref, hid_ref,
-    info_buf, pre_sum, cond_sum, tail_buf, scaled_buf, hid_buf, mod_part, mod_sum, mod_buf,
-    recv, send, local, little_recv, little_send,
+    x0_ref, x1_ref, proj_ref, m_ref, at_ref, mt_ref, qkv_ref, att_ref,
+    info_buf, pre_sum, cond_sum, tail_buf, scaled_buf, hid_buf, mod_part, mod_sum, mod_buf, a_ref, wa_buf,
+    recv, send, local, little_recv, little_send, wa_sem,
 ):
     dp_count = 2 * depth
     z, x, y, c, first, second = coordinates()
@@ -235,7 +239,6 @@
 
     hooks = (hidden, condition, modulate, collect)
 
-    sent = []
     corner = (first[0] + second[0] - x, first[1] + second[1] - y)
     spots = {"here": (x, y), "first": first, "second": second, "corner": corner}
     ids = {"here": 0, "first": 1, "second": 2, "corner": 3}
@@ -250,30 +253,6 @@
 
     def mine(g):
         return groups[g][0].at[:, pl.ds(groups[g][2], STEP)]
-
-    def copy(g, zz, kind, route, cond=None, own=False):
-        plane, sem_kind = 0, kind
-        if route == "up":
-            target = ((z + 1) * 2 + x, mp)
-        elif route == "down":
-            target = ((z - 1) * 2 + x, mp)
-        elif route == "first":
-            target, sem_kind = (z * 2 + first[0], first[1] * 2 + c), "first"
-        elif route == "second":
-            target = (z * 2 + second[0], second[1] * 2 + c)
-            sem_kind = "second" if kind == "here" else "corner"
-        else:
-            target, plane = (dp, y * 2 + 1 - c), 1
-        made = pltpu.make_async_remote_copy(
-            src_ref=mine(g) if own else slot(g, zz, spots[kind], c), dst_ref=slot(g, zz, spots[kind], c),
-            send_sem=send.at[len(sent)], recv_sem=recv.at[g, plane, ids[sem_kind], zz],
-            device_id=target, device_id_type=MESH,
-        )
-        sent.append((made, cond))
-        if cond is None:
-            made.start()
-        else:
-            pl.when(cond)(made.start)
 
     def arrive(g, zz, kind, cond=None, plane=0):
         dst = slot(g, zz, spots[kind], c if plane == 0 else 1 - c)
@@ -288,113 +267,188 @@
         below, above = jnp.maximum(z - k, 0), jnp.minimum(z + k, depth - 1)
         return ((below, z >= k, "up", z < depth - 1), (above, z < depth - k, "down", z > 0))[: 1 if k == 0 else 2]
 
-    def stage(g, k):
+    def stage(g, k, live=True):
         line_first = groups[g][3]
+        numbers = iter(range((g * (depth + 2) + k) * SENDS, (g * (depth + 2) + k + 1) * SENDS))
+
+        def copy(zz, kind, route, cond=None, own=False):
+            plane, sem_kind = 0, kind
+            if route == "up":
+                target = ((z + 1) * 2 + x, mp)
+            elif route == "down":
+                target = ((z - 1) * 2 + x, mp)
+            elif route == "first":
+                target, sem_kind = (z * 2 + first[0], first[1] * 2 + c), "first"
+            elif route == "second":
+                target = (z * 2 + second[0], second[1] * 2 + c)
+                sem_kind = "second" if kind == "here" else "corner"
+            else:
+                target, plane = (dp, y * 2 + 1 - c), 1
+            made = pltpu.make_async_remote_copy(
+                src_ref=mine(g) if own else slot(g, zz, spots[kind], c), dst_ref=slot(g, zz, spots[kind], c),
+                send_sem=send.at[next(numbers)], recv_sem=recv.at[g, plane, ids[sem_kind], zz],
+                device_id=target, device_id_type=MESH,
+            )
+            act = made.start if live else made.wait_send
+            if cond is None:
+                act()
+            else:
+                pl.when(cond)(act)
+
+        def take(zz, kind, cond=None):
+            if live:
+                arrive(g, zz, kind, cond)
+
         if k == 0:
-            pltpu.make_async_copy(mine(g), slot(g, z, spots["here"], c), local.at[g]).start()
-            copy(g, z, "here", "first", None, True)
-            copy(g, z, "here", "up", z < depth - 1, True)
-            copy(g, z, "here", "down", z > 0, True)
-            copy(g, z, "here", "second", None, True)
-            copy(g, z, "here", "core", None, True)
+            if live:
+                pltpu.make_async_copy(mine(g), slot(g, z, spots["here"], c), local.at[g]).start()
+            copy(z, "here", "first", None, True)
+            copy(z, "here", "up", z < depth - 1, True)
+            copy(z, "here", "down", z > 0, True)
+            copy(z, "here", "second", None, True)
+            copy(z, "here", "core", None, True)
         if k == 1 and not line_first:
-            arrive(g, z, "first")
-            copy(g, z, "first", "up", z < depth - 1)
-            copy(g, z, "first", "down", z > 0)
-            copy(g, z, "first", "second")
-            copy(g, z, "first", "core")
+            take(z, "first")
+            copy(z, "first", "up", z < depth - 1)
+            copy(z, "first", "down", z > 0)
+            copy(z, "first", "second")
+            copy(z, "first", "core")
         if 0 < k < depth:
-            for kind in ("here",):
-                for zz, cond, route, more in sides(k):
-                    arrive(g, zz, kind, cond)
-                    copy(g, zz, kind, route, cond & more)
-                    if line_first:
-                        copy(g, zz, kind, "first", cond)
-                    copy(g, zz, kind, "second", cond)
-                    copy(g, zz, kind, "core", cond)
-        if line_first and 0 <= k - 1 < depth:
-            for zz, cond, _, _ in sides(k - 1):
-                arrive(g, zz, "first", cond)
-                copy(g, zz, "first", "second", cond)
-                copy(g, zz, "first", "core", cond)
-        if not line_first and 0 < k - 1 < depth:
+            for zz, cond, route, more in sides(k):
+                take(zz, "here", cond)
+                copy(zz, "here", route, cond & more)
+                if line_first:
+                    copy(zz, "here", "first", cond)
+                copy(zz, "here", "second", cond)
+                copy(zz, "here", "core", cond)
+        if 0 <= k - 1 < depth and (line_first or k > 1):
             for zz, cond, route, more in sides(k - 1):
-                arrive(g, zz, "first", cond)
-                copy(g, zz, "first", route, cond & more)
-                copy(g, zz, "first", "second", cond)
-                copy(g, zz, "first", "core", cond)
+                take(zz, "first", cond)
+                if not line_first:
+                    copy(zz, "first", route, cond & more)
+                copy(zz, "first", "second", cond)
+                copy(zz, "first", "core", cond)
         if 0 <= k - 2 < depth:
             for zz, cond, _, _ in sides(k - 2):
                 for kind in ("second", "corner"):
-                    arrive(g, zz, kind, cond)
-                    copy(g, zz, kind, "core", cond)
-
-    begin()
-    for moment in range(depth + 2 + count - 1):
-        for g in range(count):
-            if 0 <= moment - g < depth + 2:
-                stage(g, moment - g)
-        for number, hook in enumerate(hooks):
-            if HOOKS[number] == moment:
-                hook()
-    mod_a.wait()
-    hid_a.wait()
-    info.wait()
-    tail_r.wait()
-    mod_ref[...] = mod_buf[...]
-    tails_ref[...] = tail_buf[...]
-    scaled_ref[...] = scaled_buf[...]
-    infos_ref[...] = info_buf[...]
-    hid_ref[...] = hid_buf[...]
-    for g in range(count):
+                    take(zz, kind, cond)
+                    copy(zz, kind, "core", cond)
+
+    def settle(g):
         for zz in range(depth):
             for kind in ("here", "first", "second", "corner"):
                 arrive(g, zz, kind, None, 1)
         pltpu.make_async_copy(mine(g), slot(g, z, spots["here"], c), local.at[g]).wait()
-    for made, cond in sent:
-        if cond is None:
-            made.wait_send()
-        else:
-            pl.when(cond)(made.wait_send)
+
+    begin()
+    steps = [
+        [(g, moment - BEHIND[g]) for g in range(count) if 0 <= moment - BEHIND[g] < depth + 2]
+        for moment in range(depth + 2 + max(BEHIND))
+    ]
+    for moment in range(depth + 2):
+        for g, k in steps[moment]:
+            stage(g, k)
+        for number, hook in enumerate(hooks):
+            if HOOKS[number] == moment:
+                hook()
+    settle(0)
+    load = lambda m: pltpu.make_async_copy(wa_all.at[m], wa_buf.at[m % 2], wa_sem.at[m % 2])
+    load(0).start()
+    mod_a.wait()
+    tail_r.wait()
+    tails_ref[...] = functools.reduce(lambda a, b: a + b, [tail_buf[i].astype(F32) for i in range(mp_count)])
+    own_images = images // mp_count
+    width = mcol_ref.shape[1]
+    for i in range(mp_count):
+        rows_of = lambda m: mod_buf[i, m * own_images : (m + 1) * own_images, :]
+        picked = functools.reduce(lambda a, m: jnp.where(mp == m, rows_of(m), a), range(1, mp_count), rows_of(0))
+        mod_ref[:, i * width : (i + 1) * width] = picked
+    for j in range(8):
+        bias = tails_ref[ROW_MOD_BIAS - ROW_PATCH + j : ROW_MOD_BIAS - ROW_PATCH + j + 1, :]
+        mod_ref[:, j * D : (j + 1) * D] += bias
+    attn_begin(
+        patch_ref, tails_ref[:PATCH_IN, :].astype(LOW), tails_ref[PATCH_IN : PATCH_IN + 1, :],
+        mod_ref, col_ref, x0_ref, a_ref, at_ref,
+    )
+    proj_ref[...] = jnp.zeros(proj_ref.shape, F32)
+
+    later = [pair for moment in steps[depth + 2 :] for pair in moment]
+
+    def heads(m, _):
+        pl.when(m + 1 < mp_count)(lambda: load(m + 1).start())
+        load(m).wait()
+        proj_ref[...] += attn_block(
+            wa_buf.at[m % 2], cos_ref, sin_ref, col_ref, row_ref, a_ref, qkv_ref.at[m], att_ref.at[m]
+        )
+        for i in range(mp_count):
+            part = later[i * len(later) // mp_count : (i + 1) * len(later) // mp_count]
+
+            @pl.when(m == i)
+            def _(part=part):
+                for g, k in part:
+                    stage(g, k)
+
+        return 0
+
+    lax.fori_loop(0, mp_count, heads, 0)
+    hid_a.wait()
+    info.wait()
+    scaled_ref[...] = scaled_buf[...]
+    infos_ref[...] = info_buf[...]
+    hid_ref[...] = hid_buf[...]
+    attn_end(mod_ref, col_ref, x0_ref, proj_ref, x1_ref, m_ref, mt_ref)
+    for g in range(1, count):
+        settle(g)
+    for g in range(count):
+        for k in range(depth + 2):
+            stage(g, k, False)
     for one in rounds:
         one.finish()
 
 
-def gather_pallas(wa, wf, small, dp, mp, collective_id=0):
+def gather_pallas(wa, wf, small, patches, tables, dp, mp, collective_id=0):
     depth = dp // 2
     groups = 1 + wf.shape[1] // STEP
     images, width = small[1].shape[0], small[7].shape[1]
     tail = small[6].shape[0]
+    tokens, heads = patches.shape[1], wa.shape[1] // 4
+    full, turned = (tokens, D), (D, tokens)
     shapes = [
-        ((mp, images, width), F32), ((mp, tail, D), LOW), ((images, D), F32), ((images, D), F32),
+        ((images // mp, mp * width), F32), ((tail, D), F32), ((images, D), F32), ((images, D), F32),
         ((dp, images, D), LOW), ((dp, 8, 128), F32), ((dp, images, D), LOW),
+        (full, F32), (full, F32), (full, F32), (full, LOW), (turned, LOW), (turned, LOW),
+        ((mp, tokens, 3 * heads), LOW), ((mp, tokens, heads), LOW),
     ]
+    hbm, vmem = pl.BlockSpec(memory_space=pl.ANY), pl.BlockSpec(memory_space=pltpu.VMEM)
     return pl.pallas_call(
         functools.partial(gather_kernel, depth, mp),
         out_shape=[jax.ShapeDtypeStruct((mp, dp * s.shape[0], s.shape[1]), s.dtype) for s in (wa, wf)]
         + [jax.ShapeDtypeStruct(*s) for s in shapes],
-        in_specs=[pl.BlockSpec(memory_space=pl.ANY)] * 2 + [pl.BlockSpec(memory_space=pltpu.VMEM)] * 8,
-        out_specs=[pl.BlockSpec(memory_space=pl.ANY)] * 2 + [pl.BlockSpec(memory_space=pltpu.VMEM)] * 7,
+        in_specs=[hbm] * 2 + [vmem] * 13,
+        out_specs=[hbm] * 2 + [vmem] * len(shapes),
         scratch_shapes=[
             pltpu.VMEM((dp, 8, 128), F32), pltpu.VMEM((mp, images, D), F32), pltpu.VMEM((mp, images, D), F32),
             pltpu.VMEM((mp, tail, D), LOW), pltpu.VMEM((dp, images, D), LOW), pltpu.VMEM((dp, images, D), LOW),
             pltpu.VMEM((dp, images, width), F32), pltpu.VMEM((dp, images, width), F32),
             pltpu.VMEM((mp, images, width), F32),
+            pltpu.VMEM(full, LOW), pltpu.VMEM((2, D, wa.shape[1]), LOW),
             pltpu.SemaphoreType.DMA((groups, 2, 4, depth)),
-            pltpu.SemaphoreType.DMA((groups * 64,)),
+            pltpu.SemaphoreType.DMA((groups * (depth + 2) * SENDS,)),
             pltpu.SemaphoreType.DMA((groups,)),
             pltpu.SemaphoreType.DMA((8 * dp,)),
             pltpu.SemaphoreType.DMA((8 * dp,)),
+            pltpu.SemaphoreType.DMA((2,)),
         ],
         compiler_params=pltpu.CompilerParams(
-            collective_id=collective_id, has_side_effects=True, vmem_limit_bytes=48 * 1024 * 1024
+            collective_id=collective_id, has_side_effects=True, vmem_limit_bytes=60 * 1024 * 1024
         ),
         name="gather_weights",
-    )(wa, wf, *small)
+    )(wa, wf, *small, patches, *tables)
 
 
 TOP = 32766.0
 RING = 14
+BETWEEN = (0, 12, 20, 28, 36)
 ORDER = (
     (0, 0, 0), (0, 0, 2), (0, 0, 1), (0, 2, 0), (0, 0, 3), (1, 0, 0), (0, 2, 2), (2, 0, 3), (1, 0, 1), (0, 2, 1),
     (0, 1, 0), (1, 1, 0), (1, 1, 1), (1, 2, 0), (2, 0, 0), (1, 2, 1), (1, 0, 2), (0, 1, 2), (2, 1, 1), (0, 1, 1),
@@ -621,7 +675,7 @@
         vec_buf[dp, count:, :] = dot(pick, grad_pre).astype(LOW)
         vec_a.push()
 
-    hooks = ((0, begin), (8, scaled_grad), (15, vector_grad), (20, hidden_grad), (27, first_grad))
+    hooks = tuple(zip(BETWEEN, (begin, scaled_grad, vector_grad, hidden_grad, first_grad), strict=True))
 
     to_second = (z * 2 + second[0], second[1] * 2 + c)
     to_first = (z * 2 + first[0], first[1] * 2 + c)
@@ -840,61 +894,67 @@
     return expo * (1.0 / jnp.sum(expo, -1, keepdims=True))
 
 
+def attn_begin(patch_ref, patch_rows, patch_bias, mod_ref, col_ref, x0_ref, a_ref, at_ref):
+    x0_ref[...] = dot_tn(patch_ref[...], patch_rows) + patch_bias
+
+    def body(block, rows):
+        lead = col_ref[rows, :1] != 0
+        normed, _ = layer_norm(x0_ref[rows, :])
+        shift, scale = spread(mod_ref, 0, block, lead), spread(mod_ref, 1, block, lead)
+        a_ref[rows, :] = (normed * (1.0 + scale) + shift).astype(LOW)
+        return lead, ()
+
+    slabs(a_ref.shape[0], body)
+    at_ref[...] = a_ref[...].T
+
+
+def attn_block(w_ref, cos_ref, sin_ref, col_ref, row_ref, a_ref, qkv_ref, att_ref):
+    tokens, width = att_ref.shape
+    made = dot(a_ref[...], w_ref[:, : 3 * width])
+    qkv_ref[:, : 2 * width] = turn(made[:, : 2 * width], cos_ref[...], sin_ref[...], 1.0).astype(LOW)
+    qkv_ref[:, 2 * width :] = made[:, 2 * width :].astype(LOW)
+    for block in range(tokens // PAIR):
+        same = same_image(col_ref, row_ref, block)
+        rows = slice(block * PAIR, (block + 1) * PAIR)
+        for head in range(width // HD):
+            take = lambda i: qkv_ref[rows, i * width + head * HD : i * width + (head + 1) * HD]
+            probs = softmax(take(0), take(1), same).astype(LOW)
+            att_ref[rows, head * HD : (head + 1) * HD] = dot(probs, take(2)).astype(LOW)
+    return dot_nt(att_ref[...], w_ref[:, 3 * width :])
+
+
+def attn_end(mod_ref, col_ref, x0_ref, proj_ref, x1_ref, m_ref, mt_ref):
+    def body(block, rows):
+        lead = col_ref[rows, :1] != 0
+        x_one = x0_ref[rows, :] + spread(mod_ref, 2, block, lead) * proj_ref[rows, :]
+        x1_ref[rows, :] = x_one
+        normed, _ = layer_norm(x_one)
+        shift, scale = spread(mod_ref, 3, block, lead), spread(mod_ref, 4, block, lead)
+        m_ref[rows, :] = (normed * (1.0 + scale) + shift).astype(LOW)
+        return lead, ()
+
+    slabs(m_ref.shape[0], body)
+    mt_ref[...] = m_ref[...].T
+
+
 def attn_forward_kernel(
     patch_ref, prow_ref, pbias_ref, mod_ref, w_ref, cos_ref, sin_ref, col_ref, row_ref,
     x0_ref, x1_ref, proj_ref, m_ref, at_ref, mt_ref, qkv_ref, att_ref, a_ref,
 ):
-    width = att_ref.shape[2]
-    tokens = a_ref.shape[0]
     step, last = pl.program_id(0), pl.num_programs(0) - 1
 
     @pl.when(step == 0)
     def _():
-        x0_ref[...] = dot_tn(patch_ref[...], prow_ref[...]) + pbias_ref[...]
-
-        def body(block, rows):
-            lead = col_ref[rows, :1] != 0
-            normed, _ = layer_norm(x0_ref[rows, :])
-            shift, scale = spread(mod_ref, 0, block, lead), spread(mod_ref, 1, block, lead)
-            a_ref[rows, :] = (normed * (1.0 + scale) + shift).astype(LOW)
-            return lead, ()
-
-        slabs(tokens, body)
-        at_ref[...] = a_ref[...].T
-
-    made = dot(a_ref[...], w_ref[0, :, : 3 * width])
-    qkv_ref[0, :, : 2 * width] = turn(made[:, : 2 * width], cos_ref[...], sin_ref[...], 1.0).astype(LOW)
-    qkv_ref[0, :, 2 * width :] = made[:, 2 * width :].astype(LOW)
-    for block in range(tokens // PAIR):
-        same = same_image(col_ref, row_ref, block)
-        rows = slice(block * PAIR, (block + 1) * PAIR)
-        for head in range(width // HD):
-            take = lambda i: qkv_ref[0, rows, i * width + head * HD : i * width + (head + 1) * HD]
-            probs = softmax(take(0), take(1), same).astype(LOW)
-            att_ref[0, rows, head * HD : (head + 1) * HD] = dot(probs, take(2)).astype(LOW)
-    part = dot_nt(att_ref[0], w_ref[0, :, 3 * width :])
-
-    @pl.when(step == 0)
-    def _():
-        proj_ref[...] = part
-
-    @pl.when(step > 0)
-    def _():
-        proj_ref[...] += part
+        attn_begin(patch_ref, prow_ref[...], pbias_ref[...], mod_ref, col_ref, x0_ref, a_ref, at_ref)
+        proj_ref[...] = jnp.zeros(proj_ref.shape, F32)
+
+    proj_ref[...] += attn_block(
+        w_ref.at[0], cos_ref, sin_ref, col_ref, row_ref, a_ref, qkv_ref.at[0], att_ref.at[0]
+    )
 
     @pl.when(step == last)
     def _():
-        def body(block, rows):
-            lead = col_ref[rows, :1] != 0
-            x_one = x0_ref[rows, :] + spread(mod_ref, 2, block, lead) * proj_ref[rows, :]
-            x1_ref[rows, :] = x_one
-            normed, _ = layer_norm(x_one)
-            shift, scale = spread(mod_ref, 3, block, lead), spread(mod_ref, 4, block, lead)
-            m_ref[rows, :] = (normed * (1.0 + scale) + shift).astype(LOW)
-            return lead, ()
-
-        slabs(tokens, body)
-        mt_ref[...] = m_ref[...].T
+        attn_end(mod_ref, col_ref, x0_ref, proj_ref, x1_ref, m_ref, mt_ref)
 
 
 def attn_forward(patches, patch_rows, patch_bias, modulation, wa_all, tables):
@@ -923,6 +983,14 @@
     )(*ins, wa_all, *tables)
 
 
+PARTS = 1
+
+
+def units(part, width):
+    size = width // PARTS
+    return slice(part * size, (part + 1) * size), slice(width + part * size, width + (part + 1) * size)
+
+
 def ffn_kernel(
     m_ref, x1_ref, proj_ref, mod_ref, head_ref, target_ref, weight_ref, col_ref, w_ref,
     yf_ref, gx1_ref, gp_ref, gpt_ref, gmot_ref, ghead_ref, loss_ref, sums_ref,
@@ -932,23 +1000,24 @@
     tokens = m_ref.shape[0]
     step, count = pl.program_id(0), pl.num_programs(0) // 2
 
+    @pl.when(step == 0)
+    def _():
+        out_ref[...] = jnp.zeros(out_ref.shape, F32)
+
+    @pl.when(step == count)
+    def _():
+        back_ref[...] = jnp.zeros(back_ref.shape, F32)
+
     @pl.when(step < count)
     def _():
-        for block in range(tokens // PAIR):
-            rows = slice(block * PAIR, (block + 1) * PAIR)
-            made = dot(m_ref[rows, :], w_ref[0, :, : 2 * width])
-            gu_ref[step, rows, :] = made
-            gate, up_val = made[:, :width], made[:, width:]
+        for part in range(PARTS):
+            own, other = units(part, width)
+            gate, up_val = dot(m_ref[...], w_ref[0, :, own]), dot(m_ref[...], w_ref[0, :, other])
+            gu_ref[step, :, own] = gate
+            gu_ref[step, :, other] = up_val
             hidden = (gate * lax.logistic(gate) * up_val).astype(LOW)
-            part = dot_nt(hidden, w_ref[0, :, 2 * width :])
-
-            @pl.when(step == 0)
-            def _(part=part, rows=rows):
-                out_ref[rows, :] = part
-
-            @pl.when(step > 0)
-            def _(part=part, rows=rows):
-                out_ref[rows, :] += part
+            last = slice(other.start + width, other.stop + width)
+            out_ref[...] += dot_nt(hidden, w_ref[0, :, last])
 
     @pl.when(step == count - 1)
     def _():
@@ -985,26 +1054,19 @@
 
     @pl.when(step >= count)
     def _():
-        for block in range(tokens // PAIR):
-            rows = slice(block * PAIR, (block + 1) * PAIR)
-            grad_hid = dot(low_ref[rows, :], w_ref[0, :, 2 * width :])
-            made = gu_ref[2 * count - 1 - step, rows, :]
-            gate, up_val = made[:, :width], made[:, width:]
+        for part in range(PARTS):
+            own, other = units(part, width)
+            last = slice(other.start + width, other.stop + width)
+            grad_hid = dot(low_ref[...], w_ref[0, :, last])
+            back = 2 * count - 1 - step
+            gate, up_val = gu_ref[back, :, own], gu_ref[back, :, other]
             sigma = lax.logistic(gate)
             act = gate * sigma
             slope = sigma * (1.0 + gate * (1.0 - sigma))
-            yf_ref[0, rows, :width] = (grad_hid * up_val * slope).astype(LOW)
-            yf_ref[0, rows, width : 2 * width] = (grad_hid * act).astype(LOW)
-            yf_ref[0, rows, 2 * width :] = (act * up_val).astype(LOW)
-            part = dot_nt(yf_ref[0, rows, : 2 * width], w_ref[0, :, : 2 * width])
-
-            @pl.when(step == count)
-            def _(part=part, rows=rows):
-                back_ref[rows, :] = part
-
-            @pl.when(step > count)
-            def _(part=part, rows=rows):
-                back_ref[rows, :] += part
+            yf_ref[0, :, own] = (grad_hid * up_val * slope).astype(LOW)
+            yf_ref[0, :, other] = (grad_hid * act).astype(LOW)
+            yf_ref[0, :, last] = (act * up_val).astype(LOW)
+        back_ref[...] += dot_nt(yf_ref[0, :, : 2 * width], w_ref[0, :, : 2 * width])
 
     @pl.when(step == 2 * count - 1)
     def _():
@@ -1248,22 +1310,33 @@
         info, embedding(timesteps.astype(F32)), placed(ROW_TIME_IN, FREQ),
         placed(ROW_TIME_BIAS, 1).astype(F32), placed(ROW_TIME_OUT, D), part,
         jnp.pad(placed(ROW_PATCH, TAIL), ((0, 64 - TAIL), (0, 0))),
-        lax.dynamic_slice_in_dim(mod_b, mp_index * mod_cols, mod_cols, 1),
+        lax.dynamic_slice_in_dim(mod_w, mp_index * mod_cols, mod_cols, 1).astype(LOW),
     )
+    own_seg = lax.dynamic_slice_in_dim(segments, mp_index * tokens, tokens)
+    own_pos = lax.dynamic_slice_in_dim(positions, mp_index * tokens, tokens, 1)
+    even = (own_seg % 2 == 0).reshape(pairs, PAIR)
+    heads = 2 * width_a // HD
+    cos_row, sin_row = (jnp.tile(t, (1, heads)) for t in rotary_tables(own_pos))
+    even_col = even.astype(jnp.int32).reshape(tokens, 1)
+    even_row = jnp.broadcast_to(even.astype(jnp.int32)[:, None], (pairs, 8, PAIR))
+    tables = (cos_row, sin_row, even_col, even_row)
+
     if regular:
-        gathered = gather_pallas(wa, wf, small, dp_count, mp_count)
+        gathered = gather_pallas(wa, wf, small, patches, tables, dp_count, mp_count)
+        wa_all, wf_all, modulation, tail, pre, cond, scaled, infos, hidden = gathered[:9]
+        x_zero, x_one, proj, m_in, a_turned, m_turned, qkv, att = gathered[9:]
     else:
-        gathered = gather_library(wa, wf, small)
-    wa_all, wf_all, mod_all, tails, pre, cond, scaled, infos, hidden = gathered
+        wa_all, wf_all, mod_all, tails, pre, cond, scaled, infos, hidden = gather_library(wa, wf, small)
+        tail = jnp.sum(tails.astype(F32), 0)
+        mod_own = lax.dynamic_slice_in_dim(mod_all, mp_index * images, images, 1)
+        mod_bias = tail[ROW_MOD_BIAS - ROW_PATCH : TAIL].reshape(-1)
+        modulation = mod_own.transpose(1, 0, 2).reshape(images, -1) + mod_bias
+        x_zero, x_one, proj, m_in, a_turned, m_turned, qkv, att = attn_forward(
+            patches, tail[:PATCH_IN].astype(LOW), tail[PATCH_IN][None, :], modulation, wa_all, tables
+        )
     count_all = dp_count * group_images
     scaled = scaled.reshape(count_all, D)
     classes_all, times_all, weights_all = (infos[:, i, :group_images].reshape(-1) for i in range(3))
-    tail = jnp.sum(tails.astype(F32), 0)
-    mod_own = lax.dynamic_slice_in_dim(mod_all, mp_index * images, images, 1)
-    mod_bias = tail[ROW_MOD_BIAS - ROW_PATCH : TAIL].reshape(-1)
-    modulation = mod_own.transpose(1, 0, 2).reshape(images, -1) + mod_bias
-    patch_rows = tail[:PATCH_IN].astype(LOW)
-    patch_bias = tail[PATCH_IN]
     head_rows = tail[PATCH_IN + 1 : PATCH_IN + 1 + OUT].astype(LOW)
     weight_sum = jnp.sum(weights_all)
 
@@ -1282,17 +1355,6 @@
     )
     own_scaled = lax.dynamic_slice_in_dim(scaled, dp_index * depth, depth, 1)
 
-    own_seg = lax.dynamic_slice_in_dim(segments, mp_index * tokens, tokens)
-    own_pos = lax.dynamic_slice_in_dim(positions, mp_index * tokens, tokens, 1)
-    even = (own_seg % 2 == 0).reshape(pairs, PAIR)
-    heads = 2 * width_a // HD
-    cos_row, sin_row = (jnp.tile(t, (1, heads)) for t in rotary_tables(own_pos))
-    even_col = even.astype(jnp.int32).reshape(tokens, 1)
-    even_row = jnp.broadcast_to(even.astype(jnp.int32)[:, None], (pairs, 8, PAIR))
-    tables = (cos_row, sin_row, even_col, even_row)
-    x_zero, x_one, proj, m_in, a_turned, m_turned, qkv, att = attn_forward(
-        patches, patch_rows, patch_bias[None, :], modulation, wa_all, tables
-    )
     first_len = jnp.sum(even.astype(F32), 1)
     own_tw = lax.dynamic_slice_in_dim(t_weight, mp_index * images, images).reshape(pairs, 2)
     per_tok = own_tw / jnp.stack([first_len, PAIR - first_len], 1)

time: 641 us -> 605 us (0.944)
  Pallas kernels: 508 us -> 465 us
  other arithmetic: 45.3 us -> 56.1 us
    pallas_call x1 -> x0, Pallas kernels: 55.5 us -> none  [attn_forward(): pl.pallas_call(attn_forward_kernel, grid=(blocks,), out_shape=[jax.ShapeD...]
    pallas_call x1, Pallas kernels: 152 us -> 174 us  [gather_pallas(): pl.pallas_call(functools.partial(gather_kernel, depth, mp), out_shape=[ja...]
  transfers between devices with their start and end apart: 2 -> 2, of which waited for: 1 -> 1; matrix products, arithmetic and copies ran while one was open for 4% -> 6% of each run, Pallas kernels for 26% -> 27%
where the time goes in v2:
time: 605 us; the launch traced here: 596 us
  Pallas kernels  465 us (77%)
  other arithmetic  56.1 us (9%)
  local copies, waits for them, and re-layouts  38.7 us (6%)
  between operations  22.8 us (4%)
  matrix products  12.8 us (2%)
    pallas_call x1, Pallas kernels, gather_pallas(): pl.pallas_call(functools.partial(gather_kernel, depth, mp), out_shape=[ja...  174 us
    pallas_call x1, Pallas kernels, weight_grads(): pl.pallas_call(functools.partial(weight_grad_kernel, depth, (ya.shape[2]...  163 us
    pallas_call x1, Pallas kernels, ffn(): pl.pallas_call(ffn_kernel, grid=(2 * blocks,), out_shape=[jax.ShapeDtypeS...  59.7 us
    pallas_call x1, Pallas kernels, attn_backward(): pl.pallas_call(attn_backward_kernel, grid=(blocks,), out_shape=[jax.Shape...  56.6 us
    sub x6, other arithmetic, adam(): weight - LEARN_RATE * (m_hat / (jnp.sqrt(v_hat) + ADAM_EPS) + WEIGHT_DECA...  27.3 us
  transfers between devices with their start and end apart: 2, of which 1 were waited for; matrix products, arithmetic and copies ran while one was open for 6% of the time, Pallas kernels for 27%

profile of v2, /device:TPU:0, one launch (start us, length us, event | category | flops | bytes accessed | tf_op | source)
XLA Modules:
  0.0 596.1 jit_solution(11904684737948387730)
XLA Ops:
  7.3 0.8 fusion.46
  8.2 0.9 reshape.357.col_ref
  9.1 1.1 convert.86
  10.2 0.7 slice_bitcast_fusion.9
  11.0 1.6 convert_bitcast_fusion.1
  12.6 1.7 convert_bitcast_fusion
  14.4 2.0 convert_element_type.69
  16.4 1.2 pad_dynamic-slice_fusion.4.t1_ref
  18.2 4.1 pad_dynamic-slice_fusion.2.t2_ref
  25.1 1.7 copy.68.cos_ref
  26.7 0.9 pad_maximum_fusion.4
  27.8 1.7 copy.69.sin_ref
  30.2 1.0 convolution_add_fusion.1.part_ref
  32.2 2.0 concatenate.62.wa_ref
  34.2 2.5 dynamic-slice_convert_fusion
  37.3 174.4 %gather_weights.1 = (bf16[4,1152,1152]{2,1,0:T(8,128)(2,1)}, bf16[4,1152,2304]{2,1,0:T(8,128)(2,1)}, f32[4,9216]{1,0:T(4,128)}, f32[64,1152]{1,0:T(8,128)}, f32[...) custom-call(bf16[144,1152]{1,0:T(8,128)(2,1)} %concatenate.62.wa_ref, ...), custom_call_target="tpu_custom_call" | custom-call | tf_op jit(solution)/shard_map/gather_weights/pallas_call | solution.py:423
  211.7 1.6 slice.296.head_ref
  213.3 1.5 slice_reduce_fusion
  217.1 59.7 %feed_forward.1 = (bf16[4,640,2304]{2,1,0:T(8,128)(2,1)}, f32[640,1152]{1,0:T(8,128)}, bf16[640,1152]{1,0:T(8,128)(2,1)}, bf16[1152,640]{1,0:T(8,128)(2,1)}, bf1...) custom-call(bf16[640,1152]{1,0:T(8,128)(2,1)} %get-tuple-element.87.m_ref, ...), custom_call_target="tpu_custom_call" | custom-call | tf_op jit(solution)/shard_map/feed_forward/pallas_call | solution.py:1100
  276.8 56.6 %attn_backward.1 = (bf16[4,640,1152]{2,1,0:T(8,128)(2,1)}, f32[24,1152]{1,0:T(8,128)}, f32[2,4,1152]{2,1,0:T(4,128)}) custom-call(bf16[640,1152]{1,0:T(8,128)(2,1)} %get-tuple-element.97.grad_ref, f32[640,1152]{1,0:T(8,128)} %get-tuple-element.98.gx1_ref, f32[640,1152]{1,0:T(8,128)} %get-tuple-element.99.x0_ref, bf16[16,640]{1,0:T(8,128)(2,1)} %patch_ref.3, ...), custom_call_target="tpu_custom_call" | custom-call | tf_op jit(solution)/shard_map/attn_backward/pallas_call | solution.py:1178
  333.4 0.8 fusion.50
  334.2 2.5 concatenate.70
  336.8 1.6 pad_maximum_fusion.2
  338.5 4.4 convert_element_type.78.mod_ref
  344.3 2.5 concatenate.68.gmod_ref
  346.8 163.5 %weight_grads.1 = (f32[3,144,1152]{2,1,0:T(8,128)}, bf16[8,32,1152]{2,1,0:T(8,128)(2,1)}) custom-call(bf16[1152,640]{1,0:T(8,128)(2,1)} %get-tuple-element.86.at_ref, bf16[1152,640]{1,0:T(8,128)(2,1)} %get-tuple-element.94.pt_ref, bf16[1152,640]{1,0:T(8,128)(2,1)} %get-tuple-element.95.mt_ref, bf16[1152,640]{1,0:T(8,128)(2,1)} %get-tuple-element.96.ot_ref, ...), custom_call_target="tpu_custom_call" | custom-call | tf_op jit(solution)/shard_map/weight_grads/pallas_call | solution.py:761
  510.3 1.9 multiply_reduce_fusion.2
  512.2 1.6 slice_bitcast_fusion.2
  513.8 0.9 fusion.10
  514.7 1.0 slice_bitcast_fusion.3
  515.7 1.2 slice.210
  516.9 0.8 fusion.48
  519.0 1.0 slice_bitcast_fusion.6
  521.8 2.3 fusion.21
  524.2 1.2 concatenate.72
  525.4 4.3 reshape.346
  530.4 4.9 multiply_reduce_fusion
  535.3 1.0 convert_reduce_fusion
  537.5 4.6 multiply_reduce_fusion.1
  542.8 0.7 maximum_maximum_fusion
  544.2 10.9 %sum_scalars.1 = f32[8,128]{1,0:T(8,128)} custom-call(f32[8,128]{1,0:T(8,128)} %broadcast.152.in_ref), custom_call_target="tpu_custom_call" | custom-call | tf_op jit(solution)/shard_map/sum_scalars/pallas_call | solution.py:816
  555.1 1.3 fusion.51
  558.4 2.3 multiply_subtract_fusion.5
  560.8 2.5 multiply_subtract_fusion.4
  563.3 14.7 %multiply_subtract_fusion = (f32[144,9216]{1,0:T(8,128)}, f32[144,9216]{1,0:T(8,128)}, f32[144,9216]{1,0:T(8,128)}) fusion(f32[144,9216]{1,0:T(8,128)} %param.52, f32[]{:T(128)} %bitcast.43, f32[]{:T(128)} %bitcast.42, f32[144,9216]{1,0:T(8,128)} %get-tuple-element.183, f32[]{:T(128)} %bitcast.41, f32[144,9216]{1,0:T(8,128)} %param.54, f32[144,9216]{1,0:T(8,128)} %param.53), kind=kLoop, calls=%fused_computation.9 | loop fusion | flops 21233664 | bytes 37158924 | tf_op jit(solution)/shard_map/sub | solution.py:86
  578.1 4.1 multiply_subtract_fusion.1
  582.3 1.9 multiply_subtract_fusion.2
  584.9 1.6 multiply_subtract_fusion.3
  (119 shorter events, 13.6 us)
Async XLA Ops:
  7.2 7.1 %copy-start.2 = (f32[2,144,768]{2,1,0:T(8,128)S(1)}, f32[2,144,768]{2,1,0:T(8,128)}, u32[]{:S(2)}) copy-start(f32[2,144,768]{2,1,0:T(8,128)} %param.46) | copy-start | bytes 2654212
  7.2 7.2 %copy-start.23 = (s32[16]{0:T(128)S(1)}, s32[16]{0:T(128)}, u32[]{:S(2)}) copy-start(s32[16]{0:T(128)} %param.36) | copy-start | bytes 196
  7.2 7.2 %copy-start.25 = (s32[16]{0:T(128)S(1)}, s32[16]{0:T(128)}, u32[]{:S(2)}) copy-start(s32[16]{0:T(128)} %param.37) | copy-start | bytes 196
  7.2 518.1 %all-gather.2.cloned.1.call-start = ((), (), s32[]{:S(2)}) async-start(), calls=%async_computation | async-start | bytes 2433024 | tf_op jit(solution)/shard_map/all_gather | solution.py:1385
  27.8 4.2 copy-start.24
  32.2 5.1 copy-start.22
  276.8 57.4 %copy-start.21 = (f32[6,4,1152]{2,1,0:T(4,128)S(1)}, f32[6,4,1152]{2,1,0:T(4,128)}, u32[]{:S(2)}) copy-start(f32[6,4,1152]{2,1,0:T(4,128)} %get-tuple-element.106) | copy-start | bytes 331780
  276.8 60.0 %copy-start.18 = (f32[32,1152]{1,0:T(8,128)S(1)}, f32[32,1152]{1,0:T(8,128)}, u32[]{:S(2)}) copy-start(f32[32,1152]{1,0:T(8,128)} %get-tuple-element.114) | copy-start | bytes 442372
  336.8 200.7 %all-reduce.8.cloned.1.call-start = ((), (), s32[]{:S(2)}) async-start(), calls=%async_computation.1 | async-start | bytes 516096 | tf_op jit(solution)/shard_map/psum | solution.py:1392
  338.5 4.4 copy-start.20
  338.5 5.1 copy-start.19
  513.8 6.2 %copy-start.1 = (f32[144,1152]{1,0:T(8,128)}, f32[144,1152]{1,0:T(8,128)S(1)}, u32[]{:S(2)}) copy-start(f32[144,1152]{1,0:T(8,128)S(1)} %get-tuple-element.143) | copy-start | bytes 1990660
  513.8 3.1 copy-start.16
  514.7 6.6 %copy-start.17 = (bf16[8,16,1152]{2,1,0:T(8,128)(2,1)S(1)}, bf16[8,16,1152]{2,1,0:T(8,128)(2,1)}, u32[]{:S(2)}) copy-start(bf16[8,16,1152]{2,1,0:T(8,128)(2,1)} %get-tuple-element.111) | copy-start | bytes 884740
  563.3 14.7 %copy-start = (f32[617,1152]{1,0:T(8,128)S(1)}, f32[617,1152]{1,0:T(8,128)}, u32[]{:S(2)}) copy-start(f32[617,1152]{1,0:T(8,128)} %param.55) | copy-start | bytes 8529412
  563.3 14.7 %copy-start.4 = (f32[617,1152]{1,0:T(8,128)S(1)}, f32[617,1152]{1,0:T(8,128)}, u32[]{:S(2)}) copy-start(f32[617,1152]{1,0:T(8,128)} %param.57) | copy-start | bytes 8529412
  563.3 14.7 %copy-start.5 = (f32[617,1152]{1,0:T(8,128)S(1)}, f32[617,1152]{1,0:T(8,128)}, u32[]{:S(2)}) copy-start(f32[617,1152]{1,0:T(8,128)} %param.56) | copy-start | bytes 8529412
  578.0 4.2 copy-start.3
  578.1 4.2 copy-start.7
  578.1 4.2 copy-start.8
  578.1 4.2 copy-start.9
  578.1 4.2 copy-start.10
  582.3 2.0 copy-start.6
  582.3 2.0 copy-start.11
  582.3 2.0 copy-start.12
  582.3 2.0 copy-start.13
  582.3 2.1 copy-start.14
  582.3 2.6 copy-start.15
Sparse Core Ops, SparseCore 0:
  336.9 63.9 all-gather.1
  406.9 130.5 all-reduce.7

commit v3 on v2

--- a/solution.py
+++ b/solution.py
@@ -169,9 +169,10 @@
     depth, mp_count, wa_ref, wf_ref, info_ref, emb_ref, t1_ref, b1_ref, t2_ref, part_ref, tail_ref, mcol_ref,
     patch_ref, cos_ref, sin_ref, col_ref, row_ref,
     wa_all, wf_all, mod_ref, tails_ref, pre_ref, cond_ref, scaled_ref, infos_ref, hid_ref,
-    x0_ref, x1_ref, proj_ref, m_ref, at_ref, mt_ref, qkv_ref, att_ref,
+    x0_out, x1_out, proj_out, m_out, at_out, mt_out, qkv_out, att_out, probs_out,
     info_buf, pre_sum, cond_sum, tail_buf, scaled_buf, hid_buf, mod_part, mod_sum, mod_buf, a_ref, wa_buf,
-    recv, send, local, little_recv, little_send, wa_sem,
+    x0_ref, x1_ref, proj_ref, m_ref, at_ref, mt_ref, qkv_ref, att_ref, probs_buf,
+    recv, send, local, little_recv, little_send, wa_sem, out_sem, probs_sem,
 ):
     dp_count = 2 * depth
     z, x, y, c, first, second = coordinates()
@@ -374,11 +375,23 @@
 
     later = [pair for moment in steps[depth + 2 :] for pair in moment]
 
+    def stored(m, i):
+        return pltpu.make_async_copy(probs_buf.at[i % 2], probs_out.at[m, i], probs_sem.at[i % 2])
+
     def heads(m, _):
         pl.when(m + 1 < mp_count)(lambda: load(m + 1).start())
         load(m).wait()
+
+        def keep(i, probs):
+            if i > 1:
+                stored(m, i - 2).wait()
+            else:
+                pl.when(m > 0)(lambda: stored(m - 1, probs_out.shape[1] - 2 + i).wait())
+            probs_buf[i % 2] = probs
+            stored(m, i).start()
+
         proj_ref[...] += attn_block(
-            wa_buf.at[m % 2], cos_ref, sin_ref, col_ref, row_ref, a_ref, qkv_ref.at[m], att_ref.at[m]
+            wa_buf.at[m % 2], cos_ref, sin_ref, col_ref, row_ref, a_ref, qkv_ref.at[m], att_ref.at[m], keep
         )
         for i in range(mp_count):
             part = later[i * len(later) // mp_count : (i + 1) * len(later) // mp_count]
@@ -391,14 +404,25 @@
         return 0
 
     lax.fori_loop(0, mp_count, heads, 0)
+    for i in range(2):
+        stored(mp_count - 1, probs_out.shape[1] - 2 + i).wait()
     hid_a.wait()
     info.wait()
     scaled_ref[...] = scaled_buf[...]
     infos_ref[...] = info_buf[...]
     hid_ref[...] = hid_buf[...]
     attn_end(mod_ref, col_ref, x0_ref, proj_ref, x1_ref, m_ref, mt_ref)
+    made = (
+        (x0_ref, x0_out), (x1_ref, x1_out), (proj_ref, proj_out), (m_ref, m_out),
+        (at_ref, at_out), (mt_ref, mt_out), (qkv_ref, qkv_out), (att_ref, att_out),
+    )
+    leaving = [pltpu.make_async_copy(a, b, out_sem.at[i]) for i, (a, b) in enumerate(made)]
+    for move in leaving:
+        move.start()
     for g in range(1, count):
         settle(g)
+    for move in leaving:
+        move.wait()
     for g in range(count):
         for k in range(depth + 2):
             stage(g, k, False)
@@ -416,27 +440,34 @@
     shapes = [
         ((images // mp, mp * width), F32), ((tail, D), F32), ((images, D), F32), ((images, D), F32),
         ((dp, images, D), LOW), ((dp, 8, 128), F32), ((dp, images, D), LOW),
+    ]
+    late = [
         (full, F32), (full, F32), (full, F32), (full, LOW), (turned, LOW), (turned, LOW),
         ((mp, tokens, 3 * heads), LOW), ((mp, tokens, heads), LOW),
     ]
+    probs = ((mp, tokens // PAIR * (heads // HD), PAIR, PAIR), F32)
     hbm, vmem = pl.BlockSpec(memory_space=pl.ANY), pl.BlockSpec(memory_space=pltpu.VMEM)
     return pl.pallas_call(
         functools.partial(gather_kernel, depth, mp),
         out_shape=[jax.ShapeDtypeStruct((mp, dp * s.shape[0], s.shape[1]), s.dtype) for s in (wa, wf)]
-        + [jax.ShapeDtypeStruct(*s) for s in shapes],
+        + [jax.ShapeDtypeStruct(*s) for s in shapes + late + [probs]],
         in_specs=[hbm] * 2 + [vmem] * 13,
-        out_specs=[hbm] * 2 + [vmem] * len(shapes),
+        out_specs=[hbm] * 2 + [vmem] * len(shapes) + [hbm] * (len(late) + 1),
         scratch_shapes=[
             pltpu.VMEM((dp, 8, 128), F32), pltpu.VMEM((mp, images, D), F32), pltpu.VMEM((mp, images, D), F32),
             pltpu.VMEM((mp, tail, D), LOW), pltpu.VMEM((dp, images, D), LOW), pltpu.VMEM((dp, images, D), LOW),
             pltpu.VMEM((dp, images, width), F32), pltpu.VMEM((dp, images, width), F32),
             pltpu.VMEM((mp, images, width), F32),
             pltpu.VMEM(full, LOW), pltpu.VMEM((2, D, wa.shape[1]), LOW),
+            *(pltpu.VMEM(*s) for s in late),
+            pltpu.VMEM((2, PAIR, PAIR), F32),
             pltpu.SemaphoreType.DMA((groups, 2, 4, depth)),
             pltpu.SemaphoreType.DMA((groups * (depth + 2) * SENDS,)),
             pltpu.SemaphoreType.DMA((groups,)),
             pltpu.SemaphoreType.DMA((8 * dp,)),
             pltpu.SemaphoreType.DMA((8 * dp,)),
+            pltpu.SemaphoreType.DMA((2,)),
+            pltpu.SemaphoreType.DMA((len(late),)),
             pltpu.SemaphoreType.DMA((2,)),
         ],
         compiler_params=pltpu.CompilerParams(
@@ -481,7 +512,7 @@
     depth, widths, mp_count, at_ref, pt_ref, mt_ref, ot_ref, ya_ref, yf_ref, gmod_ref, mod_ref, t2_ref, cond_ref, pre_ref,
     out_ref, vec_ref,
     x_all, ya_all, yf_all, work, q_send, u_send, q_recv, u_recv,
-    gmod, panel, scaled_send, scaled_recv, joined, own_vec, hid_part, vec_buf,
+    gmod, panel, panel_f, scaled_send, scaled_recv, joined, own_vec, hid_part, vec_buf,
     moves, swaps, landing, send, recv, panel_sem, little_send, little_recv,
 ):
     z, x, y, c, first, second = coordinates()
@@ -516,7 +547,12 @@
         trade(ref.at[2 * j + c], ref.at[2 * j + 1 - c], full.at[j, own, :], full.at[j, theirs, :])
 
     trade_x(2)
-    trade_y(yf_ref, yf_all, 1 - y)
+    for columns in (pl.ds(0, STEP), pl.ds(STEP, STEP)):
+        j = 1 - y
+        trade(
+            yf_ref.at[2 * j + c, :, columns], yf_ref.at[2 * j + 1 - c, :, columns],
+            yf_all.at[j, own, columns], yf_all.at[j, theirs, columns],
+        )
     trade_x(3)
     trade_x(0)
     trade_x(1)
@@ -525,7 +561,7 @@
     trade_y(ya_ref, ya_all, y)
     waits, known = [], set()
     for t, (g, kind, _) in enumerate(ORDER):
-        need = [{0, 1}, {0, 1, 2}, {3, 4, 5}][g] | (set() if kind == 0 else {7} if g == 2 else {6})
+        need = [{0, 1}, {0, 2, 3}, {4, 5, 6}][g] | (set() if kind == 0 else {8} if g == 2 else {7})
         if need - known:
             waits.append((t, sorted(need - known)))
             known |= need
@@ -616,14 +652,14 @@
     lines = gmod_ref.shape[0]
     images = lines // 8
 
-    def panels(count, source, use):
-        fetch = lambda i: pltpu.make_async_copy(source(i), panel.at[i % 2], panel_sem.at[i % 2])
+    def panels(count, source, use, hold):
+        fetch = lambda i: pltpu.make_async_copy(source(i), hold.at[i % 2], panel_sem.at[i % 2])
         fetch(0).start()
         for i in range(count):
             if i + 1 < count:
                 fetch(i + 1).start()
             fetch(i).wait()
-            use(i, panel.at[i % 2])
+            use(i, hold.at[i % 2])
 
     def one_hot(shape, hit):
         row, col = (lax.broadcasted_iota(jnp.int32, shape, i) for i in range(2))
@@ -641,9 +677,9 @@
         def use(j, piece):
             hit = lambda r, q: (r // 8 == q // lines) & (q % lines == j * images + r % 8) & (r % 8 < images)
             part = dot(one_hot((8 * dp_count, dp_count * lines), hit), every).astype(LOW)
-            scaled_send[...] += dot_nt(part, piece[...]).reshape(scaled_send.shape)
-
-        panels(8, lambda j: mod_ref.at[:, pl.ds(j * D, D)], use)
+            scaled_send[...] += dot_nt(part, piece[...].astype(LOW)).reshape(scaled_send.shape)
+
+        panels(8, lambda j: mod_ref.at[:, pl.ds(j * D, D)], use, panel_f)
         scaled_recv[dp] = scaled_send[dp]
         scaled_r.push()
 
@@ -660,7 +696,7 @@
         def use(i, piece):
             hid_part[mp, :, i * rows : (i + 1) * rows] = dot_nt(vectors, piece[...])
 
-        panels(D // rows, lambda i: t2_ref.at[pl.ds(i * rows, rows), :], use)
+        panels(D // rows, lambda i: t2_ref.at[pl.ds(i * rows, rows), :], use, panel)
         hid_r.push()
 
     def first_grad():
@@ -774,15 +810,16 @@
             pltpu.VMEM((3, slots, 1, STEP), F32),
             pltpu.VMEM((dp, *grad_mod.shape), LOW),
             pltpu.VMEM((2, rows, D), LOW),
+            pltpu.VMEM((2, rows, D), F32),
             pltpu.VMEM((dp, 8, rows), F32),
             pltpu.VMEM((dp, 8, rows), F32),
             pltpu.VMEM((8, D), F32),
             pltpu.VMEM((mp, 8, D), F32),
             pltpu.VMEM((mp, 8 * mp, D), F32),
             pltpu.VMEM(vectors, LOW),
-            pltpu.SemaphoreType.DMA((8,)),
-            pltpu.SemaphoreType.DMA((8,)),
-            pltpu.SemaphoreType.DMA((8,)),
+            pltpu.SemaphoreType.DMA((9,)),
+            pltpu.SemaphoreType.DMA((9,)),
+            pltpu.SemaphoreType.DMA((9,)),
             pltpu.SemaphoreType.DMA((2, RING)),
             pltpu.SemaphoreType.DMA((2, 3, slots)),
             pltpu.SemaphoreType.DMA((2,)),
@@ -836,7 +873,7 @@
 
 
 def by_block(*shape):
-    return pl.BlockSpec((1, *shape), lambda m: (m, 0, 0))
+    return pl.BlockSpec((1, *shape), lambda m: (m,) + (0,) * len(shape))
 
 
 def dot(left, right):
@@ -889,9 +926,9 @@
 
 
 def softmax(query, key, same):
-    scores = jnp.where(same, dot_nt(query, key) * HD ** (-0.5), -1e30)
-    expo = jnp.exp(scores - jnp.max(scores, -1, keepdims=True))
-    return expo * (1.0 / jnp.sum(expo, -1, keepdims=True))
+    scores = jnp.where(same, dot_nt(key, query) * (HD ** (-0.5) * math.log2(math.e)), -1e30)
+    expo = jnp.exp2(scores - jnp.max(scores, 0, keepdims=True))
+    return expo * (1.0 / jnp.sum(expo, 0, keepdims=True))
 
 
 def attn_begin(patch_ref, patch_rows, patch_bias, mod_ref, col_ref, x0_ref, a_ref, at_ref):
@@ -908,7 +945,7 @@
     at_ref[...] = a_ref[...].T
 
 
-def attn_block(w_ref, cos_ref, sin_ref, col_ref, row_ref, a_ref, qkv_ref, att_ref):
+def attn_block(w_ref, cos_ref, sin_ref, col_ref, row_ref, a_ref, qkv_ref, att_ref, keep):
     tokens, width = att_ref.shape
     made = dot(a_ref[...], w_ref[:, : 3 * width])
     qkv_ref[:, : 2 * width] = turn(made[:, : 2 * width], cos_ref[...], sin_ref[...], 1.0).astype(LOW)
@@ -918,8 +955,9 @@
         rows = slice(block * PAIR, (block + 1) * PAIR)
         for head in range(width // HD):
             take = lambda i: qkv_ref[rows, i * width + head * HD : i * width + (head + 1) * HD]
-            probs = softmax(take(0), take(1), same).astype(LOW)
-            att_ref[rows, head * HD : (head + 1) * HD] = dot(probs, take(2)).astype(LOW)
+            probs = softmax(take(0), take(1), same)
+            keep(block * (width // HD) + head, probs)
+            att_ref[rows, head * HD : (head + 1) * HD] = dot_tn(probs.astype(LOW), take(2)).astype(LOW)
     return dot_nt(att_ref[...], w_ref[:, 3 * width :])
 
 
@@ -939,7 +977,7 @@
 
 def attn_forward_kernel(
     patch_ref, prow_ref, pbias_ref, mod_ref, w_ref, cos_ref, sin_ref, col_ref, row_ref,
-    x0_ref, x1_ref, proj_ref, m_ref, at_ref, mt_ref, qkv_ref, att_ref, a_ref,
+    x0_ref, x1_ref, proj_ref, m_ref, at_ref, mt_ref, qkv_ref, att_ref, probs_ref, a_ref,
 ):
     step, last = pl.program_id(0), pl.num_programs(0) - 1
 
@@ -948,8 +986,11 @@
         attn_begin(patch_ref, prow_ref[...], pbias_ref[...], mod_ref, col_ref, x0_ref, a_ref, at_ref)
         proj_ref[...] = jnp.zeros(proj_ref.shape, F32)
 
+    def keep(i, probs):
+        probs_ref[0, i] = probs
+
     proj_ref[...] += attn_block(
-        w_ref.at[0], cos_ref, sin_ref, col_ref, row_ref, a_ref, qkv_ref.at[0], att_ref.at[0]
+        w_ref.at[0], cos_ref, sin_ref, col_ref, row_ref, a_ref, qkv_ref.at[0], att_ref.at[0], keep
     )
 
     @pl.when(step == last)
@@ -972,11 +1013,13 @@
         + [
             jax.ShapeDtypeStruct((blocks, tokens, 3 * width), LOW),
             jax.ShapeDtypeStruct((blocks, tokens, width), LOW),
+            jax.ShapeDtypeStruct((blocks, tokens // PAIR * (width // HD), PAIR, PAIR), F32),
         ],
         in_specs=[whole(a.shape) for a in ins] + [by_block(D, 4 * width)] + [whole(a.shape) for a in tables],
         out_specs=[whole(full)] * 4
         + [whole(turned)] * 2
-        + [by_block(tokens, 3 * width), by_block(tokens, width)],
+        + [by_block(tokens, 3 * width), by_block(tokens, width)]
+        + [by_block(tokens // PAIR * (width // HD), PAIR, PAIR)],
         scratch_shapes=[pltpu.VMEM(full, LOW)],
         compiler_params=pltpu.CompilerParams(vmem_limit_bytes=VMEM_LIMIT),
         name="attn_forward",
@@ -1114,7 +1157,7 @@
 
 
 def attn_backward_kernel(
-    grad_ref, gx1_ref, x0_ref, patch_ref, mod_ref, w_ref, qkv_ref, att_ref, cos_ref, sin_ref, col_ref, row_ref,
+    grad_ref, gx1_ref, x0_ref, patch_ref, mod_ref, w_ref, qkv_ref, att_ref, probs_ref, cos_ref, sin_ref, col_ref, row_ref,
     out_ref, rows_ref, sums_ref, tmp_ref, back_att, back_ref, low_ref,
 ):
     width = att_ref.shape[2]
@@ -1123,19 +1166,18 @@
     step, last = pl.program_id(0), pl.num_programs(0) - 1
     back_att[...] = dot(grad_ref[...], w_ref[0, :, 3 * width :]).astype(LOW)
     for block in range(tokens // PAIR):
-        same = same_image(col_ref, row_ref, block)
         rows = slice(block * PAIR, (block + 1) * PAIR)
         for head in range(width // HD):
             lanes = lambda i: slice(i * width + head * HD, i * width + (head + 1) * HD)
             query, key, value = (qkv_ref[0, rows, lanes(i)] for i in range(3))
             grad = back_att[rows, lanes(0)]
-            probs = softmax(query, key, same)
-            grad_p = dot_nt(grad, value)
-            centre = jnp.sum(probs * grad_p, -1, keepdims=True)
+            probs = probs_ref[0, block * (width // HD) + head]
+            grad_p = dot_nt(value, grad)
+            centre = jnp.sum(probs * grad_p, 0, keepdims=True)
             grad_s = (probs * (grad_p - centre)).astype(LOW)
-            tmp_ref[rows, lanes(0)] = dot(grad_s, key) * scale
-            tmp_ref[rows, lanes(1)] = dot_tn(grad_s, query) * scale
-            tmp_ref[rows, lanes(2)] = dot_tn(probs.astype(LOW), grad)
+            tmp_ref[rows, lanes(0)] = dot_tn(grad_s, key) * scale
+            tmp_ref[rows, lanes(1)] = dot(grad_s, query) * scale
+            tmp_ref[rows, lanes(2)] = dot(probs.astype(LOW), grad)
     out_ref[0, :, : 2 * width] = turn(tmp_ref[:, : 2 * width], cos_ref[...], sin_ref[...], -1.0).astype(LOW)
     out_ref[0, :, 2 * width : 3 * width] = tmp_ref[:, 2 * width :].astype(LOW)
     out_ref[0, :, 3 * width :] = att_ref[0]
@@ -1170,7 +1212,7 @@
         rows_ref[PATCH_IN + 1 :, :] = jnp.zeros((7, D), F32)
 
 
-def attn_backward(grad_proj, gx1, x_zero, patches, modulation, wa_all, qkv, att, tables):
+def attn_backward(grad_proj, gx1, x_zero, patches, modulation, wa_all, qkv, att, probs, tables):
     blocks, tokens, width = att.shape
     full = (tokens, D)
     ins = (grad_proj, gx1, x_zero, patches, modulation)
@@ -1181,7 +1223,7 @@
         out_shape=[jax.ShapeDtypeStruct((blocks, tokens, 4 * width), LOW)]
         + [jax.ShapeDtypeStruct(*o) for o in outs],
         in_specs=[whole(a.shape) for a in ins]
-        + [by_block(D, 4 * width), by_block(tokens, 3 * width), by_block(tokens, width)]
+        + [by_block(D, 4 * width), by_block(tokens, 3 * width), by_block(tokens, width), by_block(*probs.shape[1:])]
         + [whole(a.shape) for a in tables],
         out_specs=[by_block(tokens, 4 * width)] + [whole(o[0]) for o in outs],
         scratch_shapes=[
@@ -1190,7 +1232,7 @@
         ],
         compiler_params=pltpu.CompilerParams(vmem_limit_bytes=VMEM_LIMIT),
         name="attn_backward",
-    )(*ins, wa_all, qkv, att, *tables)
+    )(*ins, wa_all, qkv, att, probs, *tables)
 
 
 def gather_library(wa, wf, small):
@@ -1285,7 +1327,6 @@
     wf = jnp.concatenate([ffn_in_w[0], ffn_in_w[1], ffn_out_w.T], 1).astype(LOW)
 
     table_b = table_w.astype(LOW)
-    mod_b = mod_w.astype(LOW)
     gap = D + 16
     padded = lax.dynamic_update_slice(jnp.zeros((2 * gap + own_rows, D), LOW), table_b, (gap, 0))
 
@@ -1324,14 +1365,14 @@
     if regular:
         gathered = gather_pallas(wa, wf, small, patches, tables, dp_count, mp_count)
         wa_all, wf_all, modulation, tail, pre, cond, scaled, infos, hidden = gathered[:9]
-        x_zero, x_one, proj, m_in, a_turned, m_turned, qkv, att = gathered[9:]
+        x_zero, x_one, proj, m_in, a_turned, m_turned, qkv, att, probs = gathered[9:]
     else:
         wa_all, wf_all, mod_all, tails, pre, cond, scaled, infos, hidden = gather_library(wa, wf, small)
         tail = jnp.sum(tails.astype(F32), 0)
         mod_own = lax.dynamic_slice_in_dim(mod_all, mp_index * images, images, 1)
         mod_bias = tail[ROW_MOD_BIAS - ROW_PATCH : TAIL].reshape(-1)
         modulation = mod_own.transpose(1, 0, 2).reshape(images, -1) + mod_bias
-        x_zero, x_one, proj, m_in, a_turned, m_turned, qkv, att = attn_forward(
+        x_zero, x_one, proj, m_in, a_turned, m_turned, qkv, att, probs = attn_forward(
             patches, tail[:PATCH_IN].astype(LOW), tail[PATCH_IN][None, :], modulation, wa_all, tables
         )
     count_all = dp_count * group_images
@@ -1364,7 +1405,7 @@
         m_in, x_one, proj, modulation, head_rows, target, weights, even_col, wf_all
     )
     ya, grad_patch, sums_a = attn_backward(
-        grad_proj, grad_x1, x_zero, patches, modulation, wa_all, qkv, att, tables
+        grad_proj, grad_x1, x_zero, patches, modulation, wa_all, qkv, att, probs, tables
     )
     loss_part = loss[0, 0]
     x_turned = (a_turned, proj_turned, m_turned, mo_turned)
@@ -1375,11 +1416,11 @@
     pre_own = jnp.pad(pre.reshape(mp_count, images, D), ((0, 0), (0, 8 - images), (0, 0)))
     if regular:
         summed, vectors = weight_grads(
-            x_turned, ya, yf, grad_mod, mod_b, small[4], cond_own, pre_own.reshape(-1, D), dp_count
+            x_turned, ya, yf, grad_mod, mod_w, small[4], cond_own, pre_own.reshape(-1, D), dp_count
         )
     else:
         summed = plane_grads(x_turned, ya, yf)
-        vectors = vector_grads(grad_mod, mod_b, small[4], cond, pre)
+        vectors = vector_grads(grad_mod, mod_w.astype(LOW), small[4], cond, pre)
     own_wf, own_wa = jnp.concatenate([summed[0], summed[1]], 1), summed[2]
 
     grad_mod_all = lax.all_gather(grad_mod, BOTH, axis=0).reshape(-1, 8, images, D)

time: 605 us -> 594 us (0.982)
  Pallas kernels: 465 us -> 455 us
    pallas_call x1, Pallas kernels: 56.6 us -> 47 us  [attn_backward(): pl.pallas_call(attn_backward_kernel, grid=(blocks,), out_shape=[jax.Shape...]
  transfers between devices with their start and end apart: 2 -> 2, of which waited for: 1 -> 1; matrix products, arithmetic and copies ran while one was open for 6% -> 5% of each run, Pallas kernels for 27% -> 28%
where the time goes in v3:
time: 594 us; the launch traced here: 586 us
  Pallas kernels  455 us (77%)
  other arithmetic  51.7 us (9%)
  local copies, waits for them, and re-layouts  38.7 us (7%)
  between operations  22.8 us (4%)
  matrix products  12.8 us (2%)
    pallas_call x1, Pallas kernels, gather_pallas(): pl.pallas_call(functools.partial(gather_kernel, depth, mp), out_shape=[ja...  173 us
    pallas_call x1, Pallas kernels, weight_grads(): pl.pallas_call(functools.partial(weight_grad_kernel, depth, (ya.shape[2]...  165 us
    pallas_call x1, Pallas kernels, ffn(): pl.pallas_call(ffn_kernel, grid=(2 * blocks,), out_shape=[jax.ShapeDtypeS...  59.7 us
    pallas_call x1, Pallas kernels, attn_backward(): pl.pallas_call(attn_backward_kernel, grid=(blocks,), out_shape=[jax.Shape...  47 us
    sub x6, other arithmetic, adam(): weight - LEARN_RATE * (m_hat / (jnp.sqrt(v_hat) + ADAM_EPS) + WEIGHT_DECA...  27.3 us
  transfers between devices with their start and end apart: 2, of which 1 were waited for; matrix products, arithmetic and copies ran while one was open for 5% of the time, Pallas kernels for 28%

profile of v3, /device:TPU:0, one launch (start us, length us, event | category | flops | bytes accessed | tf_op | source)
XLA Modules:
  0.0 585.6 jit_solution(8269911267057792120)
XLA Ops:
  7.3 0.8 fusion.46
  8.2 0.9 reshape.357.col_ref
  9.1 1.1 convert.86
  10.2 0.7 slice_bitcast_fusion.9
  11.0 1.6 convert_bitcast_fusion.1
  12.6 1.7 convert_bitcast_fusion
  14.4 2.0 convert_element_type.66
  16.4 1.2 pad_dynamic-slice_fusion.4.t1_ref
  18.2 4.1 pad_dynamic-slice_fusion.2.t2_ref
  25.1 1.7 copy.68.cos_ref
  26.7 0.9 pad_maximum_fusion.4
  27.8 1.7 copy.69.sin_ref
  30.2 1.0 convolution_add_fusion.1.part_ref
  32.2 2.0 concatenate.62.wa_ref
  34.2 2.5 dynamic-slice_convert_fusion
  37.3 172.8 %gather_weights.1 = (bf16[4,1152,1152]{2,1,0:T(8,128)(2,1)}, bf16[4,1152,2304]{2,1,0:T(8,128)(2,1)}, f32[4,9216]{1,0:T(4,128)}, f32[64,1152]{1,0:T(8,128)}, f32[...) custom-call(bf16[144,1152]{1,0:T(8,128)(2,1)} %concatenate.62.wa_ref, ...), custom_call_target="tpu_custom_call" | custom-call | tf_op jit(solution)/shard_map/gather_weights/pallas_call | solution.py:450
  210.1 1.6 slice.296.head_ref
  211.7 1.5 slice_reduce_fusion
  215.5 59.7 %feed_forward.1 = (bf16[4,640,2304]{2,1,0:T(8,128)(2,1)}, f32[640,1152]{1,0:T(8,128)}, bf16[640,1152]{1,0:T(8,128)(2,1)}, bf16[1152,640]{1,0:T(8,128)(2,1)}, bf1...) custom-call(bf16[640,1152]{1,0:T(8,128)(2,1)} %get-tuple-element.88.m_ref, ...), custom_call_target="tpu_custom_call" | custom-call | tf_op jit(solution)/shard_map/feed_forward/pallas_call | solution.py:1143
  275.2 47.0 %attn_backward.1 = (bf16[4,640,1152]{2,1,0:T(8,128)(2,1)}, f32[24,1152]{1,0:T(8,128)}, f32[2,4,1152]{2,1,0:T(4,128)}) custom-call(bf16[640,1152]{1,0:T(8,128)(2,1)} %get-tuple-element.98.grad_ref, f32[640,1152]{1,0:T(8,128)} %get-tuple-element.99.gx1_ref, f32[640,1152]{1,0:T(8,128)} %get-tuple-element.100.x0_ref, bf16[16,640]{1,0:T(8,128)(2,1)} %patch_ref.3, ...), custom_call_target="tpu_custom_call" | custom-call | tf_op jit(solution)/shard_map/attn_backward/pallas_call | solution.py:1220
  322.3 0.8 fusion.50
  323.1 2.5 concatenate.70
  325.7 1.6 pad_maximum_fusion.2
  328.7 2.5 concatenate.68.gmod_ref
  331.3 164.7 %weight_grads.1 = (f32[3,144,1152]{2,1,0:T(8,128)}, bf16[8,32,1152]{2,1,0:T(8,128)(2,1)}) custom-call(bf16[1152,640]{1,0:T(8,128)(2,1)} %get-tuple-element.87.at_ref, bf16[1152,640]{1,0:T(8,128)(2,1)} %get-tuple-element.95.pt_ref, bf16[1152,640]{1,0:T(8,128)(2,1)} %get-tuple-element.96.mt_ref, bf16[1152,640]{1,0:T(8,128)(2,1)} %get-tuple-element.97.ot_ref, ...), custom_call_target="tpu_custom_call" | custom-call | tf_op jit(solution)/shard_map/weight_grads/pallas_call | solution.py:797
  496.0 1.9 multiply_reduce_fusion.2
  497.9 1.6 slice_bitcast_fusion.2
  499.5 0.9 fusion.10
  500.4 1.0 slice_bitcast_fusion.3
  501.4 1.2 slice.210
  502.6 0.8 fusion.48
  504.7 1.0 slice_bitcast_fusion.6
  507.6 2.3 fusion.21
  509.9 1.2 concatenate.72
  511.1 4.3 reshape.346
  516.1 4.9 multiply_reduce_fusion
  521.1 1.0 convert_reduce_fusion
  522.7 4.4 all-reduce.8.cloned.1.call-done
  527.0 4.6 multiply_reduce_fusion.1
  532.3 0.7 maximum_maximum_fusion
  533.7 10.9 %sum_scalars.1 = f32[8,128]{1,0:T(8,128)} custom-call(f32[8,128]{1,0:T(8,128)} %broadcast.152.in_ref), custom_call_target="tpu_custom_call" | custom-call | tf_op jit(solution)/shard_map/sum_scalars/pallas_call | solution.py:853
  544.7 1.3 fusion.51
  548.0 2.3 multiply_subtract_fusion.5
  550.3 2.5 multiply_subtract_fusion.4
  552.9 14.7 %multiply_subtract_fusion = (f32[144,9216]{1,0:T(8,128)}, f32[144,9216]{1,0:T(8,128)}, f32[144,9216]{1,0:T(8,128)}) fusion(f32[144,9216]{1,0:T(8,128)} %mod_ref.1, f32[]{:T(128)} %bitcast.43, f32[]{:T(128)} %bitcast.42, f32[144,9216]{1,0:T(8,128)} %get-tuple-element.185, f32[]{:T(128)} %bitcast.41, f32[144,9216]{1,0:T(8,128)} %param.54, f32[144,9216]{1,0:T(8,128)} %param.53), kind=kLoop, calls=%fused_computation.9 | loop fusion | flops 21233664 | bytes 37158924 | tf_op jit(solution)/shard_map/sub | solution.py:86
  567.7 4.1 multiply_subtract_fusion.1
  571.9 1.9 multiply_subtract_fusion.2
  574.5 1.6 multiply_subtract_fusion.3
  (118 shorter events, 13.1 us)
Async XLA Ops:
  7.2 7.1 %copy-start.2 = (f32[2,144,768]{2,1,0:T(8,128)S(1)}, f32[2,144,768]{2,1,0:T(8,128)}, u32[]{:S(2)}) copy-start(f32[2,144,768]{2,1,0:T(8,128)} %param.46) | copy-start | bytes 2654212
  7.2 7.2 %copy-start.23 = (s32[16]{0:T(128)S(1)}, s32[16]{0:T(128)}, u32[]{:S(2)}) copy-start(s32[16]{0:T(128)} %param.36) | copy-start | bytes 196
  7.2 7.2 %copy-start.25 = (s32[16]{0:T(128)S(1)}, s32[16]{0:T(128)}, u32[]{:S(2)}) copy-start(s32[16]{0:T(128)} %param.37) | copy-start | bytes 196
  7.2 503.9 %all-gather.2.cloned.1.call-start = ((), (), s32[]{:S(2)}) async-start(), calls=%async_computation | async-start | bytes 2433024 | tf_op jit(solution)/shard_map/all_gather | solution.py:1426
  27.8 4.2 copy-start.24
  32.2 5.1 copy-start.22
  275.2 47.8 %copy-start.21 = (f32[6,4,1152]{2,1,0:T(4,128)S(1)}, f32[6,4,1152]{2,1,0:T(4,128)}, u32[]{:S(2)}) copy-start(f32[6,4,1152]{2,1,0:T(4,128)} %get-tuple-element.108) | copy-start | bytes 331780
  275.2 50.5 %copy-start.18 = (f32[32,1152]{1,0:T(8,128)S(1)}, f32[32,1152]{1,0:T(8,128)}, u32[]{:S(2)}) copy-start(f32[32,1152]{1,0:T(8,128)} %get-tuple-element.116) | copy-start | bytes 442372
  275.2 52.1 %copy-start.20 = (f32[16,1152]{1,0:T(8,128)S(1)}, f32[16,1152]{1,0:T(8,128)}, u32[]{:S(2)}) copy-start(f32[16,1152]{1,0:T(8,128)} %get-tuple-element.109) | copy-start | bytes 221188
  275.2 52.8 %copy-start.19 = (f32[16,1152]{1,0:T(8,128)S(1)}, f32[16,1152]{1,0:T(8,128)}, u32[]{:S(2)}) copy-start(f32[16,1152]{1,0:T(8,128)} %get-tuple-element.110) | copy-start | bytes 221188
  325.6 201.4 %all-reduce.8.cloned.1.call-start = ((), (), s32[]{:S(2)}) async-start(), calls=%async_computation.1 | async-start | bytes 516096 | tf_op jit(solution)/shard_map/psum | solution.py:1433
  499.5 6.3 %copy-start.1 = (f32[144,1152]{1,0:T(8,128)}, f32[144,1152]{1,0:T(8,128)S(1)}, u32[]{:S(2)}) copy-start(f32[144,1152]{1,0:T(8,128)S(1)} %get-tuple-element.145) | copy-start | bytes 1990660
  499.5 3.1 copy-start.16
  500.4 6.6 %copy-start.17 = (bf16[8,16,1152]{2,1,0:T(8,128)(2,1)S(1)}, bf16[8,16,1152]{2,1,0:T(8,128)(2,1)}, u32[]{:S(2)}) copy-start(bf16[8,16,1152]{2,1,0:T(8,128)(2,1)} %get-tuple-element.113) | copy-start | bytes 884740
  552.9 14.7 %copy-start = (f32[617,1152]{1,0:T(8,128)S(1)}, f32[617,1152]{1,0:T(8,128)}, u32[]{:S(2)}) copy-start(f32[617,1152]{1,0:T(8,128)} %param.55) | copy-start | bytes 8529412
  552.9 14.7 %copy-start.4 = (f32[617,1152]{1,0:T(8,128)S(1)}, f32[617,1152]{1,0:T(8,128)}, u32[]{:S(2)}) copy-start(f32[617,1152]{1,0:T(8,128)} %param.57) | copy-start | bytes 8529412
  552.9 14.7 %copy-start.5 = (f32[617,1152]{1,0:T(8,128)S(1)}, f32[617,1152]{1,0:T(8,128)}, u32[]{:S(2)}) copy-start(f32[617,1152]{1,0:T(8,128)} %param.56) | copy-start | bytes 8529412
  567.6 4.2 copy-start.3
  567.6 4.2 copy-start.7
  567.6 4.2 copy-start.8
  567.6 4.2 copy-start.9
  567.6 4.2 copy-start.10
  571.8 2.0 copy-start.6
  571.8 2.0 copy-start.11
  571.9 2.0 copy-start.12
  571.9 2.0 copy-start.13
  571.9 2.1 copy-start.14
  571.9 2.6 copy-start.15
Sparse Core Ops, SparseCore 0:
  325.7 65.1 all-gather.1
  397.0 130.0 all-reduce.7

commit v4 on v3

--- a/solution.py
+++ b/solution.py
@@ -864,7 +864,7 @@
     )(values)
 
 
-SLAB = 64
+SLAB = 160
 VMEM_LIMIT = 60 * 1024 * 1024
 
 

time: 594 us -> 588 us (0.990)
  Pallas kernels: 455 us -> 449 us
where the time goes in v4:
time: 588 us; the launch traced here: 579 us
  Pallas kernels  449 us (76%)
  other arithmetic  51.7 us (9%)
  local copies, waits for them, and re-layouts  38.7 us (7%)
  between operations  22.8 us (4%)
  matrix products  12.8 us (2%)
    pallas_call x1, Pallas kernels, gather_pallas(): pl.pallas_call(functools.partial(gather_kernel, depth, mp), out_shape=[ja...  171 us
    pallas_call x1, Pallas kernels, weight_grads(): pl.pallas_call(functools.partial(weight_grad_kernel, depth, (ya.shape[2]...  165 us
    pallas_call x1, Pallas kernels, ffn(): pl.pallas_call(ffn_kernel, grid=(2 * blocks,), out_shape=[jax.ShapeDtypeS...  56.5 us
    pallas_call x1, Pallas kernels, attn_backward(): pl.pallas_call(attn_backward_kernel, grid=(blocks,), out_shape=[jax.Shape...  45.5 us
    sub x6, other arithmetic, adam(): weight - LEARN_RATE * (m_hat / (jnp.sqrt(v_hat) + ADAM_EPS) + WEIGHT_DECA...  27.3 us
    dot_general x3, matrix products, matmul_tn(): lax.dot_general(left, right, (((0,), (0,)), ((), ())), preferred_element_...  11.8 us
  transfers between devices with their start and end apart: 2, of which 1 were waited for; matrix products, arithmetic and copies ran while one was open for 5% of the time, Pallas kernels for 28%

profile of v4, /device:TPU:0, one launch (start us, length us, event | category | flops | bytes accessed | tf_op | source)
XLA Modules:
  0.0 579.1 jit_solution(17949033001064462994)
XLA Ops:
  7.3 0.8 fusion.46
  8.2 0.9 reshape.357.col_ref
  9.1 1.1 convert.86
  10.2 0.7 slice_bitcast_fusion.9
  11.0 1.6 convert_bitcast_fusion.1
  12.6 1.7 convert_bitcast_fusion
  14.4 2.0 convert_element_type.66
  16.4 1.2 pad_dynamic-slice_fusion.4.t1_ref
  18.2 4.1 pad_dynamic-slice_fusion.2.t2_ref
  25.1 1.7 copy.68.cos_ref
  26.7 0.9 pad_maximum_fusion.4
  27.8 1.7 copy.69.sin_ref
  30.2 1.0 convolution_add_fusion.1.part_ref
  32.2 2.0 concatenate.62.wa_ref
  34.2 2.5 dynamic-slice_convert_fusion
  37.3 171.3 %gather_weights.1 = (bf16[4,1152,1152]{2,1,0:T(8,128)(2,1)}, bf16[4,1152,2304]{2,1,0:T(8,128)(2,1)}, f32[4,9216]{1,0:T(4,128)}, f32[64,1152]{1,0:T(8,128)}, f32[...) custom-call(bf16[144,1152]{1,0:T(8,128)(2,1)} %concatenate.62.wa_ref, ...), custom_call_target="tpu_custom_call" | custom-call | tf_op jit(solution)/shard_map/gather_weights/pallas_call | solution.py:450
  208.6 1.6 slice.296.head_ref
  210.2 1.5 slice_reduce_fusion
  214.0 56.5 %feed_forward.1 = (bf16[4,640,2304]{2,1,0:T(8,128)(2,1)}, f32[640,1152]{1,0:T(8,128)}, bf16[640,1152]{1,0:T(8,128)(2,1)}, bf16[1152,640]{1,0:T(8,128)(2,1)}, bf1...) custom-call(bf16[640,1152]{1,0:T(8,128)(2,1)} %get-tuple-element.88.m_ref, ...), custom_call_target="tpu_custom_call" | custom-call | tf_op jit(solution)/shard_map/feed_forward/pallas_call | solution.py:1143
  270.5 45.5 %attn_backward.1 = (bf16[4,640,1152]{2,1,0:T(8,128)(2,1)}, f32[24,1152]{1,0:T(8,128)}, f32[2,4,1152]{2,1,0:T(4,128)}) custom-call(bf16[640,1152]{1,0:T(8,128)(2,1)} %get-tuple-element.98.grad_ref, f32[640,1152]{1,0:T(8,128)} %get-tuple-element.99.gx1_ref, f32[640,1152]{1,0:T(8,128)} %get-tuple-element.100.x0_ref, bf16[16,640]{1,0:T(8,128)(2,1)} %patch_ref.3, ...), custom_call_target="tpu_custom_call" | custom-call | tf_op jit(solution)/shard_map/attn_backward/pallas_call | solution.py:1220
  316.1 0.8 fusion.50
  316.9 2.5 concatenate.70
  319.5 1.6 pad_maximum_fusion.2
  322.5 2.5 concatenate.68.gmod_ref
  325.1 164.8 %weight_grads.1 = (f32[3,144,1152]{2,1,0:T(8,128)}, bf16[8,32,1152]{2,1,0:T(8,128)(2,1)}) custom-call(bf16[1152,640]{1,0:T(8,128)(2,1)} %get-tuple-element.87.at_ref, bf16[1152,640]{1,0:T(8,128)(2,1)} %get-tuple-element.95.pt_ref, bf16[1152,640]{1,0:T(8,128)(2,1)} %get-tuple-element.96.mt_ref, bf16[1152,640]{1,0:T(8,128)(2,1)} %get-tuple-element.97.ot_ref, ...), custom_call_target="tpu_custom_call" | custom-call | tf_op jit(solution)/shard_map/weight_grads/pallas_call | solution.py:797
  489.9 1.9 multiply_reduce_fusion.2
  491.7 1.6 slice_bitcast_fusion.2
  493.4 0.9 fusion.10
  494.3 1.0 slice_bitcast_fusion.3
  495.3 1.2 slice.210
  496.5 0.8 fusion.48
  498.6 1.0 slice_bitcast_fusion.6
  501.4 2.3 fusion.21
  503.8 1.2 concatenate.72
  505.0 4.3 reshape.346
  510.0 4.9 multiply_reduce_fusion
  514.9 1.0 convert_reduce_fusion
  516.5 3.9 all-reduce.8.cloned.1.call-done
  520.4 4.6 multiply_reduce_fusion.1
  525.7 0.7 maximum_maximum_fusion
  527.1 10.9 %sum_scalars.1 = f32[8,128]{1,0:T(8,128)} custom-call(f32[8,128]{1,0:T(8,128)} %broadcast.152.in_ref), custom_call_target="tpu_custom_call" | custom-call | tf_op jit(solution)/shard_map/sum_scalars/pallas_call | solution.py:853
  538.1 1.3 fusion.51
  541.4 2.3 multiply_subtract_fusion.5
  543.7 2.5 multiply_subtract_fusion.4
  546.3 14.7 %multiply_subtract_fusion = (f32[144,9216]{1,0:T(8,128)}, f32[144,9216]{1,0:T(8,128)}, f32[144,9216]{1,0:T(8,128)}) fusion(f32[144,9216]{1,0:T(8,128)} %mod_ref.1, f32[]{:T(128)} %bitcast.43, f32[]{:T(128)} %bitcast.42, f32[144,9216]{1,0:T(8,128)} %get-tuple-element.185, f32[]{:T(128)} %bitcast.41, f32[144,9216]{1,0:T(8,128)} %param.54, f32[144,9216]{1,0:T(8,128)} %param.53), kind=kLoop, calls=%fused_computation.9 | loop fusion | flops 21233664 | bytes 37158924 | tf_op jit(solution)/shard_map/sub | solution.py:86
  561.1 4.1 multiply_subtract_fusion.1
  565.3 1.9 multiply_subtract_fusion.2
  567.9 1.6 multiply_subtract_fusion.3
  (118 shorter events, 13.1 us)
Async XLA Ops:
  7.2 7.1 %copy-start.2 = (f32[2,144,768]{2,1,0:T(8,128)S(1)}, f32[2,144,768]{2,1,0:T(8,128)}, u32[]{:S(2)}) copy-start(f32[2,144,768]{2,1,0:T(8,128)} %param.46) | copy-start | bytes 2654212
  7.2 7.2 %copy-start.23 = (s32[16]{0:T(128)S(1)}, s32[16]{0:T(128)}, u32[]{:S(2)}) copy-start(s32[16]{0:T(128)} %param.36) | copy-start | bytes 196
  7.2 7.2 %copy-start.25 = (s32[16]{0:T(128)S(1)}, s32[16]{0:T(128)}, u32[]{:S(2)}) copy-start(s32[16]{0:T(128)} %param.37) | copy-start | bytes 196
  7.2 497.7 %all-gather.2.cloned.1.call-start = ((), (), s32[]{:S(2)}) async-start(), calls=%async_computation | async-start | bytes 2433024 | tf_op jit(solution)/shard_map/all_gather | solution.py:1426
  27.8 4.2 copy-start.24
  32.2 5.1 copy-start.22
  270.5 46.3 %copy-start.21 = (f32[6,4,1152]{2,1,0:T(4,128)S(1)}, f32[6,4,1152]{2,1,0:T(4,128)}, u32[]{:S(2)}) copy-start(f32[6,4,1152]{2,1,0:T(4,128)} %get-tuple-element.108) | copy-start | bytes 331780
  270.5 49.0 %copy-start.18 = (f32[32,1152]{1,0:T(8,128)S(1)}, f32[32,1152]{1,0:T(8,128)}, u32[]{:S(2)}) copy-start(f32[32,1152]{1,0:T(8,128)} %get-tuple-element.116) | copy-start | bytes 442372
  270.5 50.6 %copy-start.20 = (f32[16,1152]{1,0:T(8,128)S(1)}, f32[16,1152]{1,0:T(8,128)}, u32[]{:S(2)}) copy-start(f32[16,1152]{1,0:T(8,128)} %get-tuple-element.109) | copy-start | bytes 221188
  270.5 51.3 %copy-start.19 = (f32[16,1152]{1,0:T(8,128)S(1)}, f32[16,1152]{1,0:T(8,128)}, u32[]{:S(2)}) copy-start(f32[16,1152]{1,0:T(8,128)} %get-tuple-element.110) | copy-start | bytes 221188
  319.4 201.0 %all-reduce.8.cloned.1.call-start = ((), (), s32[]{:S(2)}) async-start(), calls=%async_computation.1 | async-start | bytes 516096 | tf_op jit(solution)/shard_map/psum | solution.py:1433
  493.3 6.3 %copy-start.1 = (f32[144,1152]{1,0:T(8,128)}, f32[144,1152]{1,0:T(8,128)S(1)}, u32[]{:S(2)}) copy-start(f32[144,1152]{1,0:T(8,128)S(1)} %get-tuple-element.145) | copy-start | bytes 1990660
  493.4 3.1 copy-start.16
  494.3 6.6 %copy-start.17 = (bf16[8,16,1152]{2,1,0:T(8,128)(2,1)S(1)}, bf16[8,16,1152]{2,1,0:T(8,128)(2,1)}, u32[]{:S(2)}) copy-start(bf16[8,16,1152]{2,1,0:T(8,128)(2,1)} %get-tuple-element.113) | copy-start | bytes 884740
  546.3 14.7 %copy-start = (f32[617,1152]{1,0:T(8,128)S(1)}, f32[617,1152]{1,0:T(8,128)}, u32[]{:S(2)}) copy-start(f32[617,1152]{1,0:T(8,128)} %param.55) | copy-start | bytes 8529412
  546.3 14.7 %copy-start.4 = (f32[617,1152]{1,0:T(8,128)S(1)}, f32[617,1152]{1,0:T(8,128)}, u32[]{:S(2)}) copy-start(f32[617,1152]{1,0:T(8,128)} %param.57) | copy-start | bytes 8529412
  546.3 14.7 %copy-start.5 = (f32[617,1152]{1,0:T(8,128)S(1)}, f32[617,1152]{1,0:T(8,128)}, u32[]{:S(2)}) copy-start(f32[617,1152]{1,0:T(8,128)} %param.56) | copy-start | bytes 8529412
  561.0 4.2 copy-start.3
  561.0 4.2 copy-start.7
  561.0 4.2 copy-start.8
  561.0 4.2 copy-start.9
  561.0 4.2 copy-start.10
  565.2 2.0 copy-start.6
  565.2 2.0 copy-start.11
  565.3 2.0 copy-start.12
  565.3 2.0 copy-start.13
  565.3 2.1 copy-start.14
  565.3 2.6 copy-start.15
Sparse Core Ops, SparseCore 0:
  319.5 65.1 all-gather.1
  390.8 129.6 all-reduce.7
